TPU v7x, 256 devices: a whole 4x4x8 slice. The times are simulated.
256 devices in a mesh: slab: 16 (over x_hi, z), face: 4 (over x_lo, core), band: 4 (over y).
Axes of the slice: x: 4 (x_hi: 2, x_lo: 2; x = x_hi * 2 + x_lo), y: 4, z: 8, core: 2. Of those that a mesh axis runs over, the one named last changes fastest.
Arguments:
- wavefunctions: float32 [96, 24, 24, 1024], P('slab', 'face', None, 'band'), may hold values from -6 to 6
- rotation: float32 [1024, 1024], P(None, 'band'), may hold values from -0.1875 to 0.1875
- cell_matrix: float32 [343, 343], replicated, may hold values from -0.02 to 0.02, as said below
- potential: float32 [96, 24, 24], P('slab', 'face'), may hold values from -0.3 to 0.3
- center: float32 [1], replicated, may hold values from -0.2 to 0.2
- halfwidth: float32 [1], replicated, may hold values from 1 to 1.5
Outputs:
- filtered: float32 [96, 24, 24, 1024], P('slab', 'face', None, 'band')
Inputs may be any that keep to these rules, and one draw needn't show every extreme that they name: cell_matrix is symmetric.
All inputs are finite; a program needn't handle non-finite values.
Results may differ from a plain program's by a relative error of at most 0.0001.
Values sent between devices are 32-bit elements; how exact they have to be, the bound alone decides.
No kernel may reach another device: no remote copies, remote signals or barrier semaphores. Data moves between devices by JAX's collectives and lax.ppermute only.
A program may use at most 192 MiB of HBM per device.

v0:
```python
import jax
import jax.numpy as jnp
from jax import lax
from jax.sharding import PartitionSpec as P

ORDER = 6


highest = lax.Precision.HIGHEST


def passed_along(value, axis, steps):
    count = lax.axis_size(axis)
    pairs = [(source, (source + steps) % count) for source in range(count)]
    return lax.ppermute(value, axis, pairs)


def pad_along(values, which_axis, before, behind):
    widths = [(0, 0)] * values.ndim
    widths[which_axis] = (before, behind)
    return jnp.pad(values, widths)


def split_cells(values, which_axis, cell_count):
    regular = lax.slice_in_dim(values, 0, cell_count * ORDER, axis=which_axis)
    regular = regular.reshape(
        values.shape[:which_axis] + (cell_count, ORDER) + values.shape[which_axis + 1 :]
    )
    closing = lax.slice_in_dim(values, ORDER, cell_count * ORDER + 1, stride=ORDER, axis=which_axis)
    closing = jnp.expand_dims(closing, which_axis + 1)
    return jnp.concatenate([regular, closing], which_axis + 1)


def join_cells(values, which_axis):
    cell_count = values.shape[which_axis]
    outer_shape = values.shape[:which_axis]
    inner_shape = values.shape[which_axis + 2 :]
    regular = lax.slice_in_dim(values, 0, ORDER, axis=which_axis + 1)
    regular = regular.reshape(outer_shape + (cell_count * ORDER,) + inner_shape)
    closing = lax.slice_in_dim(values, ORDER, ORDER + 1, axis=which_axis + 1)
    spaced = pad_along(closing, which_axis + 1, 0, ORDER - 1)
    spaced = spaced.reshape(outer_shape + (cell_count * ORDER,) + inner_shape)
    spaced = lax.slice_in_dim(spaced, 0, cell_count * ORDER - ORDER + 1, axis=which_axis)
    return pad_along(regular, which_axis, 0, 1) + pad_along(spaced, which_axis, ORDER, 0)


def cell_apply(extended, kernel):
    counts = [(extended.shape[index] - 1) // ORDER for index in range(3)]
    local_cells = split_cells(extended, 0, counts[0])
    local_cells = split_cells(local_cells, 2, counts[1])
    local_cells = split_cells(local_cells, 4, counts[2])
    product = jnp.einsum("ijkpqr,apbqcrn->aibjckn", kernel, local_cells, precision=highest)
    return join_cells(join_cells(join_cells(product, 4), 2), 0)


def fold_end(values, which_axis):
    length = values.shape[which_axis]
    first_slice = lax.slice_in_dim(values, 0, 1, axis=which_axis) + lax.slice_in_dim(
        values, length - 1, length, axis=which_axis
    )
    return jnp.concatenate(
        [first_slice, lax.slice_in_dim(values, 1, length - 1, axis=which_axis)], which_axis
    )


def pull_ghosts(owned):
    from_above = passed_along(owned[:1], "slab", -1)
    widened = jnp.concatenate([owned, from_above], 0)
    beside = passed_along(widened[:, :1], "face", -1)
    return jnp.concatenate([widened, beside], 1)


def partial_sums(extended, kernel, potential):
    wrapped = jnp.concatenate([extended, extended[:, :, :1]], 2)
    summed = fold_end(cell_apply(wrapped, kernel), 2)
    local_term = potential[:, :, :, None] * extended[:-1, :-1]
    return summed + pad_along(pad_along(local_term, 0, 0, 1), 1, 0, 1)


def push_sums(partial_field):
    from_below = passed_along(partial_field[:, -1:], "face", 1)
    trimmed = partial_field[:, :-1]
    trimmed = jnp.concatenate([trimmed[:, :1] + from_below, trimmed[:, 1:]], 1)
    under_slab = passed_along(trimmed[-1:], "slab", 1)
    trimmed = trimmed[:-1]
    return jnp.concatenate([trimmed[:1] + under_slab, trimmed[1:]], 0)


def shards(wavefunctions, rotation, cell_matrix, potential, center, halfwidth):
    node_side = ORDER + 1
    kernel = cell_matrix.reshape((node_side,) * 6)
    rotated = jnp.einsum(
        "xyzb,bc->xyzc",
        lax.all_gather(wavefunctions, "band", axis=3, tiled=True),
        rotation,
        precision=highest,
    )
    shift_value = center[0]
    scale_value = halfwidth[0]

    def scaled(owned):
        image = push_sums(partial_sums(pull_ghosts(owned), kernel, potential))
        return (image - shift_value * owned) / scale_value

    previous = rotated
    current = scaled(rotated)
    previous, current = (current, 2.0 * scaled(current) - previous)
    return current


def solution(mesh):
    placed = (
        P("slab", "face", None, "band"),
        P(None, "band"),
        P(),
        P("slab", "face", None),
        P(),
        P(),
    )
    return jax.shard_map(
        shards,
        mesh=mesh,
        in_specs=placed,
        out_specs=P("slab", "face", None, "band"),
        check_vma=False,
    )
```

profile of v0, /device:TPU:1, one launch (start us, length us, event | category | flops | bytes accessed | tf_op | source)
XLA Modules:
  0.0 198.2 jit_solution(8676890420417965294)
XLA Ops:
  6.5 0.7 all-gather.2.cloned.1.call-update
  7.3 51.1 %all-gather.2.cloned.1.call-done = f32[6,6,24,1024]{3,2,1,0:T(8,128)} async-done(((f32[6,6,24,256]{3,2,1,0:T(8,128)}), f32[6,6,24,1024]{3,2,1,0:T(8,128)}) %all-gather.2.cloned.1.call-update) | async-done | bytes 3538960 | tf_op jit(solution)/shard_map/all_gather | solution.py:94
  58.4 4.9 %broadcast_multiply_fusion.1 = (f32[6,6,24,256]{3,2,1,0:T(8,128)S(1)}, f32[6,6,24,256]{3,2,1,0:T(8,128)S(1)}) fusion(f32[6,6,24]{2,1,0:T(8,128)} %param.9, f32[6,6,24,1024]{3,2,1,0:T(8,128)} %all-gather.2.cloned.1.call-done, f32[1024,256]{1,0:T(8,128)S(1)} %copy-done), kind=kOutput, calls=%fused_computation.76 | convolution fusion | flops 2718130176 | bytes 6360448 | tf_op jit(solution)/shard_map/xyzb,bc->xyzc/dot_general | solution.py:92
  63.3 5.5 %collective-permute-start = (f32[1,6,24,256]{3,2,1,0:T(8,128)S(1)}, f32[1,6,24,256]{3,2,1,0:T(8,128)S(1)}, u32[]{:S(2)}, u32[]{:S(2)}) collective-permute-start(f32[1,6,24,256]{3,2,1,0:T(8,128)S(1)} %slice.234), channel_id=1, source_target_pairs={{0,240},{16,0},{32,16},{48,32},{64,48},{80,64},{96,80},{112,96},{1... | collective-permute-start | bytes 442376 | tf_op jit(solution)/shard_map/ppermute | solution.py:15
  68.8 2.5 %collective-permute-done = f32[1,6,24,256]{3,2,1,0:T(8,128)S(1)} collective-permute-done((f32[1,6,24,256]{3,2,1,0:T(8,128)S(1)}, f32[1,6,24,256]{3,2,1,0:T(8,128)S(1)}, u32[]{:S(2)}, u32[]{:S(2)}) %collective-permute-start) | collective-permute-done | bytes 147488 | tf_op jit(solution)/shard_map/ppermute | solution.py:15
  71.3 1.7 collective-permute-start.1
  73.0 6.6 %reshape.68 = f32[7,7,7,7,7,7]{5,4,3,2,1,0:T(8,128)} reshape(f32[343,343]{1,0:T(8,128)S(1)} %copy-done.2) | data formatting | bytes 941192 | tf_op jit(solution)/shard_map/reshape | solution.py:91
  80.0 1.3 pad_maximum_fusion
  81.3 1.1 fusion.31
  82.4 3.9 %slice.188 = f32[1,7,1,7,4,256]{5,4,3,1,2,0:T(4,128)S(1)} slice(f32[1,7,1,7,25,256]{5,4,3,1,2,0:T(8,128)} %pad_maximum_fusion), slice={[0:1:1], [0:7:1], [0:1:1], [0:7:1], [6:25:6], [0:256:1]} | slice | bytes 401408 | tf_op jit(solution)/shard_map/slice | solution.py:29
  86.4 0.2 copy.21
  86.6 3.3 %reshape.66 = f32[1,7,1,7,4,6,256]{6,2,5,4,3,1,0:T(1,128)} reshape(f32[1,7,1,7,24,256]{5,4,3,1,2,0:T(8,128)} %fusion.31) | data formatting | bytes 2408448 | tf_op jit(solution)/shard_map/reshape | solution.py:26
  89.9 1.5 copy.20
  91.4 0.3 maximum_bitcast_fusion.12
  91.7 21.6 %fusion.12 = f32[1,7,1,7,4,7,256]{6,5,3,1,4,2,0:T(8,128)S(1)} fusion(f32[7,7,7,7,7,7]{5,4,3,2,1,0:T(8,128)} %reshape.68, f32[7,7,4,7,256,1,1]{4,3,1,0,6,5,2:T(8,128)S(1)} %maximum_bitcast_fusion.12), kind=kOutput, calls=%fused_computation.36 | convolution fusion | flops 1445670912 | bytes 3280452 | tf_op jit(solution)/shard_map/ijkpqr,apbqcrn->aibjckn/dot_general | solution.py:52
  113.4 0.2 slice.241
  113.6 0.2 copy.42
  113.8 0.6 pad.74.clone
  114.5 0.7 slice.242
  115.2 1.2 copy.23
  116.6 0.2 fusion.19
  117.5 0.3 collective-permute-start.2
  117.9 2.2 %collective-permute-done.2 = f32[7,1,24,256]{3,2,1,0:T(8,128)S(1)} collective-permute-done((f32[7,1,24,256]{3,2,1,0:T(8,128)S(1)}, f32[7,1,24,256]{3,2,1,0:T(8,128)S(1)}, u32[]{:S(2)}, u32[]{:S(2)}) %collective-permute-start.2) | collective-permute-done | bytes 172064 | tf_op jit(solution)/shard_map/ppermute | solution.py:15
  121.6 7.6 %collective-permute-done.3 = f32[1,6,24,256]{3,2,1,0:T(8,128)S(1)} collective-permute-done((f32[1,6,24,256]{3,2,1,0:T(8,128)S(1)}, f32[1,6,24,256]{3,2,1,0:T(8,128)S(1)}, u32[]{:S(2)}, u32[]{:S(2)}) %collective-permute-start.3) | collective-permute-done | bytes 147488 | tf_op jit(solution)/shard_map/ppermute | solution.py:15
  129.2 0.2 broadcast_multiply_fusion
  129.5 1.5 collective-permute-start.4
  131.0 2.5 %collective-permute-done.4 = f32[1,6,24,256]{3,2,1,0:T(8,128)S(1)} collective-permute-done((f32[1,6,24,256]{3,2,1,0:T(8,128)S(1)}, f32[1,6,24,256]{3,2,1,0:T(8,128)S(1)}, u32[]{:S(2)}, u32[]{:S(2)}) %collective-permute-start.4) | collective-permute-done | bytes 147488 | tf_op jit(solution)/shard_map/ppermute | solution.py:15
  133.6 4.0 %collective-permute-start.5 = (f32[7,1,24,256]{3,2,1,0:T(8,128)S(1)}, f32[7,1,24,256]{3,2,1,0:T(8,128)S(1)}, u32[]{:S(2)}, u32[]{:S(2)}) collective-permute-start(f32[7,1,24,256]{3,2,1,0:T(8,128)S(1)} %pad_maximum_fusion.10), channel_id=1, source_target_pairs={{0,12},{4,0},{8,4},{12,8},{1,13},{5,1},{9,5},{13,9},{2,14},{6,2},{... | collective-permute-start | bytes 516104 | tf_op jit(solution)/shard_map/ppermute | solution.py:15
  137.6 3.3 %collective-permute-done.5 = f32[7,1,24,256]{3,2,1,0:T(8,128)S(1)} collective-permute-done((f32[7,1,24,256]{3,2,1,0:T(8,128)S(1)}, f32[7,1,24,256]{3,2,1,0:T(8,128)S(1)}, u32[]{:S(2)}, u32[]{:S(2)}) %collective-permute-start.5) | collective-permute-done | bytes 172064 | tf_op jit(solution)/shard_map/ppermute | solution.py:15
  141.3 1.3 pad_maximum_fusion.1
  142.6 1.1 fusion.30
  143.7 3.9 %slice.215 = f32[1,7,1,7,4,256]{5,4,3,1,2,0:T(4,128)S(1)} slice(f32[1,7,1,7,25,256]{5,4,3,1,2,0:T(8,128)} %pad_maximum_fusion.1), slice={[0:1:1], [0:7:1], [0:1:1], [0:7:1], [6:25:6], [0:256:1]} | slice | bytes 401408 | tf_op jit(solution)/shard_map/slice | solution.py:29
  147.7 0.2 copy.29
  147.9 3.3 %reshape.76 = f32[1,7,1,7,4,6,256]{6,2,5,4,3,1,0:T(1,128)} reshape(f32[1,7,1,7,24,256]{5,4,3,1,2,0:T(8,128)} %fusion.30) | data formatting | bytes 2408448 | tf_op jit(solution)/shard_map/reshape | solution.py:26
  151.2 1.5 copy.28
  152.7 0.3 maximum_bitcast_fusion.13
  153.0 21.6 %fusion.15 = f32[1,7,1,7,4,7,256]{6,5,3,1,4,2,0:T(8,128)S(1)} fusion(f32[7,7,7,7,7,7]{5,4,3,2,1,0:T(8,128)} %reshape.68, f32[7,7,4,7,256,1,1]{4,3,1,0,6,5,2:T(8,128)S(1)} %maximum_bitcast_fusion.13), kind=kOutput, calls=%fused_computation.37 | convolution fusion | flops 1445670912 | bytes 3280452 | tf_op jit(solution)/shard_map/ijkpqr,apbqcrn->aibjckn/dot_general | solution.py:52
  174.7 0.2 slice.255
  174.9 0.2 copy.43
  175.1 0.6 pad.84.clone
  175.8 0.7 slice.256
  176.5 1.2 copy.31
  177.9 0.2 fusion.23
  178.2 0.2 pad_bitcast_fusion
  179.0 2.2 %collective-permute-done.6 = f32[7,1,24,256]{3,2,1,0:T(8,128)S(1)} collective-permute-done((f32[7,1,24,256]{3,2,1,0:T(8,128)S(1)}, f32[7,1,24,256]{3,2,1,0:T(8,128)S(1)}, u32[]{:S(2)}, u32[]{:S(2)}) %collective-permute-start.6) | collective-permute-done | bytes 172064 | tf_op jit(solution)/shard_map/ppermute | solution.py:15
  181.4 8.5 %collective-permute-done.7 = f32[1,6,24,256]{3,2,1,0:T(8,128)S(1)} collective-permute-done((f32[1,6,24,256]{3,2,1,0:T(8,128)S(1)}, f32[1,6,24,256]{3,2,1,0:T(8,128)S(1)}, u32[]{:S(2)}, u32[]{:S(2)}) %collective-permute-start.7) | collective-permute-done | bytes 147488 | tf_op jit(solution)/shard_map/ppermute | solution.py:15
  189.9 1.1 fusion.38
  191.0 0.4 copy-done.1
  (53 shorter events, 2.9 us)
Async XLA Ops:
  6.5 51.8 %copy-start = (f32[1024,256]{1,0:T(8,128)S(1)}, f32[1024,256]{1,0:T(8,128)}, u32[]{:S(2)}) copy-start(f32[1024,256]{1,0:T(8,128)} %param.7) | copy-start | bytes 3145732
  6.5 51.8 %all-gather.2.cloned.1.call-start = ((), (), s32[]{:S(2)}) async-start(), calls=%async_computation | async-start | bytes 4423680 | tf_op jit(solution)/shard_map/all_gather | solution.py:94
  63.3 9.7 %copy-start.2 = (f32[343,343]{1,0:T(8,128)S(1)}, f32[343,343]{1,0:T(8,128)}, u32[]{:S(2)}) copy-start(f32[343,343]{1,0:T(8,128)} %param.8) | copy-start | bytes 1411792
  63.3 8.0 %collective-permute-start = (f32[1,6,24,256]{3,2,1,0:T(8,128)S(1)}, f32[1,6,24,256]{3,2,1,0:T(8,128)S(1)}, u32[]{:S(2)}, u32[]{:S(2)}) collective-permute-start(f32[1,6,24,256]{3,2,1,0:T(8,128)S(1)} %slice.234), channel_id=1, source_target_pairs={{0,240},{16,0},{32,16},{48,32},{64,48},{80,64},{96,80},{112,96},{1... | collective-permute-start | bytes 442376 | tf_op jit(solution)/shard_map/ppermute | solution.py:15
  71.3 8.3 %collective-permute-start.1 = (f32[7,1,24,256]{3,2,1,0:T(8,128)S(1)}, f32[7,1,24,256]{3,2,1,0:T(8,128)S(1)}, u32[]{:S(2)}, u32[]{:S(2)}) collective-permute-start(f32[7,1,24,256]{3,2,1,0:T(8,128)S(1)} %pad_maximum_fusion.11), channel_id=1, source_target_pairs={{0,12},{4,0},{8,4},{12,8},{1,13},{5,1},{9,5},{13,9},{2,14},{6,2},{... | collective-permute-start | bytes 516104 | tf_op jit(solution)/shard_map/ppermute | solution.py:15
  117.5 2.6 %collective-permute-start.2 = (f32[7,1,24,256]{3,2,1,0:T(8,128)S(1)}, f32[7,1,24,256]{3,2,1,0:T(8,128)S(1)}, u32[]{:S(2)}, u32[]{:S(2)}) collective-permute-start(f32[7,1,24,256]{3,2,1,0:T(8,128)S(1)} %pad_add_fusion.9), channel_id=1, source_target_pairs={{0,4},{4,8},{8,12},{12,0},{1,5},{5,9},{9,13},{13,1},{2,6},{6,10},{... | collective-permute-start | bytes 516104 | tf_op jit(solution)/shard_map/ppermute | solution.py:15
  120.1 9.1 %copy-start.3 = (f32[6,6,24]{2,1,0:T(8,128)S(1)}, f32[6,6,24]{2,1,0:T(8,128)}, u32[]{:S(2)}) copy-start(f32[6,6,24]{2,1,0:T(8,128)} %param.9) | copy-start | bytes 10372
  120.2 9.0 %collective-permute-start.3 = (f32[1,6,24,256]{3,2,1,0:T(8,128)S(1)}, f32[1,6,24,256]{3,2,1,0:T(8,128)S(1)}, u32[]{:S(2)}, u32[]{:S(2)}) collective-permute-start(f32[1,6,24,256]{3,2,1,0:T(8,128)S(1)} %pad_maximum_fusion.13), channel_id=1, source_target_pairs={{0,16},{16,32},{32,48},{48,64},{64,80},{80,96},{96,112},{112,128},... | collective-permute-start | bytes 442376 | tf_op jit(solution)/shard_map/ppermute | solution.py:15
  129.5 4.1 %collective-permute-start.4 = (f32[1,6,24,256]{3,2,1,0:T(8,128)S(1)}, f32[1,6,24,256]{3,2,1,0:T(8,128)S(1)}, u32[]{:S(2)}, u32[]{:S(2)}) collective-permute-start(f32[1,6,24,256]{3,2,1,0:T(8,128)S(1)} %slice.248), channel_id=1, source_target_pairs={{0,240},{16,0},{32,16},{48,32},{64,48},{80,64},{96,80},{112,96},{1... | collective-permute-start | bytes 442376 | tf_op jit(solution)/shard_map/ppermute | solution.py:15
  133.6 7.3 %collective-permute-start.5 = (f32[7,1,24,256]{3,2,1,0:T(8,128)S(1)}, f32[7,1,24,256]{3,2,1,0:T(8,128)S(1)}, u32[]{:S(2)}, u32[]{:S(2)}) collective-permute-start(f32[7,1,24,256]{3,2,1,0:T(8,128)S(1)} %pad_maximum_fusion.10), channel_id=1, source_target_pairs={{0,12},{4,0},{8,4},{12,8},{1,13},{5,1},{9,5},{13,9},{2,14},{6,2},{... | collective-permute-start | bytes 516104 | tf_op jit(solution)/shard_map/ppermute | solution.py:15
  178.8 2.4 %collective-permute-start.6 = (f32[7,1,24,256]{3,2,1,0:T(8,128)S(1)}, f32[7,1,24,256]{3,2,1,0:T(8,128)S(1)}, u32[]{:S(2)}, u32[]{:S(2)}) collective-permute-start(f32[7,1,24,256]{3,2,1,0:T(8,128)S(1)} %pad_add_fusion.8), channel_id=1, source_target_pairs={{0,4},{4,8},{8,12},{12,0},{1,5},{5,9},{9,13},{13,1},{2,6},{6,10},{... | collective-permute-start | bytes 516104 | tf_op jit(solution)/shard_map/ppermute | solution.py:15
  181.3 8.6 %collective-permute-start.7 = (f32[1,6,24,256]{3,2,1,0:T(8,128)S(1)}, f32[1,6,24,256]{3,2,1,0:T(8,128)S(1)}, u32[]{:S(2)}, u32[]{:S(2)}) collective-permute-start(f32[1,6,24,256]{3,2,1,0:T(8,128)S(1)} %pad_maximum_fusion.12), channel_id=1, source_target_pairs={{0,16},{16,32},{32,48},{48,64},{64,80},{80,96},{96,112},{112,128},... | collective-permute-start | bytes 442376 | tf_op jit(solution)/shard_map/ppermute | solution.py:15
  189.9 1.5 copy-start.1
Sparse Core Ops, SparseCore 0:
  9.2 49.1 all-gather.1
where the time goes:
time: 199 us; the launch traced here: 198 us
  waiting for transfers between devices  80.6 us (41%)
  matrix products  48.2 us (24%)
  local copies, waits for them, and re-layouts  31.8 us (16%)
  between operations  15.2 us (8%)
  starting transfers between devices  13.3 us (7%)
  other arithmetic  9.14 us (5%)
    all_gather x1, waiting for transfers between devices, shards(): lax.all_gather(wavefunctions, 'band', axis=3, tiled=True)  51.1 us
    dot_general x2, matrix products, cell_apply(): jnp.einsum('ijkpqr,apbqcrn->aibjckn', kernel, local_cells, precision=high...  43.3 us
    ppermute x8, waiting for transfers between devices, passed_along(): return lax.ppermute(value, axis, pairs)  28.8 us
    ppermute x8, starting transfers between devices, passed_along(): return lax.ppermute(value, axis, pairs)  13.3 us
    reshape x6, local copies, waits for them, and re-layouts, split_cells(): regular.reshape(values.shape[:which_axis] + (cell_count, ORDER) + values....  9.8 us
    slice x2, local copies, waits for them, and re-layouts, split_cells(): lax.slice_in_dim(values, ORDER, cell_count * ORDER + 1, stride=ORDER, axi...  7.89 us
    reshape x1, local copies, waits for them, and re-layouts, shards(): kernel = cell_matrix.reshape((node_side,) * 6)  6.6 us
    dot_general x1, matrix products, shards(): jnp.einsum('xyzb,bc->xyzc', lax.all_gather(wavefunctions, 'band', axis=3,...  4.91 us
  transfers between devices with their start and end apart: 9, of which 8 were waited for; matrix products, arithmetic and copies ran while one was open for 3% of the time, Pallas kernels for 0%

commit v1 on v0

v1 whole, which is shorter than its diff:
```python
import functools

import jax
import jax.numpy as jnp
import numpy as np
from jax import lax
from jax.experimental import pallas as pl
from jax.experimental.pallas import tpu as pltpu
from jax.sharding import PartitionSpec as P

ORDER = 6
SIDE = ORDER + 1
NZ = 24
LANES = 128
ROWS = 56
OWNED = 36 * NZ
CELL_ROWS = SIDE * ROWS
KPAD = 400
LAYER = NZ * ROWS
XROWS = 3 * ORDER * ROWS + KPAD
F32 = jnp.float32
BF16 = jnp.bfloat16
LIMIT = 48 * 1024 * 1024


def place(x, y):
    if x == 6:
        return y
    if x == 0:
        return 8 + y
    if y == 6:
        return 46 + x - 1
    return 16 + (x - 1) * 6 + y


def selection():
    chosen = np.zeros((KPAD, SIDE**3), np.float32)
    for p in range(SIDE):
        for q in range(SIDE):
            for r in range(SIDE):
                chosen[r * ROWS + place(p, q), (p * SIDE + q) * SIDE + r] = 1.0
    return chosen


def split(values):
    high = values.astype(BF16)
    return high, (values - high.astype(F32)).astype(BF16)


def dot(a, b):
    return jnp.dot(a, b, preferred_element_type=F32)


def prepare_kernel(cell, chosen, chosen_t, rotation, k_high, k_low, r_high, r_low):
    high, low = split(cell[...])
    k_high[...] = dot(dot(chosen[...], high).astype(BF16), chosen_t[...]).astype(BF16)
    k_low[...] = dot(dot(chosen[...], low).astype(BF16), chosen_t[...]).astype(BF16)
    r_high[...], r_low[...] = split(rotation[...])


def cells_product(x_ref, y_ref, xh_ref, xl_ref, k_high, k_low):
    high, low = split(x_ref[...])
    xh_ref[...] = high
    xl_ref[...] = low
    y_ref[...] = jnp.zeros_like(y_ref)
    kh = k_high[...]
    kl = k_low[...]
    step = ORDER * ROWS
    for pair in range(2):
        first, second = 2 * pair * step, (2 * pair + 1) * step
        xh = jnp.concatenate([xh_ref[first : first + KPAD], xh_ref[second : second + KPAD]], 1)
        xl = jnp.concatenate([xl_ref[first : first + KPAD], xl_ref[second : second + KPAD]], 1)
        product = dot(kh, xh) + (dot(kh, xl) + dot(kl, xh))
        y_ref[first : first + CELL_ROWS] += product[:CELL_ROWS, :LANES]
        y_ref[second : second + CELL_ROWS] += product[:CELL_ROWS, LANES:]
    y_ref[0:ROWS] += y_ref[LAYER : LAYER + ROWS]


def first_kernel(w, gx, gy, gxy, k_high, k_low, local, scale, p_out, f0, f6, s0, s6, x_ref, y_ref, xh_ref, xl_ref):
    x_ref[...] = jnp.zeros_like(x_ref)
    for z in range(NZ):
        at = z * ROWS
        x_ref[at : at + 6] = gx[pl.ds(z, 6, stride=NZ)]
        x_ref[at + 6 : at + 7] = gxy[z : z + 1]
        x_ref[at + 8 : at + 14] = w[pl.ds(z, 6, stride=NZ)]
        x_ref[at + 14 : at + 15] = gy[z : z + 1]
        x_ref[at + 16 : at + 46] = w[pl.ds(6 * NZ + z, 30, stride=NZ)]
        x_ref[at + 46 : at + 51] = gy[pl.ds(NZ + z, 5, stride=NZ)]
    x_ref[LAYER : LAYER + ROWS] = x_ref[0:ROWS]
    cells_product(x_ref, y_ref, xh_ref, xl_ref, k_high, k_low)
    p_out[...] = (y_ref[0:LAYER] + local[...] * x_ref[0:LAYER]) * scale[0]
    for z in range(NZ):
        at = z * ROWS
        s6[pl.ds(z, 7, stride=NZ)] = p_out[at : at + 7]
        s0[pl.ds(z, 7, stride=NZ)] = p_out[at + 8 : at + 15]
        f0[z : z + 1] = p_out[at + 8 : at + 9]
        f0[pl.ds(NZ + z, 5, stride=NZ)] = p_out[pl.ds(at + 16, 5, stride=6)]
        f0[6 * NZ + z : 6 * NZ + z + 1] = p_out[at : at + 1]
        f6[z : z + 1] = p_out[at + 14 : at + 15]
        f6[pl.ds(NZ + z, 5, stride=NZ)] = p_out[at + 46 : at + 51]
        f6[6 * NZ + z : 6 * NZ + z + 1] = p_out[at + 6 : at + 7]


def corner_kernel(s0, s6, r0, r6, t0, t6):
    t0[...] = s0[...]
    t6[...] = s6[...]
    t0[0:NZ] += r0[0:NZ]
    t0[6 * NZ : 7 * NZ] += r6[0:NZ]
    t6[0:NZ] += r0[6 * NZ : 7 * NZ]
    t6[6 * NZ : 7 * NZ] += r6[6 * NZ : 7 * NZ]


def second_kernel(p_in, r0, r6, t0, t6, q0, q6, w, k_high, k_low, local, scale, out, push_x, push_y, push_c, x_ref, y_ref, xh_ref, xl_ref, n_ref):
    x_ref[0:LAYER] = p_in[...]
    x_ref[LAYER:] = jnp.zeros((XROWS - LAYER, LANES), F32)
    n_ref[0 : 7 * NZ] = t0[...] + q0[...]
    n_ref[7 * NZ :] = t6[...] + q6[...]
    for z in range(NZ):
        at = z * ROWS
        x_ref[at : at + 7] = n_ref[pl.ds(7 * NZ + z, 7, stride=NZ)]
        x_ref[at + 8 : at + 15] = n_ref[pl.ds(z, 7, stride=NZ)]
        x_ref[pl.ds(at + 16, 5, stride=6)] += r0[pl.ds(NZ + z, 5, stride=NZ)]
        x_ref[at + 46 : at + 51] += r6[pl.ds(NZ + z, 5, stride=NZ)]
    x_ref[LAYER : LAYER + ROWS] = x_ref[0:ROWS]
    cells_product(x_ref, y_ref, xh_ref, xl_ref, k_high, k_low)
    y_ref[0:LAYER] = (y_ref[0:LAYER] + local[...] * x_ref[0:LAYER]) * (2.0 * scale[0])
    for z in range(NZ):
        at = z * ROWS
        out[pl.ds(z, 6, stride=NZ)] = y_ref[at + 8 : at + 14]
        out[pl.ds(6 * NZ + z, 30, stride=NZ)] = y_ref[at + 16 : at + 46]
        push_x[pl.ds(z, 6, stride=NZ)] = y_ref[at : at + 6]
        push_c[z : z + 1] = y_ref[at + 6 : at + 7]
        push_y[z : z + 1] = y_ref[at + 14 : at + 15]
        push_y[pl.ds(NZ + z, 5, stride=NZ)] = y_ref[at + 46 : at + 51]
    out[...] -= w[...]


def finish_kernel(q, rx, ry, rc, out):
    out[...] = q[...]
    out[0 : 6 * NZ] += rx[...]
    for x in range(6):
        out[x * 6 * NZ : x * 6 * NZ + NZ] += ry[x * NZ : (x + 1) * NZ]
    out[0:NZ] += rc[...]


def piece(values, rows, r_high, r_low):
    high, low = split(values)
    rh = r_high[rows]
    return dot(high, rh) + (dot(low, rh) + dot(high, r_low[rows]))


def band_rows(me, steps, chunk):
    owner = lax.rem(me + steps + 4, 4)
    return pl.ds(pl.multiple_of(owner * 256 + chunk * LANES, LANES), LANES)


def near_terms(me, chunk, own, left, right, r_high, r_low):
    return (
        piece(own[...], band_rows(me, 0, chunk), r_high, r_low)
        + piece(left[...], band_rows(me, -1, chunk), r_high, r_low)
        + piece(right[...], band_rows(me, 1, chunk), r_high, r_low)
    )


def far_terms(me, chunk, low_half, high_half, r_high, r_low):
    rows = band_rows(me, 2, chunk)
    return jnp.concatenate(
        [piece(low_half[...], rows, r_high, r_low), piece(high_half[...], rows, r_high, r_low)], 0
    )


def turn_first(me, own, left, right, r_high, r_low, out):
    out[...] = near_terms(me[0], 0, own, left, right, r_high, r_low)


def turn_second(me, total, low_half, high_half, own, left, right, r_high, r_low, out):
    out[...] = total[...] + (
        near_terms(me[0], 1, own, left, right, r_high, r_low)
        + far_terms(me[0], 0, low_half, high_half, r_high, r_low)
    )


def turn_last(me, total, low_half, high_half, r_high, r_low, out):
    out[...] = total[...] + far_terms(me[0], 1, low_half, high_half, r_high, r_low)


VM = pl.BlockSpec(memory_space=pltpu.VMEM)
SM = pl.BlockSpec(memory_space=pltpu.SMEM)


def call(kernel, name, in_specs, shapes, scratch=(), flops=0, moved=0, grid=None, aliases=None):
    return pl.pallas_call(
        kernel,
        name=name,
        in_specs=in_specs,
        out_specs=[VM] * len(shapes),
        out_shape=[jax.ShapeDtypeStruct(*shape) for shape in shapes],
        scratch_shapes=list(scratch),
        compiler_params=pltpu.CompilerParams(vmem_limit_bytes=LIMIT),
        cost_estimate=pl.CostEstimate(flops=flops, bytes_accessed=moved, transcendentals=0),
        input_output_aliases=aliases or {},
    )


OP_SCRATCH = (
    pltpu.VMEM((XROWS, LANES), F32),
    pltpu.VMEM((LAYER + ROWS, LANES), F32),
    pltpu.VMEM((XROWS, LANES), BF16),
    pltpu.VMEM((XROWS, LANES), BF16),
)
OP_FLOPS = 2 * 3 * 512 * 512 * 512


def passed_along(value, axis, steps):
    count = lax.axis_size(axis)
    return lax.ppermute(value, axis, [(s, (s + steps) % count) for s in range(count)])


def passed_diagonal(value, steps):
    slabs, faces = lax.axis_size("slab"), lax.axis_size("face")
    pairs = [
        (a * faces + b, ((a + steps) % slabs) * faces + (b + steps) % faces)
        for a in range(slabs)
        for b in range(faces)
    ]
    return lax.ppermute(value, ("slab", "face"), pairs)


def shards(wavefunctions, rotation, cell_matrix, potential, center, halfwidth):
    chosen = selection()
    me = lax.axis_index("band").astype(jnp.int32).reshape(1)
    scale = 1.0 / halfwidth

    chunks = []
    for j in range(2):
        w = wavefunctions[..., j * LANES : (j + 1) * LANES]
        gx = passed_along(w[0].reshape(6 * NZ, LANES), "slab", -1)
        gy = passed_along(w[:, 0].reshape(6 * NZ, LANES), "face", -1)
        gxy = passed_diagonal(w[0, 0], -1)
        chunks.append((w.reshape(OWNED, LANES), gx, gy, gxy))

    k_high, k_low, r_high, r_low = call(
        prepare_kernel,
        "prepare",
        [VM] * 4,
        [((KPAD, KPAD), BF16)] * 2 + [((1024, 256), BF16)] * 2,
        flops=4 * 2 * KPAD * KPAD * KPAD,
        moved=4 << 20,
    )(cell_matrix, jnp.asarray(chosen, BF16), jnp.asarray(chosen.T, BF16), rotation)

    shifted = potential - center[0]
    by_layer = jnp.transpose(shifted, (2, 0, 1))
    local = jnp.concatenate(
        [
            jnp.zeros((NZ, 8), F32),
            by_layer[:, 0],
            jnp.zeros((NZ, 2), F32),
            by_layer[:, 1:].reshape(NZ, 30),
            jnp.zeros((NZ, 10), F32),
        ],
        1,
    ).reshape(LAYER, 1)

    plane = ((7 * NZ, LANES), F32)
    edge = ((6 * NZ, LANES), F32)
    block = ((OWNED, LANES), F32)

    filtered = []
    for w, gx, gy, gxy in chunks:
        p, f0, f6, s0, s6 = call(
            first_kernel,
            "first",
            [VM] * 7 + [SM],
            [((LAYER, LANES), F32)] + [plane] * 4,
            OP_SCRATCH,
            OP_FLOPS,
            4 << 20,
        )(w, gx, gy, gxy, k_high, k_low, local, scale)
        r0 = passed_along(f6, "face", 1)
        r6 = passed_along(f0, "face", -1)
        t0, t6 = call(corner_kernel, "corner", [VM] * 4, [plane] * 2, moved=1 << 19)(s0, s6, r0, r6)
        q0 = passed_along(t6, "slab", 1)
        q6 = passed_along(t0, "slab", -1)
        q, push_x, push_y, push_c = call(
            second_kernel,
            "second",
            [VM] * 11 + [SM],
            [block, edge, edge, ((NZ, LANES), F32)],
            OP_SCRATCH + (pltpu.VMEM((14 * NZ, LANES), F32),),
            OP_FLOPS,
            4 << 20,
        )(p, r0, r6, t0, t6, q0, q6, w, k_high, k_low, local, scale)
        rx = passed_along(push_x, "slab", 1)
        ry = passed_along(push_y, "face", 1)
        rc = passed_diagonal(push_c, 1)
        (f,) = call(finish_kernel, "finish", [VM] * 4, [block], moved=1 << 20)(q, rx, ry, rc)
        filtered.append(f)

    near, far = [], []
    for f in filtered:
        left = passed_along(f, "band", 1)
        right = passed_along(f, "band", -1)
        near.append((f, left, right))
        far.append(
            (
                passed_along(left[: OWNED // 2], "band", 1),
                passed_along(right[OWNED // 2 :], "band", -1),
            )
        )

    result = [((OWNED, 256), F32)]
    turn_flops = 2 * 3 * 1024 * 256 * 256
    (total,) = call(turn_first, "turn_first", [SM] + [VM] * 5, result, (), 2 * turn_flops, 3 << 20)(
        me, *near[0], r_high, r_low
    )
    (total,) = call(turn_second, "turn_second", [SM] + [VM] * 8, result, (), 3 * turn_flops, 4 << 20, aliases={1: 0})(
        me, total, *far[0], *near[1], r_high, r_low
    )
    (total,) = call(turn_last, "turn_last", [SM] + [VM] * 5, result, (), turn_flops, 3 << 20, aliases={1: 0})(
        me, total, *far[1], r_high, r_low
    )
    return total.reshape(6, 6, NZ, 256)


def solution(mesh):
    placed = (
        P("slab", "face", None, "band"),
        P(None, "band"),
        P(),
        P("slab", "face", None),
        P(),
        P(),
    )
    return jax.shard_map(
        shards,
        mesh=mesh,
        in_specs=placed,
        out_specs=P("slab", "face", None, "band"),
        check_vma=False,
    )
```

time: 199 us -> 91.7 us (0.46)
  waiting for transfers between devices: 80.6 us -> 19.3 us
  matrix products: 48.2 us -> 0 us
  starting transfers between devices: 13.3 us -> 43 us
  local copies, waits for them, and re-layouts: 31.8 us -> 10.2 us
  Pallas kernels: 0 us -> 16.2 us
  between operations: 15.2 us -> 1.56 us
  other arithmetic: 9.14 us -> 0.01 us
    all_gather x1 -> x0, waiting for transfers between devices: 51.1 us -> none  [shards(): lax.all_gather(wavefunctions, 'band', axis=3, tiled=True)]
    dot_general x3 -> x0, matrix products: 48.2 us -> none  [the longest x2 43.3 us: cell_apply(): jnp.einsum('ijkpqr,apbqcrn->aibjckn', kernel, local_cells, precision=high...]
    ppermute x8 -> x28, starting transfers between devices: 13.3 us -> 43 us  [the longest x24 39.3 us: passed_along(): lax.ppermute(value, axis, [(s, (s + steps) % count) for s in range(count)])]
    reshape x11 -> x3, local copies, waits for them, and re-layouts: 16.9 us -> 0.33 us  [the longest x1 0.25 us: shards(): local = jnp.concatenate([jnp.zeros((NZ, 8), F32), by_layer[:, 0], jnp.zer...]
    pallas_call x0 -> x12, Pallas kernels: none -> 16.2 us  [the longest x2 4.01 us: shards(): call(first_kernel, 'first', [VM] * 7 + [SM], [((LAYER, LANES), F32)] + [p...]
    ppermute x8 -> x28, waiting for transfers between devices: 28.8 us -> 19.3 us  [the longest x4 13.5 us: passed_diagonal(): return lax.ppermute(value, ('slab', 'face'), pairs)]
    concatenate x8 -> x0, other arithmetic: 5.14 us -> none  [the longest x4 4.8 us: split_cells(): return jnp.concatenate([regular, closing], which_axis + 1)]
    slice x12 -> x8, local copies, waits for them, and re-layouts: 12.2 us -> 7.35 us  [the longest x1 1.63 us: shards(): gx = passed_along(w[0].reshape(6 * NZ, LANES), 'slab', -1)]
  transfers between devices with their start and end apart: 9 -> 28, of which waited for: 8 -> 4; matrix products, arithmetic and copies ran while one was open for 3% -> 8% of each run, Pallas kernels for 0% -> 15%
where the time goes in v1:
time: 91.7 us; the launch traced here: 90.4 us
  starting transfers between devices  43 us (47%)
  waiting for transfers between devices  19.3 us (21%)
  Pallas kernels  16.2 us (18%)
  local copies, waits for them, and re-layouts  10.2 us (11%)
  between operations  1.56 us (2%)
    ppermute x24, starting transfers between devices, passed_along(): lax.ppermute(value, axis, [(s, (s + steps) % count) for s in range(count)])  39.3 us
    ppermute x4, waiting for transfers between devices, passed_diagonal(): return lax.ppermute(value, ('slab', 'face'), pairs)  13.5 us
    ppermute x24, waiting for transfers between devices, passed_along(): lax.ppermute(value, axis, [(s, (s + steps) % count) for s in range(count)])  5.85 us
    pallas_call x2, Pallas kernels, shards(): call(first_kernel, 'first', [VM] * 7 + [SM], [((LAYER, LANES), F32)] + [p...  4.01 us
    ppermute x4, starting transfers between devices, passed_diagonal(): return lax.ppermute(value, ('slab', 'face'), pairs)  3.77 us
    pallas_call x1, Pallas kernels, shards(): call(turn_second, 'turn_second', [SM] + [VM] * 8, result, (), 3 * turn_fl...  3.64 us
    pallas_call x1, Pallas kernels, shards(): call(turn_last, 'turn_last', [SM] + [VM] * 5, result, (), turn_flops, 3 <...  2.72 us
    pallas_call x2, Pallas kernels, shards(): call(second_kernel, 'second', [VM] * 11 + [SM], [block, edge, edge, ((NZ,...  2.35 us
  transfers between devices with their start and end apart: 28, of which 4 were waited for; matrix products, arithmetic and copies ran while one was open for 8% of the time, Pallas kernels for 15%

profile of v1, /device:TPU:1, one launch (start us, length us, event | category | flops | bytes accessed | tf_op | source)
XLA Modules:
  0.0 90.4 jit_solution(13611425405207494236)
XLA Ops:
  0.0 1.6 %fusion.1 = (f32[1,6,24,128]{3,2,1,0:T(8,128)}, f32[1,6,24,128]{3,2,1,0:T(8,128)}) fusion(f32[6,6,24,256]{3,2,1,0:T(8,128)} %param.8), kind=kLoop, calls=%fused_computation.5 | loop fusion | bytes 294912 | tf_op jit(solution)/shard_map/slice | solution.py:237
  1.6 8.9 %collective-permute-start.14 = (f32[144,128]{1,0:T(8,128)}, f32[144,128]{1,0:T(8,128)S(1)}, u32[]{:S(2)}, u32[]{:S(2)}) collective-permute-start(f32[144,128]{1,0:T(8,128)} %bitcast.9), channel_id=1, source_target_pairs={{0,240},{16,0},{32,16},{48,32},{64,48},{80,64},{96,80},{112,96},{1... | collective-permute-start | bytes 221192 | tf_op jit(solution)/shard_map/ppermute | solution.py:216
  10.5 1.6 %fusion = (f32[6,1,24,128]{3,2,1,0:T(8,128)}, f32[6,1,24,128]{3,2,1,0:T(8,128)}) fusion(f32[6,6,24,256]{3,2,1,0:T(8,128)} %param.8), kind=kLoop, calls=%fused_computation.4 | loop fusion | bytes 294912 | tf_op jit(solution)/shard_map/slice | solution.py:238
  12.1 1.0 %collective-permute-start.15 = (f32[144,128]{1,0:T(8,128)}, f32[144,128]{1,0:T(8,128)}, u32[]{:S(2)}, u32[]{:S(2)}) collective-permute-start(f32[144,128]{1,0:T(8,128)} %bitcast.10), channel_id=1, source_target_pairs={{0,12},{4,0},{8,4},{12,8},{1,13},{5,1},{9,5},{13,9},{2,14},{6,2},{... | collective-permute-start | bytes 221192 | tf_op jit(solution)/shard_map/ppermute | solution.py:216
  13.0 0.7 collective-permute-start
  13.8 0.6 collective-permute-start.1
  14.4 1.3 %slice_bitcast_fusion = (f32[24,128]{1,0:T(8,128)S(1)}, f32[24,128]{1,0:T(8,128)}) fusion(f32[6,6,24,256]{3,2,1,0:T(8,128)} %param.8), kind=kLoop, calls=%fused_computation.1 | loop fusion | bytes 49152 | tf_op jit(solution)/shard_map/squeeze | solution.py:239
  15.7 1.3 %collective-permute-start.2 = (f32[24,128]{1,0:T(8,128)}, f32[24,128]{1,0:T(8,128)S(1)}, u32[]{:S(2)}, u32[]{:S(2)}) collective-permute-start(f32[24,128]{1,0:T(8,128)} %get-tuple-element.58), channel_id=1, source_target_pairs={{0,252},{4,240},{8,244},{12,248},{16,12},{20,0},{24,4},{28,8},{32,... | collective-permute-start | bytes 36872 | tf_op jit(solution)/shard_map/ppermute | solution.py:226
  17.0 1.2 %fusion.2 = (f32[6,6,24,128]{3,2,1,0:T(8,128)S(1)}, f32[6,6,24,128]{3,2,1,0:T(8,128)S(1)}) fusion(f32[6,6,24,256]{3,2,1,0:T(8,128)} %param.8), kind=kLoop, calls=%fused_computation.6 | loop fusion | bytes 1769472 | tf_op jit(solution)/shard_map/slice | solution.py:236
  19.0 1.3 %prepare.1 = (bf16[400,400]{1,0:T(8,128)(2,1)S(1)}, bf16[400,400]{1,0:T(8,128)(2,1)S(1)}, bf16[1024,256]{1,0:T(8,128)(2,1)S(1)}, bf16[1024,256]{1,0:T(8,128)(2,1)S(1)}) custom-call(f32[343,343]{1,0:T(8,128)S(1)} %copy-done.5, bf16[400,343]{1,0:T(8,128)(2,1)S(1)} %copy-done.7, bf16[343,400]{1,0:T(8,128)(2,1)S(1)} %copy-done.6, f32[1024,256]{1,0:T(8,128)S(1)} %copy-done), custom_call_target="tpu_custom_call" | custom-call | flops 512000000 | bytes 4194304 | tf_op jit(solution)/shard_map/prepare/pallas_call | solution.py:242
  20.3 0.1 copy.26
  20.4 0.1 copy.25
  20.5 0.1 concatenate.3
  20.5 0.2 reshape.24.local
  21.5 2.5 %collective-permute-start.16 = (f32[24,128]{1,0:T(8,128)S(1)}, f32[24,128]{1,0:T(8,128)S(1)}, u32[]{:S(2)}, u32[]{:S(2)}) collective-permute-start(f32[24,128]{1,0:T(8,128)S(1)} %get-tuple-element.57), channel_id=1, source_target_pairs={{0,252},{4,240},{8,244},{12,248},{16,12},{20,0},{24,4},{28,8},{32,... | collective-permute-start | bytes 36872 | tf_op jit(solution)/shard_map/ppermute | solution.py:226
  24.0 2.0 %first.2 = (f32[1344,128]{1,0:T(8,128)S(1)}, f32[168,128]{1,0:T(8,128)S(1)}, f32[168,128]{1,0:T(8,128)S(1)}, f32[168,128]{1,0:T(8,128)S(1)}, f32[168,128]{1,0:T(8,128)S(1)}) custom-call(f32[864,128]{1,0:T(8,128)S(1)} %bitcast.22, f32[144,128]{1,0:T(8,128)} %collective-permute-done.gx, f32[144,128]{1,0:T(8,128)} %collective-permute-done.1.gy, ...), custom_call_target="tpu_custom_call" | custom-call | flops 805306368 | bytes 4194304 | tf_op jit(solution)/shard_map/first/pallas_call | solution.py:270
  26.0 0.1 collective-permute-start.3
  26.1 0.5 collective-permute-start.4
  26.6 2.0 %first.3 = (f32[1344,128]{1,0:T(8,128)S(1)}, f32[168,128]{1,0:T(8,128)S(1)}, f32[168,128]{1,0:T(8,128)S(1)}, f32[168,128]{1,0:T(8,128)S(1)}, f32[168,128]{1,0:T(8,128)S(1)}) custom-call(f32[864,128]{1,0:T(8,128)S(1)} %bitcast.20, f32[144,128]{1,0:T(8,128)S(1)} %collective-permute-done.14.gx, f32[144,128]{1,0:T(8,128)} %collective-permute-done.15.gy, ...), custom_call_target="tpu_custom_call" | custom-call | flops 805306368 | bytes 4194304 | tf_op jit(solution)/shard_map/first/pallas_call | solution.py:270
  28.6 1.4 %collective-permute-start.17 = (f32[168,128]{1,0:T(8,128)S(1)}, f32[168,128]{1,0:T(8,128)S(1)}, u32[]{:S(2)}, u32[]{:S(2)}) collective-permute-start(f32[168,128]{1,0:T(8,128)S(1)} %get-tuple-element.47), channel_id=1, source_target_pairs={{0,4},{4,8},{8,12},{12,0},{1,5},{5,9},{9,13},{13,1},{2,6},{6,10},{... | collective-permute-start | bytes 258056 | tf_op jit(solution)/shard_map/ppermute | solution.py:216
  30.0 0.1 collective-permute-done.4.r6
  30.1 0.5 collective-permute-start.5
  30.6 4.6 %collective-permute-start.6 = (f32[168,128]{1,0:T(8,128)S(1)}, f32[168,128]{1,0:T(8,128)S(1)}, u32[]{:S(2)}, u32[]{:S(2)}) collective-permute-start(f32[168,128]{1,0:T(8,128)S(1)} %get-tuple-element.38.t0), channel_id=1, source_target_pairs={{0,240},{16,0},{32,16},{48,32},{64,48},{80,64},{96,80},{112,96},{1... | collective-permute-start | bytes 258056 | tf_op jit(solution)/shard_map/ppermute | solution.py:216
  35.3 0.1 collective-permute-start.19
  35.4 5.1 %collective-permute-start.20 = (f32[168,128]{1,0:T(8,128)S(1)}, f32[168,128]{1,0:T(8,128)S(1)}, u32[]{:S(2)}, u32[]{:S(2)}) collective-permute-start(f32[168,128]{1,0:T(8,128)S(1)} %get-tuple-element.51.t0), channel_id=1, source_target_pairs={{0,240},{16,0},{32,16},{48,32},{64,48},{80,64},{96,80},{112,96},{1... | collective-permute-start | bytes 258056 | tf_op jit(solution)/shard_map/ppermute | solution.py:216
  40.5 1.2 %second.2 = (f32[864,128]{1,0:T(8,128)S(1)}, f32[144,128]{1,0:T(8,128)S(1)}, f32[144,128]{1,0:T(8,128)S(1)}, f32[24,128]{1,0:T(8,128)S(1)}) custom-call(f32[1344,128]{1,0:T(8,128)S(1)} %get-tuple-element.33.p_in, f32[168,128]{1,0:T(8,128)S(1)} %collective-permute-done.3.r0, f32[168,128]{1,0:T(8,128)S(1)} %collective-permute-done.4.r6, ...), custom_call_target="tpu_custom_call" | custom-call | flops 805306368 | bytes 4194304 | tf_op jit(solution)/shard_map/second/pallas_call | solution.py:284
  41.6 0.1 collective-permute-start.7
  41.7 2.9 %collective-permute-start.8 = (f32[144,128]{1,0:T(8,128)S(1)}, f32[144,128]{1,0:T(8,128)S(1)}, u32[]{:S(2)}, u32[]{:S(2)}) collective-permute-start(f32[144,128]{1,0:T(8,128)S(1)} %get-tuple-element.42), channel_id=1, source_target_pairs={{0,4},{4,8},{8,12},{12,0},{1,5},{5,9},{9,13},{13,1},{2,6},{6,10},{... | collective-permute-start | bytes 221192 | tf_op jit(solution)/shard_map/ppermute | solution.py:216
  44.6 6.7 %collective-permute-done.9.rc = f32[24,128]{1,0:T(8,128)S(1)} collective-permute-done((f32[24,128]{1,0:T(8,128)S(1)}, f32[24,128]{1,0:T(8,128)S(1)}, u32[]{:S(2)}, u32[]{:S(2)}) %collective-permute-start.9) | collective-permute-done | bytes 12320 | tf_op jit(solution)/shard_map/ppermute | solution.py:226
  51.4 1.4 %collective-permute-start.10 = (f32[864,128]{1,0:T(8,128)S(1)}, f32[864,128]{1,0:T(8,128)S(1)}, u32[]{:S(2)}, u32[]{:S(2)}) collective-permute-start(f32[864,128]{1,0:T(8,128)S(1)} %finish.2.own), channel_id=1, source_target_pairs={{0,1},{1,2},{2,3},{3,0},{4,5},{5,6},{6,7},{7,4},{8,9},{9,10},{10,1... | collective-permute-start | bytes 1327112 | tf_op jit(solution)/shard_map/ppermute | solution.py:216
  52.8 1.5 %collective-permute-start.11 = (f32[864,128]{1,0:T(8,128)S(1)}, f32[864,128]{1,0:T(8,128)S(1)}, u32[]{:S(2)}, u32[]{:S(2)}) collective-permute-start(f32[864,128]{1,0:T(8,128)S(1)} %finish.2.own), channel_id=1, source_target_pairs={{0,3},{1,0},{2,1},{3,2},{4,7},{5,4},{6,5},{7,6},{8,11},{9,8},{10,9... | collective-permute-start | bytes 1327112 | tf_op jit(solution)/shard_map/ppermute | solution.py:216
  54.3 1.2 %second.3 = (f32[864,128]{1,0:T(8,128)S(1)}, f32[144,128]{1,0:T(8,128)S(1)}, f32[144,128]{1,0:T(8,128)S(1)}, f32[24,128]{1,0:T(8,128)S(1)}) custom-call(f32[1344,128]{1,0:T(8,128)S(1)} %get-tuple-element.46.p_in, f32[168,128]{1,0:T(8,128)S(1)} %collective-permute-done.17.r0, f32[168,128]{1,0:T(8,128)S(1)} %collective-permute-done.18.r6, ...), custom_call_target="tpu_custom_call" | custom-call | flops 805306368 | bytes 4194304 | tf_op jit(solution)/shard_map/second/pallas_call | solution.py:284
  55.5 0.1 collective-permute-start.21
  55.6 1.7 %collective-permute-start.22 = (f32[144,128]{1,0:T(8,128)S(1)}, f32[144,128]{1,0:T(8,128)S(1)}, u32[]{:S(2)}, u32[]{:S(2)}) collective-permute-start(f32[144,128]{1,0:T(8,128)S(1)} %get-tuple-element.55), channel_id=1, source_target_pairs={{0,4},{4,8},{8,12},{12,0},{1,5},{5,9},{9,13},{13,1},{2,6},{6,10},{... | collective-permute-start | bytes 221192 | tf_op jit(solution)/shard_map/ppermute | solution.py:216
  57.3 6.7 %collective-permute-done.23.rc = f32[24,128]{1,0:T(8,128)S(1)} collective-permute-done((f32[24,128]{1,0:T(8,128)S(1)}, f32[24,128]{1,0:T(8,128)S(1)}, u32[]{:S(2)}, u32[]{:S(2)}) %collective-permute-start.23) | collective-permute-done | bytes 12320 | tf_op jit(solution)/shard_map/ppermute | solution.py:226
  64.1 0.2 collective-permute-start.24
  64.3 2.6 %collective-permute-start.25 = (f32[864,128]{1,0:T(8,128)S(1)}, f32[864,128]{1,0:T(8,128)S(1)}, u32[]{:S(2)}, u32[]{:S(2)}) collective-permute-start(f32[864,128]{1,0:T(8,128)S(1)} %finish.3.own), channel_id=1, source_target_pairs={{0,3},{1,0},{2,1},{3,2},{4,7},{5,4},{6,5},{7,6},{8,11},{9,8},{10,9... | collective-permute-start | bytes 1327112 | tf_op jit(solution)/shard_map/ppermute | solution.py:216
  66.9 0.7 slice.64
  67.6 0.7 slice.65
  68.4 2.7 %collective-permute-start.13 = (f32[432,128]{1,0:T(8,128)}, f32[432,128]{1,0:T(8,128)}, u32[]{:S(2)}, u32[]{:S(2)}) collective-permute-start(f32[432,128]{1,0:T(8,128)} %slice.65), channel_id=1, source_target_pairs={{0,3},{1,0},{2,1},{3,2},{4,7},{5,4},{6,5},{7,6},{8,11},{9,8},{10,9... | collective-permute-start | bytes 663560 | tf_op jit(solution)/shard_map/ppermute | solution.py:216
  71.0 5.7 %collective-permute-done.24.left = f32[864,128]{1,0:T(8,128)S(1)} collective-permute-done((f32[864,128]{1,0:T(8,128)S(1)}, f32[864,128]{1,0:T(8,128)S(1)}, u32[]{:S(2)}, u32[]{:S(2)}) %collective-permute-start.24) | collective-permute-done | bytes 442400 | tf_op jit(solution)/shard_map/ppermute | solution.py:216
  76.7 0.7 slice.66
  77.5 0.7 slice.67
  78.2 2.7 %collective-permute-start.27 = (f32[432,128]{1,0:T(8,128)}, f32[432,128]{1,0:T(8,128)}, u32[]{:S(2)}, u32[]{:S(2)}) collective-permute-start(f32[432,128]{1,0:T(8,128)} %slice.67), channel_id=1, source_target_pairs={{0,3},{1,0},{2,1},{3,2},{4,7},{5,4},{6,5},{7,6},{8,11},{9,8},{10,9... | collective-permute-start | bytes 663560 | tf_op jit(solution)/shard_map/ppermute | solution.py:216
  80.9 1.0 %copy-done.4 = f32[864,128]{1,0:T(8,128)S(1)} copy-done((f32[864,128]{1,0:T(8,128)S(1)}, f32[864,128]{1,0:T(8,128)}, u32[]{:S(2)}) %copy-start.4) | copy-done | bytes 442392
  81.9 2.1 %turn_first.1.total = f32[864,256]{1,0:T(8,128)} custom-call(s32[1]{0:T(128)} %bitcast.me, f32[864,128]{1,0:T(8,128)S(1)} %finish.2.own, f32[864,128]{1,0:T(8,128)S(1)} %copy-done.2, f32[864,128]{1,0:T(8,128)S(1)} %copy-done.4, bf16[1024,256]{1,0:T(8,128)(2,1)S(1)} %get-tuple-element.44.r_high, bf16[1024,256]{1,0:T(8,128)(2,1)S(1)} %get-tuple-element.45.r_low), custom_call_target="tpu_custom_call" | custom-call | flops 805306368 | bytes 3145728 | tf_op jit(solution)/shard_map/turn_first/pallas_call | solution.py:313
  84.0 3.6 %turn_second.1.total = f32[864,256]{1,0:T(8,128)} custom-call(s32[1]{0:T(128)} %bitcast.me, f32[864,256]{1,0:T(8,128)} %turn_first.1.total, f32[432,128]{1,0:T(8,128)S(1)} %collective-permute-done.12.low_half, f32[432,128]{1,0:T(8,128)} %collective-permute-done.13.high_half, f32[864,128]{1,0:T(8,128)S(1)} %finish.3.own, ...), custom_call_target="tpu_custom_call", output_to_operand_aliasing={{}: (1, {})} | custom-call | flops 1207959552 | bytes 4194304 | tf_op jit(solution)/shard_map/turn_second/pallas_call | solution.py:316
  87.6 2.7 %turn_last.1 = f32[864,256]{1,0:T(8,128)} custom-call(s32[1]{0:T(128)} %bitcast.me, f32[864,256]{1,0:T(8,128)} %turn_second.1.total, f32[432,128]{1,0:T(8,128)} %collective-permute-done.26.low_half, f32[432,128]{1,0:T(8,128)} %collective-permute-done.27.high_half, bf16[1024,256]{1,0:T(8,128)(2,1)S(1)} %get-tuple-element.44.r_high, ...), custom_call_target="tpu_custom_call", output_to_operand_aliasing={{}: (1, {})} | custom-call | flops 402653184 | bytes 3145728 | tf_op jit(solution)/shard_map/turn_last/pallas_call | solution.py:319
  (57 shorter events, 0.2 us)
Async XLA Ops:
  0.0 18.9 %copy-start.7 = (bf16[400,343]{1,0:T(8,128)(2,1)S(1)}, bf16[400,343]{1,0:T(8,128)(2,1)}, u32[]{:S(2)}) copy-start(bf16[400,343]{1,0:T(8,128)(2,1)} %constant.3.clone.chosen) | copy-start | bytes 823204
  1.6 17.3 %copy-start = (f32[1024,256]{1,0:T(8,128)S(1)}, f32[1024,256]{1,0:T(8,128)}, u32[]{:S(2)}) copy-start(f32[1024,256]{1,0:T(8,128)} %rotation.1) | copy-start | bytes 3145732
  1.6 25.0 %collective-permute-start.14 = (f32[144,128]{1,0:T(8,128)}, f32[144,128]{1,0:T(8,128)S(1)}, u32[]{:S(2)}, u32[]{:S(2)}) collective-permute-start(f32[144,128]{1,0:T(8,128)} %bitcast.9), channel_id=1, source_target_pairs={{0,240},{16,0},{32,16},{48,32},{64,48},{80,64},{96,80},{112,96},{1... | collective-permute-start | bytes 221192 | tf_op jit(solution)/shard_map/ppermute | solution.py:216
  12.1 14.5 %collective-permute-start.15 = (f32[144,128]{1,0:T(8,128)}, f32[144,128]{1,0:T(8,128)}, u32[]{:S(2)}, u32[]{:S(2)}) collective-permute-start(f32[144,128]{1,0:T(8,128)} %bitcast.10), channel_id=1, source_target_pairs={{0,12},{4,0},{8,4},{12,8},{1,13},{5,1},{9,5},{13,9},{2,14},{6,2},{... | collective-permute-start | bytes 221192 | tf_op jit(solution)/shard_map/ppermute | solution.py:216
  13.0 10.9 %collective-permute-start = (f32[144,128]{1,0:T(8,128)}, f32[144,128]{1,0:T(8,128)}, u32[]{:S(2)}, u32[]{:S(2)}) collective-permute-start(f32[144,128]{1,0:T(8,128)} %bitcast.2), channel_id=1, source_target_pairs={{0,240},{16,0},{32,16},{48,32},{64,48},{80,64},{96,80},{112,96},{1... | collective-permute-start | bytes 221192 | tf_op jit(solution)/shard_map/ppermute | solution.py:216
  13.8 10.2 %collective-permute-start.1 = (f32[144,128]{1,0:T(8,128)}, f32[144,128]{1,0:T(8,128)}, u32[]{:S(2)}, u32[]{:S(2)}) collective-permute-start(f32[144,128]{1,0:T(8,128)} %bitcast.3), channel_id=1, source_target_pairs={{0,12},{4,0},{8,4},{12,8},{1,13},{5,1},{9,5},{13,9},{2,14},{6,2},{... | collective-permute-start | bytes 221192 | tf_op jit(solution)/shard_map/ppermute | solution.py:216
  15.7 3.2 %copy-start.8 = (f32[6,6,24]{2,1,0:T(8,128)S(1)}, f32[6,6,24]{2,1,0:T(8,128)}, u32[]{:S(2)}) copy-start(f32[6,6,24]{2,1,0:T(8,128)} %param.11) | copy-start | bytes 10372
  15.7 3.2 %copy-start.5 = (f32[343,343]{1,0:T(8,128)S(1)}, f32[343,343]{1,0:T(8,128)}, u32[]{:S(2)}) copy-start(f32[343,343]{1,0:T(8,128)} %cell.1) | copy-start | bytes 1411792
  15.7 3.2 %copy-start.6 = (bf16[343,400]{1,0:T(8,128)(2,1)S(1)}, bf16[343,400]{1,0:T(8,128)(2,1)}, u32[]{:S(2)}) copy-start(bf16[343,400]{1,0:T(8,128)(2,1)} %constant.4.clone.chosen_t) | copy-start | bytes 823204
  15.7 5.8 %collective-permute-start.2 = (f32[24,128]{1,0:T(8,128)}, f32[24,128]{1,0:T(8,128)S(1)}, u32[]{:S(2)}, u32[]{:S(2)}) collective-permute-start(f32[24,128]{1,0:T(8,128)} %get-tuple-element.58), channel_id=1, source_target_pairs={{0,252},{4,240},{8,244},{12,248},{16,12},{20,0},{24,4},{28,8},{32,... | collective-permute-start | bytes 36872 | tf_op jit(solution)/shard_map/ppermute | solution.py:226
  21.5 5.1 %collective-permute-start.16 = (f32[24,128]{1,0:T(8,128)S(1)}, f32[24,128]{1,0:T(8,128)S(1)}, u32[]{:S(2)}, u32[]{:S(2)}) collective-permute-start(f32[24,128]{1,0:T(8,128)S(1)} %get-tuple-element.57), channel_id=1, source_target_pairs={{0,252},{4,240},{8,244},{12,248},{16,12},{20,0},{24,4},{28,8},{32,... | collective-permute-start | bytes 36872 | tf_op jit(solution)/shard_map/ppermute | solution.py:226
  26.0 4.0 %collective-permute-start.3 = (f32[168,128]{1,0:T(8,128)S(1)}, f32[168,128]{1,0:T(8,128)S(1)}, u32[]{:S(2)}, u32[]{:S(2)}) collective-permute-start(f32[168,128]{1,0:T(8,128)S(1)} %get-tuple-element.34), channel_id=1, source_target_pairs={{0,4},{4,8},{8,12},{12,0},{1,5},{5,9},{9,13},{13,1},{2,6},{6,10},{... | collective-permute-start | bytes 258056 | tf_op jit(solution)/shard_map/ppermute | solution.py:216
  26.1 4.0 %collective-permute-start.4 = (f32[168,128]{1,0:T(8,128)S(1)}, f32[168,128]{1,0:T(8,128)S(1)}, u32[]{:S(2)}, u32[]{:S(2)}) collective-permute-start(f32[168,128]{1,0:T(8,128)S(1)} %get-tuple-element.35), channel_id=1, source_target_pairs={{0,12},{4,0},{8,4},{12,8},{1,13},{5,1},{9,5},{13,9},{2,14},{6,2},{... | collective-permute-start | bytes 258056 | tf_op jit(solution)/shard_map/ppermute | solution.py:216
  28.6 6.7 %collective-permute-start.17 = (f32[168,128]{1,0:T(8,128)S(1)}, f32[168,128]{1,0:T(8,128)S(1)}, u32[]{:S(2)}, u32[]{:S(2)}) collective-permute-start(f32[168,128]{1,0:T(8,128)S(1)} %get-tuple-element.47), channel_id=1, source_target_pairs={{0,4},{4,8},{8,12},{12,0},{1,5},{5,9},{9,13},{13,1},{2,6},{6,10},{... | collective-permute-start | bytes 258056 | tf_op jit(solution)/shard_map/ppermute | solution.py:216
  30.0 5.3 %collective-permute-start.18 = (f32[168,128]{1,0:T(8,128)S(1)}, f32[168,128]{1,0:T(8,128)S(1)}, u32[]{:S(2)}, u32[]{:S(2)}) collective-permute-start(f32[168,128]{1,0:T(8,128)S(1)} %get-tuple-element.48), channel_id=1, source_target_pairs={{0,12},{4,0},{8,4},{12,8},{1,13},{5,1},{9,5},{13,9},{2,14},{6,2},{... | collective-permute-start | bytes 258056 | tf_op jit(solution)/shard_map/ppermute | solution.py:216
  30.1 10.3 %collective-permute-start.5 = (f32[168,128]{1,0:T(8,128)S(1)}, f32[168,128]{1,0:T(8,128)S(1)}, u32[]{:S(2)}, u32[]{:S(2)}) collective-permute-start(f32[168,128]{1,0:T(8,128)S(1)} %get-tuple-element.39.t6), channel_id=1, source_target_pairs={{0,16},{16,32},{32,48},{48,64},{64,80},{80,96},{96,112},{112,128},... | collective-permute-start | bytes 258056 | tf_op jit(solution)/shard_map/ppermute | solution.py:216
  30.6 9.8 %collective-permute-start.6 = (f32[168,128]{1,0:T(8,128)S(1)}, f32[168,128]{1,0:T(8,128)S(1)}, u32[]{:S(2)}, u32[]{:S(2)}) collective-permute-start(f32[168,128]{1,0:T(8,128)S(1)} %get-tuple-element.38.t0), channel_id=1, source_target_pairs={{0,240},{16,0},{32,16},{48,32},{64,48},{80,64},{96,80},{112,96},{1... | collective-permute-start | bytes 258056 | tf_op jit(solution)/shard_map/ppermute | solution.py:216
  35.3 19.0 %collective-permute-start.19 = (f32[168,128]{1,0:T(8,128)S(1)}, f32[168,128]{1,0:T(8,128)S(1)}, u32[]{:S(2)}, u32[]{:S(2)}) collective-permute-start(f32[168,128]{1,0:T(8,128)S(1)} %get-tuple-element.52.t6), channel_id=1, source_target_pairs={{0,16},{16,32},{32,48},{48,64},{64,80},{80,96},{96,112},{112,128},... | collective-permute-start | bytes 258056 | tf_op jit(solution)/shard_map/ppermute | solution.py:216
  35.4 18.9 %collective-permute-start.20 = (f32[168,128]{1,0:T(8,128)S(1)}, f32[168,128]{1,0:T(8,128)S(1)}, u32[]{:S(2)}, u32[]{:S(2)}) collective-permute-start(f32[168,128]{1,0:T(8,128)S(1)} %get-tuple-element.51.t0), channel_id=1, source_target_pairs={{0,240},{16,0},{32,16},{48,32},{64,48},{80,64},{96,80},{112,96},{1... | collective-permute-start | bytes 258056 | tf_op jit(solution)/shard_map/ppermute | solution.py:216
  41.6 9.7 %collective-permute-start.7 = (f32[144,128]{1,0:T(8,128)S(1)}, f32[144,128]{1,0:T(8,128)S(1)}, u32[]{:S(2)}, u32[]{:S(2)}) collective-permute-start(f32[144,128]{1,0:T(8,128)S(1)} %get-tuple-element.41), channel_id=1, source_target_pairs={{0,16},{16,32},{32,48},{48,64},{64,80},{80,96},{96,112},{112,128},... | collective-permute-start | bytes 221192 | tf_op jit(solution)/shard_map/ppermute | solution.py:216
  41.7 9.6 %collective-permute-start.8 = (f32[144,128]{1,0:T(8,128)S(1)}, f32[144,128]{1,0:T(8,128)S(1)}, u32[]{:S(2)}, u32[]{:S(2)}) collective-permute-start(f32[144,128]{1,0:T(8,128)S(1)} %get-tuple-element.42), channel_id=1, source_target_pairs={{0,4},{4,8},{8,12},{12,0},{1,5},{5,9},{9,13},{13,1},{2,6},{6,10},{... | collective-permute-start | bytes 221192 | tf_op jit(solution)/shard_map/ppermute | solution.py:216
  44.6 6.7 %collective-permute-start.9 = (f32[24,128]{1,0:T(8,128)S(1)}, f32[24,128]{1,0:T(8,128)S(1)}, u32[]{:S(2)}, u32[]{:S(2)}) collective-permute-start(f32[24,128]{1,0:T(8,128)S(1)} %get-tuple-element.43), channel_id=1, source_target_pairs={{0,20},{4,24},{8,28},{12,16},{16,36},{20,40},{24,44},{28,32},{32,5... | collective-permute-start | bytes 36872 | tf_op jit(solution)/shard_map/ppermute | solution.py:226
  51.4 15.5 %collective-permute-start.10 = (f32[864,128]{1,0:T(8,128)S(1)}, f32[864,128]{1,0:T(8,128)S(1)}, u32[]{:S(2)}, u32[]{:S(2)}) collective-permute-start(f32[864,128]{1,0:T(8,128)S(1)} %finish.2.own), channel_id=1, source_target_pairs={{0,1},{1,2},{2,3},{3,0},{4,5},{5,6},{6,7},{7,4},{8,9},{9,10},{10,1... | collective-permute-start | bytes 1327112 | tf_op jit(solution)/shard_map/ppermute | solution.py:216
  52.8 14.8 %collective-permute-start.11 = (f32[864,128]{1,0:T(8,128)S(1)}, f32[864,128]{1,0:T(8,128)S(1)}, u32[]{:S(2)}, u32[]{:S(2)}) collective-permute-start(f32[864,128]{1,0:T(8,128)S(1)} %finish.2.own), channel_id=1, source_target_pairs={{0,3},{1,0},{2,1},{3,2},{4,7},{5,4},{6,5},{7,6},{8,11},{9,8},{10,9... | collective-permute-start | bytes 1327112 | tf_op jit(solution)/shard_map/ppermute | solution.py:216
  55.5 8.6 %collective-permute-start.21 = (f32[144,128]{1,0:T(8,128)S(1)}, f32[144,128]{1,0:T(8,128)S(1)}, u32[]{:S(2)}, u32[]{:S(2)}) collective-permute-start(f32[144,128]{1,0:T(8,128)S(1)} %get-tuple-element.54), channel_id=1, source_target_pairs={{0,16},{16,32},{32,48},{48,64},{64,80},{80,96},{96,112},{112,128},... | collective-permute-start | bytes 221192 | tf_op jit(solution)/shard_map/ppermute | solution.py:216
  55.6 8.5 %collective-permute-start.22 = (f32[144,128]{1,0:T(8,128)S(1)}, f32[144,128]{1,0:T(8,128)S(1)}, u32[]{:S(2)}, u32[]{:S(2)}) collective-permute-start(f32[144,128]{1,0:T(8,128)S(1)} %get-tuple-element.55), channel_id=1, source_target_pairs={{0,4},{4,8},{8,12},{12,0},{1,5},{5,9},{9,13},{13,1},{2,6},{6,10},{... | collective-permute-start | bytes 221192 | tf_op jit(solution)/shard_map/ppermute | solution.py:216
  57.3 6.7 %collective-permute-start.23 = (f32[24,128]{1,0:T(8,128)S(1)}, f32[24,128]{1,0:T(8,128)S(1)}, u32[]{:S(2)}, u32[]{:S(2)}) collective-permute-start(f32[24,128]{1,0:T(8,128)S(1)} %get-tuple-element.56), channel_id=1, source_target_pairs={{0,20},{4,24},{8,28},{12,16},{16,36},{20,40},{24,44},{28,32},{32,5... | collective-permute-start | bytes 36872 | tf_op jit(solution)/shard_map/ppermute | solution.py:226
  64.1 12.6 %collective-permute-start.24 = (f32[864,128]{1,0:T(8,128)S(1)}, f32[864,128]{1,0:T(8,128)S(1)}, u32[]{:S(2)}, u32[]{:S(2)}) collective-permute-start(f32[864,128]{1,0:T(8,128)S(1)} %finish.3.own), channel_id=1, source_target_pairs={{0,1},{1,2},{2,3},{3,0},{4,5},{5,6},{6,7},{7,4},{8,9},{9,10},{10,1... | collective-permute-start | bytes 1327112 | tf_op jit(solution)/shard_map/ppermute | solution.py:216
  64.3 13.2 %collective-permute-start.25 = (f32[864,128]{1,0:T(8,128)S(1)}, f32[864,128]{1,0:T(8,128)S(1)}, u32[]{:S(2)}, u32[]{:S(2)}) collective-permute-start(f32[864,128]{1,0:T(8,128)S(1)} %finish.3.own), channel_id=1, source_target_pairs={{0,3},{1,0},{2,1},{3,2},{4,7},{5,4},{6,5},{7,6},{8,11},{9,8},{10,9... | collective-permute-start | bytes 1327112 | tf_op jit(solution)/shard_map/ppermute | solution.py:216
  66.9 10.6 %copy-start.1 = (f32[864,128]{1,0:T(8,128)}, f32[864,128]{1,0:T(8,128)S(1)}, u32[]{:S(2)}) copy-start(f32[864,128]{1,0:T(8,128)S(1)} %collective-permute-done.10.left) | copy-start | bytes 1327108
  67.6 16.4 %collective-permute-start.12 = (f32[432,128]{1,0:T(8,128)}, f32[432,128]{1,0:T(8,128)S(1)}, u32[]{:S(2)}, u32[]{:S(2)}) collective-permute-start(f32[432,128]{1,0:T(8,128)} %slice.64), channel_id=1, source_target_pairs={{0,1},{1,2},{2,3},{3,0},{4,5},{5,6},{6,7},{7,4},{8,9},{9,10},{10,1... | collective-permute-start | bytes 663560 | tf_op jit(solution)/shard_map/ppermute | solution.py:216
  67.6 10.6 %copy-start.3 = (f32[864,128]{1,0:T(8,128)}, f32[864,128]{1,0:T(8,128)S(1)}, u32[]{:S(2)}) copy-start(f32[864,128]{1,0:T(8,128)S(1)} %collective-permute-done.11.right) | copy-start | bytes 1327108
  68.4 15.6 %collective-permute-start.13 = (f32[432,128]{1,0:T(8,128)}, f32[432,128]{1,0:T(8,128)}, u32[]{:S(2)}, u32[]{:S(2)}) collective-permute-start(f32[432,128]{1,0:T(8,128)} %slice.65), channel_id=1, source_target_pairs={{0,3},{1,0},{2,1},{3,2},{4,7},{5,4},{6,5},{7,6},{8,11},{9,8},{10,9... | collective-permute-start | bytes 663560 | tf_op jit(solution)/shard_map/ppermute | solution.py:216
  77.5 10.1 %collective-permute-start.26 = (f32[432,128]{1,0:T(8,128)}, f32[432,128]{1,0:T(8,128)}, u32[]{:S(2)}, u32[]{:S(2)}) collective-permute-start(f32[432,128]{1,0:T(8,128)} %slice.66), channel_id=1, source_target_pairs={{0,1},{1,2},{2,3},{3,0},{4,5},{5,6},{6,7},{7,4},{8,9},{9,10},{10,1... | collective-permute-start | bytes 663560 | tf_op jit(solution)/shard_map/ppermute | solution.py:216
  77.5 3.4 %copy-start.2 = (f32[864,128]{1,0:T(8,128)S(1)}, f32[864,128]{1,0:T(8,128)}, u32[]{:S(2)}) copy-start(f32[864,128]{1,0:T(8,128)} %copy-done.1) | copy-start | bytes 1327108
  78.2 9.4 %collective-permute-start.27 = (f32[432,128]{1,0:T(8,128)}, f32[432,128]{1,0:T(8,128)}, u32[]{:S(2)}, u32[]{:S(2)}) collective-permute-start(f32[432,128]{1,0:T(8,128)} %slice.67), channel_id=1, source_target_pairs={{0,3},{1,0},{2,1},{3,2},{4,7},{5,4},{6,5},{7,6},{8,11},{9,8},{10,9... | collective-permute-start | bytes 663560 | tf_op jit(solution)/shard_map/ppermute | solution.py:216
  80.9 1.0 %copy-start.4 = (f32[864,128]{1,0:T(8,128)S(1)}, f32[864,128]{1,0:T(8,128)}, u32[]{:S(2)}) copy-start(f32[864,128]{1,0:T(8,128)} %copy-done.3) | copy-start | bytes 1327108

commit v2 on v0

v2 whole, which is shorter than its diff:
```python
import jax
import jax.numpy as jnp
import numpy as np
from jax import lax
from jax.experimental import pallas as pl
from jax.experimental.pallas import tpu as pltpu
from jax.sharding import PartitionSpec as P

ORDER = 6
SIDE = ORDER + 1
NZ = 24
LANES = 128
PARTS = 2
ROWS = 56
CELL_ROWS = SIDE * ROWS
KPAD = 400
LAYER = NZ * ROWS
XROWS = 3 * ORDER * ROWS + KPAD
YROWS = LAYER + ROWS
F32 = jnp.float32
BF16 = jnp.bfloat16
LIMIT = 48 * 1024 * 1024

LINES = (
    [(0, y) for y in range(6)]
    + [(x, 0) for x in range(1, 6)]
    + [(1, 1), (2, 1), (3, 1)]
    + [(4, 1), (5, 1)]
    + [(x, y) for x in range(1, 6) for y in range(2, 6)]
)
LINES1 = 14
LINES2 = 36 - LINES1
SET1 = LINES1 * NZ
SET2 = LINES2 * NZ
EDGE = 6 * NZ
PLANE = 7 * NZ
PLACES = {line: index for index, line in enumerate(LINES)}
PLACES.update({(6, y): 36 + y for y in range(7)})
PLACES.update({(x, 6): 43 + x for x in range(6)})


def selection():
    chosen = np.zeros((KPAD, SIDE**3), np.float32)
    for (p, q), row in PLACES.items():
        for r in range(SIDE):
            chosen[r * ROWS + row, (p * SIDE + q) * SIDE + r] = 1.0
    return chosen


def split(values):
    high = values.astype(BF16)
    return high, (values - high.astype(F32)).astype(BF16)


def dot(a, b):
    return jnp.dot(a, b, preferred_element_type=F32)


def line(index):
    return pl.ds(index * NZ, NZ)


def arrange_kernel(w, w1, w2):
    for index, (x, y) in enumerate(LINES):
        if index < LINES1:
            w1[line(index)] = w[line(x * 6 + y)]
        else:
            w2[line(index - LINES1)] = w[line(x * 6 + y)]


def hold_kernel(w2, left1, out):
    out[...] = w2[...]


def prepare_kernel(me, cell, chosen, chosen_t, rotation, k_high, k_low, r_high, r_low, far_high, far_low):
    high, low = split(cell[...])
    k_high[...] = dot(dot(chosen[...], high).astype(BF16), chosen_t[...]).astype(BF16)
    k_low[...] = dot(dot(chosen[...], low).astype(BF16), chosen_t[...]).astype(BF16)
    for index, steps in enumerate((0, -1, 1, 2)):
        owner = lax.rem(me[0] + steps + 4, 4)
        high, low = split(rotation[pl.ds(pl.multiple_of(owner * 256, 256), 256)])
        if index < 3:
            r_high[pl.ds(index * 256, 256)] = high
            r_low[pl.ds(index * 256, 256)] = low
        else:
            far_high[...] = high
            far_low[...] = low


def turned(values, r_high, r_low):
    high, low = split(values)
    rh = r_high[...]
    return dot(high, rh) + (dot(low, rh) + dot(high, r_low[...]))


def near_kernel(own, left, right, r_high, r_low, total):
    total[...] = turned(jnp.concatenate([own[...], left[...], right[...]], 1), r_high, r_low)


def far_kernel(total, far, far_high, far_low, z1, pull_x):
    values = total[...] + turned(far[...], far_high, far_low)
    for part in range(2):
        lanes = values[:, part * LANES : (part + 1) * LANES]
        z1[pl.ds(part * SET1, SET1)] = lanes
        pull_x[pl.ds(part * EDGE, EDGE)] = lanes[:EDGE]


def edge_kernel(z1, gx, pull_y):
    for part in range(2):
        base = part * PLANE
        pull_y[pl.ds(base, NZ)] = z1[pl.ds(part * SET1, NZ)]
        pull_y[pl.ds(base + NZ, 5 * NZ)] = z1[pl.ds(part * SET1 + EDGE, 5 * NZ)]
        pull_y[pl.ds(base + EDGE, NZ)] = gx[pl.ds(part * EDGE, NZ)]


def cells_product(parts, x_ref, y_ref, xh_ref, xl_ref, k_high, k_low):
    kh = k_high[...]
    kl = k_low[...]
    step = ORDER * ROWS
    for part in range(parts):
        high, low = split(x_ref[part])
        xh_ref[...] = high
        xl_ref[...] = low
        y_ref[part] = jnp.zeros((YROWS, LANES), F32)
        for pair in range(2):
            first, second = 2 * pair * step, (2 * pair + 1) * step
            xh = jnp.concatenate([xh_ref[first : first + KPAD], xh_ref[second : second + KPAD]], 1)
            xl = jnp.concatenate([xl_ref[first : first + KPAD], xl_ref[second : second + KPAD]], 1)
            product = dot(kh, xh) + (dot(kh, xl) + dot(kl, xh))
            y_ref[part, first : first + CELL_ROWS] += product[:CELL_ROWS, :LANES]
            y_ref[part, second : second + CELL_ROWS] += product[:CELL_ROWS, LANES:]
        y_ref[part, 0:ROWS] += y_ref[part, LAYER:YROWS]


def every(start, count):
    return pl.ds(start, count, stride=NZ)


def first_kernel(
    z1, total2, far2, far_high, far_low, gx, gy, k_high, k_low, local, scale,
    z2, p_out, f0, f6, s0, s6, x_ref, y_ref, xh_ref, xl_ref,
):
    values = total2[...] + turned(far2[...], far_high, far_low)
    for part in range(PARTS):
        z2[pl.ds(part * SET2, SET2)] = values[:, part * LANES : (part + 1) * LANES]
    for part in range(PARTS):
        xs = x_ref.at[part]
        xs[LAYER:] = jnp.zeros((XROWS - LAYER, LANES), F32)
        for z in range(NZ):
            at = z * ROWS
            xs[at : at + LINES1] = z1[every(part * SET1 + z, LINES1)]
            xs[at + LINES1 : at + 36] = z2[every(part * SET2 + z, LINES2)]
            xs[at + 36 : at + 42] = gx[every(part * EDGE + z, 6)]
            xs[at + 42 : at + 43] = gy[part * PLANE + EDGE + z : part * PLANE + EDGE + z + 1]
            xs[at + 43 : at + 49] = gy[every(part * PLANE + z, 6)]
            xs[at + 49 : at + 56] = jnp.zeros((7, LANES), F32)
        xs[LAYER:YROWS] = xs[0:ROWS]
    cells_product(PARTS, x_ref, y_ref, xh_ref, xl_ref, k_high, k_low)
    for part in range(PARTS):
        ps = p_out.at[part]
        ps[...] = (y_ref[part, 0:LAYER] + local[...] * x_ref[part, 0:LAYER]) * scale[0]
        base = part * PLANE
        for z in range(NZ):
            at = z * ROWS
            s6[every(base + z, 7)] = ps[at + 36 : at + 43]
            s0[every(base + z, 6)] = ps[at : at + 6]
            s0[base + EDGE + z : base + EDGE + z + 1] = ps[at + 43 : at + 44]
            f0[base + z : base + z + 1] = ps[at : at + 1]
            f0[every(base + NZ + z, 5)] = ps[at + 6 : at + 11]
            f0[base + EDGE + z : base + EDGE + z + 1] = ps[at + 36 : at + 37]
            f6[every(base + z, 6)] = ps[at + 43 : at + 49]
            f6[base + EDGE + z : base + EDGE + z + 1] = ps[at + 42 : at + 43]


def corner_kernel(s0, s6, r0, r6, t0, t6):
    t0[...] = s0[...]
    t6[...] = s6[...]
    for part in range(PARTS):
        low = pl.ds(part * PLANE, NZ)
        high = pl.ds(part * PLANE + EDGE, NZ)
        t0[low] += r0[low]
        t0[high] += r6[low]
        t6[low] += r0[high]
        t6[high] += r6[high]


def second_kernel(
    p_in, r0, r6, t0, t6, q0, q6, v1, v2, k_high, k_low, local, scale,
    out1, out2, push_x, push_y, push_c, x_ref, y_ref, xh_ref, xl_ref, n0, n6,
):
    n0[...] = t0[...] + q0[...]
    n6[...] = t6[...] + q6[...]
    for part in range(PARTS):
        xs = x_ref.at[part]
        xs[0:LAYER] = p_in[part]
        xs[LAYER:] = jnp.zeros((XROWS - LAYER, LANES), F32)
        base = part * PLANE
        for z in range(NZ):
            at = z * ROWS
            xs[at : at + 6] = n0[every(base + z, 6)]
            xs[at + 6 : at + 11] += r0[every(base + NZ + z, 5)]
            xs[at + 36 : at + 43] = n6[every(base + z, 7)]
            xs[at + 43 : at + 44] = n0[base + EDGE + z : base + EDGE + z + 1]
            xs[at + 44 : at + 49] += r6[every(base + NZ + z, 5)]
        xs[LAYER:YROWS] = xs[0:ROWS]
    cells_product(PARTS, x_ref, y_ref, xh_ref, xl_ref, k_high, k_low)
    for part in range(PARTS):
        ys = y_ref.at[part]
        ys[0:LAYER] = (ys[0:LAYER] + local[...] * x_ref[part, 0:LAYER]) * (2.0 * scale[0])
        for z in range(NZ):
            at = z * ROWS
            out1[every(part * SET1 + z, LINES1)] = ys[at : at + LINES1]
            out2[every(part * SET2 + z, LINES2)] = ys[at + LINES1 : at + 36]
            push_x[every(part * EDGE + z, 6)] = ys[at + 36 : at + 42]
            push_c[part * NZ + z : part * NZ + z + 1] = ys[at + 42 : at + 43]
            push_y[every(part * EDGE + z, 6)] = ys[at + 43 : at + 49]
    out1[...] -= v1[...]
    out2[...] -= v2[...]


def last_kernel(q1, q2, rx, ry, rc, out):
    for part in range(PARTS):
        lanes = pl.ds(part * LANES, LANES)
        base = part * EDGE
        for index, (x, y) in enumerate(LINES):
            if index < LINES1:
                value = q1[pl.ds(part * SET1 + index * NZ, NZ)]
                if x == 0:
                    value = value + rx[pl.ds(base + y * NZ, NZ)]
                if y == 0:
                    value = value + ry[pl.ds(base + x * NZ, NZ)]
                if x == 0 and y == 0:
                    value = value + rc[pl.ds(part * NZ, NZ)]
            else:
                value = q2[pl.ds(part * SET2 + (index - LINES1) * NZ, NZ)]
            out[line(x * 6 + y), lanes] = value


VM = pl.BlockSpec(memory_space=pltpu.VMEM)
SM = pl.BlockSpec(memory_space=pltpu.SMEM)


def call(kernel, name, in_specs, shapes, scratch=()):
    inputs, outputs = len(in_specs), len(shapes)

    def body(*refs):
        kernel(*refs[:inputs], *refs[inputs + 1 : inputs + 1 + outputs], *refs[inputs + outputs + 2 :])

    return pl.pallas_call(
        body,
        name=name,
        in_specs=in_specs + [pl.BlockSpec(memory_space=pl.ANY)],
        out_specs=[VM] * outputs + [pl.BlockSpec(memory_space=pl.ANY)],
        out_shape=[jax.ShapeDtypeStruct(*shape) for shape in shapes] + [jax.ShapeDtypeStruct((8, LANES), F32)],
        scratch_shapes=list(scratch),
        compiler_params=pltpu.CompilerParams(vmem_limit_bytes=LIMIT),
        cost_estimate=pl.CostEstimate(flops=1, bytes_accessed=1, transcendentals=0),
        input_output_aliases={inputs: outputs},
    )


class Sequence:
    def __init__(self):
        self.token = jnp.zeros((8, LANES), F32)

    def __call__(self, kernel, *operands):
        *results, self.token = kernel(*operands, self.token)
        return results


def rows_of(count):
    return ((count, LANES), F32)


def passed_along(value, axis, steps):
    count = lax.axis_size(axis)
    return lax.ppermute(value, axis, [(s, (s + steps) % count) for s in range(count)])


def passed_diagonal(value, steps):
    slabs, faces = lax.axis_size("slab"), lax.axis_size("face")
    pairs = [
        (a * faces + b, ((a + steps) % slabs) * faces + (b + steps) % faces)
        for a in range(slabs)
        for b in range(faces)
    ]
    return lax.ppermute(value, ("slab", "face"), pairs)


def local_term(shifted):
    by_layer = jnp.transpose(shifted, (2, 0, 1))
    return jnp.concatenate(
        [
            by_layer[:, 0],
            by_layer[:, 1:, 0],
            by_layer[:, 1:, 1],
            by_layer[:, 1:, 2:].reshape(NZ, 20),
            jnp.zeros((NZ, ROWS - 36), F32),
        ],
        1,
    ).reshape(LAYER, 1)


def shards(wavefunctions, rotation, cell_matrix, potential, center, halfwidth):
    run = Sequence()
    chosen = selection()
    me = lax.axis_index("band").astype(jnp.int32).reshape(1)
    scale = 1.0 / halfwidth
    operator_scratch = [
        pltpu.VMEM((PARTS, XROWS, LANES), F32),
        pltpu.VMEM((PARTS, YROWS, LANES), F32),
        pltpu.VMEM((XROWS, LANES), BF16),
        pltpu.VMEM((XROWS, LANES), BF16),
    ]
    edge, plane = rows_of(PARTS * EDGE), rows_of(PARTS * PLANE)
    wide1, wide2 = ((SET1, 256), F32), ((SET2, 256), F32)
    set1, set2 = rows_of(PARTS * SET1), rows_of(PARTS * SET2)

    w1, w2 = run(call(arrange_kernel, "arrange", [VM], [wide1, wide2]), wavefunctions.reshape(36 * NZ, 256))
    left1 = passed_along(w1, "band", 1)
    right1 = passed_along(w1, "band", -1)
    right2 = passed_along(w2, "band", -1)
    local = local_term(potential - center[0])
    k_high, k_low, r_high, r_low, far_high, far_low = run(
        call(
            prepare_kernel,
            "prepare",
            [SM] + [VM] * 4,
            [((KPAD, KPAD), BF16)] * 2 + [((768, 256), BF16)] * 2 + [((256, 256), BF16)] * 2,
        ),
        me, cell_matrix, jnp.asarray(chosen, BF16), jnp.asarray(chosen.T, BF16), rotation,
    )
    common = (k_high, k_low, local, scale)
    far1 = passed_along(left1, "band", 1)
    (held2,) = run(call(hold_kernel, "hold", [VM, pl.BlockSpec(memory_space=pl.ANY)], [wide2]), w2, left1)
    left2 = passed_along(held2, "band", 1)
    (total1,) = run(call(near_kernel, "near1", [VM] * 5, [wide1]), w1, left1, right1, r_high, r_low)
    z1, pull_x = run(call(far_kernel, "far1", [VM] * 4, [set1, edge]), total1, far1, far_high, far_low)
    gx = passed_along(pull_x, "slab", -1)
    far2 = passed_along(right2, "band", -1)
    (total2,) = run(call(near_kernel, "near2", [VM] * 5, [wide2]), w2, left2, right2, r_high, r_low)
    (pull_y,) = run(call(edge_kernel, "edge", [VM] * 2, [plane]), z1, gx)
    gy = passed_along(pull_y, "face", -1)

    z2, p, f0, f6, s0, s6 = run(
        call(
            first_kernel,
            "first",
            [VM] * 10 + [SM],
            [set2, ((PARTS, LAYER, LANES), F32)] + [plane] * 4,
            operator_scratch,
        ),
        z1, total2, far2, far_high, far_low, gx, gy, *common,
    )
    r0 = passed_along(f6, "face", 1)
    r6 = passed_along(f0, "face", -1)
    t0, t6 = run(call(corner_kernel, "corner", [VM] * 4, [plane] * 2), s0, s6, r0, r6)
    q0 = passed_along(t6, "slab", 1)
    q6 = passed_along(t0, "slab", -1)
    q1, q2, push_x, push_y, push_c = run(
        call(
            second_kernel,
            "second",
            [VM] * 12 + [SM],
            [set1, set2, edge, edge, rows_of(PARTS * NZ)],
            operator_scratch + [pltpu.VMEM((PARTS * PLANE, LANES), F32)] * 2,
        ),
        p, r0, r6, t0, t6, q0, q6, z1, z2, *common,
    )
    rx = passed_along(push_x, "slab", 1)
    ry = passed_along(push_y, "face", 1)
    rc = passed_diagonal(push_c, 1)
    (result,) = run(call(last_kernel, "last", [VM] * 5, [((36 * NZ, 256), F32)]), q1, q2, rx, ry, rc)
    return result.reshape(6, 6, NZ, 256)


def solution(mesh):
    placed = (
        P("slab", "face", None, "band"),
        P(None, "band"),
        P(),
        P("slab", "face", None),
        P(),
        P(),
    )
    return jax.shard_map(
        shards,
        mesh=mesh,
        in_specs=placed,
        out_specs=P("slab", "face", None, "band"),
        check_vma=False,
    )
```

time: 199 us -> 79.3 us (0.40)
  waiting for transfers between devices: 80.6 us -> 28.4 us
  matrix products: 48.2 us -> 0 us
  local copies, waits for them, and re-layouts: 31.8 us -> 7.93 us
  starting transfers between devices: 13.3 us -> 29 us
  between operations: 15.2 us -> 1.5 us
  Pallas kernels: 0 us -> 12.1 us
  other arithmetic: 9.14 us -> 0.01 us
    all_gather x1 -> x0, waiting for transfers between devices: 51.1 us -> none  [shards(): lax.all_gather(wavefunctions, 'band', axis=3, tiled=True)]
    dot_general x3 -> x0, matrix products: 48.2 us -> none  [the longest x2 43.3 us: cell_apply(): jnp.einsum('ijkpqr,apbqcrn->aibjckn', kernel, local_cells, precision=high...]
    reshape x11 -> x3, local copies, waits for them, and re-layouts: 16.9 us -> 0.35 us  [the longest x1 0.25 us: local_term(): return jnp.concatenate([by_layer[:, 0], by_layer[:, 1:, 0], by_layer[:, 1...]
    ppermute x8 -> x15, starting transfers between devices: 13.3 us -> 29 us  [the longest x14 28.7 us: passed_along(): lax.ppermute(value, axis, [(s, (s + steps) % count) for s in range(count)])]
    slice x12 -> x3, local copies, waits for them, and re-layouts: 12.2 us -> 0.01 us  [the longest x2 0.01 us: local_term(): by_layer[:, 1:, 2:].reshape(NZ, 20)]
    pallas_call x0 -> x11, Pallas kernels: none -> 12.1 us  [__call__(): *results, self.token = kernel(*operands, self.token)]
    unnamed x12 -> x16, local copies, waits for them, and re-layouts: 1.07 us -> 7.23 us
    concatenate x8 -> x0, other arithmetic: 5.14 us -> none  [the longest x4 4.8 us: split_cells(): return jnp.concatenate([regular, closing], which_axis + 1)]
  transfers between devices with their start and end apart: 9 -> 15, of which waited for: 8 -> 8; matrix products, arithmetic and copies ran while one was open for 3% -> 1% of each run, Pallas kernels for 0% -> 7%
where the time goes in v2:
time: 79.3 us; the launch traced here: 78.9 us
  starting transfers between devices  29 us (37%)
  waiting for transfers between devices  28.4 us (36%)
  Pallas kernels  12.1 us (15%)
  local copies, waits for them, and re-layouts  7.93 us (10%)
  between operations  1.5 us (2%)
    ppermute x14, starting transfers between devices, passed_along(): lax.ppermute(value, axis, [(s, (s + steps) % count) for s in range(count)])  28.7 us
    ppermute x14, waiting for transfers between devices, passed_along(): lax.ppermute(value, axis, [(s, (s + steps) % count) for s in range(count)])  18.7 us
    pallas_call x11, Pallas kernels, __call__(): *results, self.token = kernel(*operands, self.token)  12.1 us
    ppermute x1, waiting for transfers between devices, passed_diagonal(): return lax.ppermute(value, ('slab', 'face'), pairs)  9.68 us
    unnamed x16, local copies, waits for them, and re-layouts  7.23 us
  transfers between devices with their start and end apart: 15, of which 8 were waited for; matrix products, arithmetic and copies ran while one was open for 1% of the time, Pallas kernels for 7%

profile of v2, /device:TPU:1, one launch (start us, length us, event | category | flops | bytes accessed | tf_op | source)
XLA Modules:
  0.0 78.9 jit_solution(4827401274442333375)
XLA Ops:
  0.0 1.2 %copy-done.1 = f32[6,6,24,256]{3,2,1,0:T(8,128)S(1)} copy-done((f32[6,6,24,256]{3,2,1,0:T(8,128)S(1)}, f32[6,6,24,256]{3,2,1,0:T(8,128)}, u32[]{:S(2)}) %copy-start.1) | copy-done | bytes 884760
  1.2 0.8 arrange.1
  2.0 2.1 %collective-permute-start = (f32[336,256]{1,0:T(8,128)}, f32[336,256]{1,0:T(8,128)S(1)}, u32[]{:S(2)}, u32[]{:S(2)}) collective-permute-start(f32[336,256]{1,0:T(8,128)} %get-tuple-element.43.refs_0_), channel_id=1, source_target_pairs={{0,1},{1,2},{2,3},{3,0},{4,5},{5,6},{6,7},{7,4},{8,9},{9,10},{10,1... | collective-permute-start | bytes 1032200 | tf_op jit(solution)/shard_map/ppermute | solution.py:277
  4.1 1.4 %collective-permute-start.4 = (f32[528,256]{1,0:T(8,128)S(1)}, f32[528,256]{1,0:T(8,128)S(1)}, u32[]{:S(2)}, u32[]{:S(2)}) collective-permute-start(f32[528,256]{1,0:T(8,128)S(1)} %get-tuple-element.47.refs_0_), channel_id=1, source_target_pairs={{0,3},{1,0},{2,1},{3,2},{4,7},{5,4},{6,5},{7,6},{8,11},{9,8},{10,9... | collective-permute-start | bytes 1622024 | tf_op jit(solution)/shard_map/ppermute | solution.py:277
  5.5 1.5 %collective-permute-start.1 = (f32[336,256]{1,0:T(8,128)}, f32[336,256]{1,0:T(8,128)}, u32[]{:S(2)}, u32[]{:S(2)}) collective-permute-start(f32[336,256]{1,0:T(8,128)} %get-tuple-element.43.refs_0_), channel_id=1, source_target_pairs={{0,3},{1,0},{2,1},{3,2},{4,7},{5,4},{6,5},{7,6},{8,11},{9,8},{10,9... | collective-permute-start | bytes 1032200 | tf_op jit(solution)/shard_map/ppermute | solution.py:277
  7.0 4.5 %collective-permute-done.refs_1_ = f32[336,256]{1,0:T(8,128)S(1)} collective-permute-done((f32[336,256]{1,0:T(8,128)}, f32[336,256]{1,0:T(8,128)S(1)}, u32[]{:S(2)}, u32[]{:S(2)}) %collective-permute-start) | collective-permute-done | bytes 344096 | tf_op jit(solution)/shard_map/ppermute | solution.py:277
  11.5 1.6 %collective-permute-start.2 = (f32[336,256]{1,0:T(8,128)S(1)}, f32[336,256]{1,0:T(8,128)}, u32[]{:S(2)}, u32[]{:S(2)}) collective-permute-start(f32[336,256]{1,0:T(8,128)S(1)} %collective-permute-done.refs_1_), channel_id=1, source_target_pairs={{0,1},{1,2},{2,3},{3,0},{4,5},{5,6},{6,7},{7,4},{8,9},{9,10},{10,1... | collective-permute-start | bytes 1032200 | tf_op jit(solution)/shard_map/ppermute | solution.py:277
  13.0 1.2 %copy-done = f32[1024,256]{1,0:T(8,128)S(1)} copy-done((f32[1024,256]{1,0:T(8,128)S(1)}, f32[1024,256]{1,0:T(8,128)}, u32[]{:S(2)}) %copy-start) | copy-done | bytes 1048600
  14.3 1.0 %copy-done.4 = f32[343,343]{1,0:T(8,128)S(1)} copy-done((f32[343,343]{1,0:T(8,128)S(1)}, f32[343,343]{1,0:T(8,128)}, u32[]{:S(2)}) %copy-start.4) | copy-done | bytes 470620
  15.3 1.0 %copy-done.5 = bf16[343,400]{1,0:T(8,128)(2,1)S(1)} copy-done((bf16[343,400]{1,0:T(8,128)(2,1)S(1)}, bf16[343,400]{1,0:T(8,128)(2,1)}, u32[]{:S(2)}) %copy-start.5) | copy-done | bytes 274424
  16.3 1.0 %copy-done.6 = bf16[400,343]{1,0:T(8,128)(2,1)S(1)} copy-done((bf16[400,343]{1,0:T(8,128)(2,1)S(1)}, bf16[400,343]{1,0:T(8,128)(2,1)}, u32[]{:S(2)}) %copy-start.6) | copy-done | bytes 274424
  17.3 1.2 %prepare.1 = (bf16[400,400]{1,0:T(8,128)(2,1)S(1)}, bf16[400,400]{1,0:T(8,128)(2,1)S(1)}, bf16[768,256]{1,0:T(8,128)(2,1)S(1)}, bf16[768,256]{1,0:T(8,128)(2,1)S...) custom-call(s32[1]{0:T(128)} %bitcast.1.refs_0_, ...), custom_call_target="tpu_custom_call", output_to_operand_aliasing={{6}: (5, {})} | custom-call | flops 1 | bytes 1 | tf_op jit(solution)/shard_map/prepare/pallas_call | solution.py:267
  18.5 1.6 %collective-permute-start.3 = (f32[528,256]{1,0:T(8,128)S(1)}, f32[528,256]{1,0:T(8,128)S(1)}, u32[]{:S(2)}, u32[]{:S(2)}) collective-permute-start(f32[528,256]{1,0:T(8,128)S(1)} %get-tuple-element.55), channel_id=1, source_target_pairs={{0,1},{1,2},{2,3},{3,0},{4,5},{5,6},{6,7},{7,4},{8,9},{9,10},{10,1... | collective-permute-start | bytes 1622024 | tf_op jit(solution)/shard_map/ppermute | solution.py:277
  20.1 1.2 %collective-permute-start.5 = (f32[528,256]{1,0:T(8,128)S(1)}, f32[528,256]{1,0:T(8,128)S(1)}, u32[]{:S(2)}, u32[]{:S(2)}) collective-permute-start(f32[528,256]{1,0:T(8,128)S(1)} %collective-permute-done.4.refs_2_), channel_id=1, source_target_pairs={{0,3},{1,0},{2,1},{3,2},{4,7},{5,4},{6,5},{7,6},{8,11},{9,8},{10,9... | collective-permute-start | bytes 1622024 | tf_op jit(solution)/shard_map/ppermute | solution.py:277
  22.0 2.3 %collective-permute-done.1.refs_2_ = f32[336,256]{1,0:T(8,128)} collective-permute-done((f32[336,256]{1,0:T(8,128)}, f32[336,256]{1,0:T(8,128)}, u32[]{:S(2)}, u32[]{:S(2)}) %collective-permute-start.1) | collective-permute-done | bytes 344096 | tf_op jit(solution)/shard_map/ppermute | solution.py:277
  24.2 1.7 %near1.1 = (f32[336,256]{1,0:T(8,128)S(1)}, f32[8,128]{1,0:T(8,128)S(1)}) custom-call(f32[336,256]{1,0:T(8,128)} %get-tuple-element.43.refs_0_, f32[336,256]{1,0:T(8,128)S(1)} %collective-permute-done.refs_1_, f32[336,256]{1,0:T(8,128)} %collective-permute-done.1.refs_2_, ...), custom_call_target="tpu_custom_call", output_to_operand_aliasing={{1}: (5, {})} | custom-call | flops 1 | bytes 1 | tf_op jit(solution)/shard_map/near1/pallas_call | solution.py:267
  25.9 0.0 collective-permute-done.2.refs_1_
  25.9 1.3 %far1.1 = (f32[672,128]{1,0:T(8,128)S(1)}, f32[288,128]{1,0:T(8,128)S(1)}, f32[8,128]{1,0:T(8,128)S(1)}) custom-call(f32[336,256]{1,0:T(8,128)S(1)} %get-tuple-element.50.refs_0_, f32[336,256]{1,0:T(8,128)} %collective-permute-done.2.refs_1_, bf16[256,256]{1,0:T(8,128)(2,1)S(1)} %get-tuple-element.51.refs_2_.refs_3_, ...), custom_call_target="tpu_custom_call", output_to_operand_aliasing={{2}: (4, {})} | custom-call | flops 1 | bytes 1 | tf_op jit(solution)/shard_map/far1/pallas_call | solution.py:267
  27.2 8.3 %collective-permute-start.6 = (f32[288,128]{1,0:T(8,128)S(1)}, f32[288,128]{1,0:T(8,128)S(1)}, u32[]{:S(2)}, u32[]{:S(2)}) collective-permute-start(f32[288,128]{1,0:T(8,128)S(1)} %get-tuple-element.58), channel_id=1, source_target_pairs={{0,240},{16,0},{32,16},{48,32},{64,48},{80,64},{96,80},{112,96},{1... | collective-permute-start | bytes 442376 | tf_op jit(solution)/shard_map/ppermute | solution.py:277
  35.5 0.0 collective-permute-done.3.refs_1_
  35.5 0.8 %near2.1 = (f32[528,256]{1,0:T(8,128)S(1)}, f32[8,128]{1,0:T(8,128)S(1)}) custom-call(f32[528,256]{1,0:T(8,128)S(1)} %get-tuple-element.47.refs_0_, f32[528,256]{1,0:T(8,128)S(1)} %collective-permute-done.3.refs_1_, f32[528,256]{1,0:T(8,128)S(1)} %collective-permute-done.4.refs_2_, ...), custom_call_target="tpu_custom_call", output_to_operand_aliasing={{1}: (5, {})} | custom-call | flops 1 | bytes 1 | tf_op jit(solution)/shard_map/near2/pallas_call | solution.py:267
  36.4 0.0 copy-start.2
  36.4 0.8 %copy-done.2 = f32[528,256]{1,0:T(8,128)} copy-done((f32[528,256]{1,0:T(8,128)}, f32[528,256]{1,0:T(8,128)S(1)}, u32[]{:S(2)}) %copy-start.2) | copy-done | bytes 540696
  37.2 0.4 collective-permute-done.6.refs_1_.refs_5_
  37.6 0.7 edge.1
  38.3 4.2 %collective-permute-start.7 = (f32[336,128]{1,0:T(8,128)}, f32[336,128]{1,0:T(8,128)S(1)}, u32[]{:S(2)}, u32[]{:S(2)}) collective-permute-start(f32[336,128]{1,0:T(8,128)} %get-tuple-element.60), channel_id=1, source_target_pairs={{0,12},{4,0},{8,4},{12,8},{1,13},{5,1},{9,5},{13,9},{2,14},{6,2},{... | collective-permute-start | bytes 516104 | tf_op jit(solution)/shard_map/ppermute | solution.py:277
  42.4 0.1 copy.32
  42.5 0.1 copy.33
  42.6 0.1 copy.34
  42.7 0.1 copy.37
  42.8 0.1 concatenate.3
  42.9 0.2 reshape.20.refs_9_.refs_11_
  43.8 2.1 %collective-permute-done.7.refs_6_ = f32[336,128]{1,0:T(8,128)S(1)} collective-permute-done((f32[336,128]{1,0:T(8,128)}, f32[336,128]{1,0:T(8,128)S(1)}, u32[]{:S(2)}, u32[]{:S(2)}) %collective-permute-start.7) | collective-permute-done | bytes 172064 | tf_op jit(solution)/shard_map/ppermute | solution.py:277
  45.9 1.0 %copy-done.3 = f32[528,256]{1,0:T(8,128)S(1)} copy-done((f32[528,256]{1,0:T(8,128)S(1)}, f32[528,256]{1,0:T(8,128)}, u32[]{:S(2)}) %copy-start.3) | copy-done | bytes 540696
  47.0 2.3 %first.1 = (f32[1056,128]{1,0:T(8,128)S(1)}, f32[2,1344,128]{2,1,0:T(8,128)S(1)}, f32[336,128]{1,0:T(8,128)S(1)}, f32[336,128]{1,0:T(8,128)S(1)}, f32[336,128]{1...) custom-call(f32[672,128]{1,0:T(8,128)S(1)} %get-tuple-element.54.refs_0_.refs_7_, ...), custom_call_target="tpu_custom_call", output_to_operand_aliasing={{6}: (11, {})} | custom-call | flops 1 | bytes 1 | tf_op jit(solution)/shard_map/first/pallas_call | solution.py:267
  49.3 0.1 collective-permute-start.8
  49.4 0.5 collective-permute-start.9
  49.9 1.8 %collective-permute-done.8.refs_2_.refs_1_ = f32[336,128]{1,0:T(8,128)S(1)} collective-permute-done((f32[336,128]{1,0:T(8,128)S(1)}, f32[336,128]{1,0:T(8,128)S(1)}, u32[]{:S(2)}, u32[]{:S(2)}) %collective-permute-start.8) | collective-permute-done | bytes 172064 | tf_op jit(solution)/shard_map/ppermute | solution.py:277
  51.7 3.4 %collective-permute-done.9.refs_3_.refs_2_ = f32[336,128]{1,0:T(8,128)S(1)} collective-permute-done((f32[336,128]{1,0:T(8,128)S(1)}, f32[336,128]{1,0:T(8,128)S(1)}, u32[]{:S(2)}, u32[]{:S(2)}) %collective-permute-start.9) | collective-permute-done | bytes 172064 | tf_op jit(solution)/shard_map/ppermute | solution.py:277
  55.2 0.1 collective-permute-start.10
  55.3 5.9 %collective-permute-start.11 = (f32[336,128]{1,0:T(8,128)S(1)}, f32[336,128]{1,0:T(8,128)S(1)}, u32[]{:S(2)}, u32[]{:S(2)}) collective-permute-start(f32[336,128]{1,0:T(8,128)S(1)} %get-tuple-element.70.refs_3_), channel_id=1, source_target_pairs={{0,240},{16,0},{32,16},{48,32},{64,48},{80,64},{96,80},{112,96},{1... | collective-permute-start | bytes 516104 | tf_op jit(solution)/shard_map/ppermute | solution.py:277
  61.2 4.1 %collective-permute-done.10.refs_5_ = f32[336,128]{1,0:T(8,128)S(1)} collective-permute-done((f32[336,128]{1,0:T(8,128)S(1)}, f32[336,128]{1,0:T(8,128)S(1)}, u32[]{:S(2)}, u32[]{:S(2)}) %collective-permute-start.10) | collective-permute-done | bytes 172064 | tf_op jit(solution)/shard_map/ppermute | solution.py:277
  65.3 2.2 %second.1 = (f32[672,128]{1,0:T(8,128)S(1)}, f32[1056,128]{1,0:T(8,128)S(1)}, f32[288,128]{1,0:T(8,128)S(1)}, f32[288,128]{1,0:T(8,128)S(1)}, f32[48,128]{1,0:T(8,128)S(1)}, /*index=5*/f32[8,128]{1,0:T(8,128)S(1)}) custom-call(f32[2,1344,128]{2,1,0:T(8,128)S(1)} %get-tuple-element.64.refs_0_, ...), custom_call_target="tpu_custom_call", output_to_operand_aliasing={{5}: (13, {})} | custom-call | flops 1 | bytes 1 | tf_op jit(solution)/shard_map/second/pallas_call | solution.py:267
  67.5 0.1 collective-permute-start.12
  67.6 0.3 collective-permute-start.13
  67.9 0.3 collective-permute-start.14
  68.2 9.7 %collective-permute-done.14.refs_4_ = f32[48,128]{1,0:T(8,128)S(1)} collective-permute-done((f32[48,128]{1,0:T(8,128)S(1)}, f32[48,128]{1,0:T(8,128)S(1)}, u32[]{:S(2)}, u32[]{:S(2)}) %collective-permute-start.14) | collective-permute-done | bytes 24608 | tf_op jit(solution)/shard_map/ppermute | solution.py:287
  77.9 1.0 %last.1 = (f32[864,256]{1,0:T(8,128)}, f32[8,128]{1,0:T(8,128)S(1)}) custom-call(f32[672,128]{1,0:T(8,128)S(1)} %get-tuple-element.74.refs_0_, f32[1056,128]{1,0:T(8,128)S(1)} %get-tuple-element.75.refs_1_, f32[288,128]{1,0:T(8,128)S(1)} %collective-permute-done.12.refs_2_, ...), custom_call_target="tpu_custom_call", output_to_operand_aliasing={{1}: (5, {})} | custom-call | flops 1 | bytes 1 | tf_op jit(solution)/shard_map/last/pallas_call | solution.py:267
  (23 shorter events, 0.1 us)
Async XLA Ops:
  0.0 1.2 %copy-start.1 = (f32[6,6,24,256]{3,2,1,0:T(8,128)S(1)}, f32[6,6,24,256]{3,2,1,0:T(8,128)}, u32[]{:S(2)}) copy-start(f32[6,6,24,256]{3,2,1,0:T(8,128)} %param.8) | copy-start | bytes 2654212
  2.0 9.5 %collective-permute-start = (f32[336,256]{1,0:T(8,128)}, f32[336,256]{1,0:T(8,128)S(1)}, u32[]{:S(2)}, u32[]{:S(2)}) collective-permute-start(f32[336,256]{1,0:T(8,128)} %get-tuple-element.43.refs_0_), channel_id=1, source_target_pairs={{0,1},{1,2},{2,3},{3,0},{4,5},{5,6},{6,7},{7,4},{8,9},{9,10},{10,1... | collective-permute-start | bytes 1032200 | tf_op jit(solution)/shard_map/ppermute | solution.py:277
  4.1 16.0 %collective-permute-start.4 = (f32[528,256]{1,0:T(8,128)S(1)}, f32[528,256]{1,0:T(8,128)S(1)}, u32[]{:S(2)}, u32[]{:S(2)}) collective-permute-start(f32[528,256]{1,0:T(8,128)S(1)} %get-tuple-element.47.refs_0_), channel_id=1, source_target_pairs={{0,3},{1,0},{2,1},{3,2},{4,7},{5,4},{6,5},{7,6},{8,11},{9,8},{10,9... | collective-permute-start | bytes 1622024 | tf_op jit(solution)/shard_map/ppermute | solution.py:277
  5.5 18.7 %collective-permute-start.1 = (f32[336,256]{1,0:T(8,128)}, f32[336,256]{1,0:T(8,128)}, u32[]{:S(2)}, u32[]{:S(2)}) collective-permute-start(f32[336,256]{1,0:T(8,128)} %get-tuple-element.43.refs_0_), channel_id=1, source_target_pairs={{0,3},{1,0},{2,1},{3,2},{4,7},{5,4},{6,5},{7,6},{8,11},{9,8},{10,9... | collective-permute-start | bytes 1032200 | tf_op jit(solution)/shard_map/ppermute | solution.py:277
  11.5 14.4 %collective-permute-start.2 = (f32[336,256]{1,0:T(8,128)S(1)}, f32[336,256]{1,0:T(8,128)}, u32[]{:S(2)}, u32[]{:S(2)}) collective-permute-start(f32[336,256]{1,0:T(8,128)S(1)} %collective-permute-done.refs_1_), channel_id=1, source_target_pairs={{0,1},{1,2},{2,3},{3,0},{4,5},{5,6},{6,7},{7,4},{8,9},{9,10},{10,1... | collective-permute-start | bytes 1032200 | tf_op jit(solution)/shard_map/ppermute | solution.py:277
  13.0 1.2 %copy-start = (f32[1024,256]{1,0:T(8,128)S(1)}, f32[1024,256]{1,0:T(8,128)}, u32[]{:S(2)}) copy-start(f32[1024,256]{1,0:T(8,128)} %refs_4_.1) | copy-start | bytes 3145732
  14.3 1.0 %copy-start.4 = (f32[343,343]{1,0:T(8,128)S(1)}, f32[343,343]{1,0:T(8,128)}, u32[]{:S(2)}) copy-start(f32[343,343]{1,0:T(8,128)} %refs_1_.1) | copy-start | bytes 1411792
  15.3 1.0 %copy-start.5 = (bf16[343,400]{1,0:T(8,128)(2,1)S(1)}, bf16[343,400]{1,0:T(8,128)(2,1)}, u32[]{:S(2)}) copy-start(bf16[343,400]{1,0:T(8,128)(2,1)} %constant.14.clone.refs_3_) | copy-start | bytes 823204
  16.3 1.0 %copy-start.6 = (bf16[400,343]{1,0:T(8,128)(2,1)S(1)}, bf16[400,343]{1,0:T(8,128)(2,1)}, u32[]{:S(2)}) copy-start(bf16[400,343]{1,0:T(8,128)(2,1)} %constant.4.clone.refs_2_) | copy-start | bytes 823204
  18.5 17.0 %collective-permute-start.3 = (f32[528,256]{1,0:T(8,128)S(1)}, f32[528,256]{1,0:T(8,128)S(1)}, u32[]{:S(2)}, u32[]{:S(2)}) collective-permute-start(f32[528,256]{1,0:T(8,128)S(1)} %get-tuple-element.55), channel_id=1, source_target_pairs={{0,1},{1,2},{2,3},{3,0},{4,5},{5,6},{6,7},{7,4},{8,9},{9,10},{10,1... | collective-permute-start | bytes 1622024 | tf_op jit(solution)/shard_map/ppermute | solution.py:277
  20.1 25.8 %collective-permute-start.5 = (f32[528,256]{1,0:T(8,128)S(1)}, f32[528,256]{1,0:T(8,128)S(1)}, u32[]{:S(2)}, u32[]{:S(2)}) collective-permute-start(f32[528,256]{1,0:T(8,128)S(1)} %collective-permute-done.4.refs_2_), channel_id=1, source_target_pairs={{0,3},{1,0},{2,1},{3,2},{4,7},{5,4},{6,5},{7,6},{8,11},{9,8},{10,9... | collective-permute-start | bytes 1622024 | tf_op jit(solution)/shard_map/ppermute | solution.py:277
  24.2 11.3 %copy-start.7 = (f32[6,6,24]{2,1,0:T(8,128)S(1)}, f32[6,6,24]{2,1,0:T(8,128)}, u32[]{:S(2)}) copy-start(f32[6,6,24]{2,1,0:T(8,128)} %param.11) | copy-start | bytes 10372
  27.2 10.4 %collective-permute-start.6 = (f32[288,128]{1,0:T(8,128)S(1)}, f32[288,128]{1,0:T(8,128)S(1)}, u32[]{:S(2)}, u32[]{:S(2)}) collective-permute-start(f32[288,128]{1,0:T(8,128)S(1)} %get-tuple-element.58), channel_id=1, source_target_pairs={{0,240},{16,0},{32,16},{48,32},{64,48},{80,64},{96,80},{112,96},{1... | collective-permute-start | bytes 442376 | tf_op jit(solution)/shard_map/ppermute | solution.py:277
  36.4 0.8 %copy-start.2 = (f32[528,256]{1,0:T(8,128)}, f32[528,256]{1,0:T(8,128)S(1)}, u32[]{:S(2)}) copy-start(f32[528,256]{1,0:T(8,128)S(1)} %get-tuple-element.57.refs_1_) | copy-start | bytes 1622020
  38.3 7.7 %collective-permute-start.7 = (f32[336,128]{1,0:T(8,128)}, f32[336,128]{1,0:T(8,128)S(1)}, u32[]{:S(2)}, u32[]{:S(2)}) collective-permute-start(f32[336,128]{1,0:T(8,128)} %get-tuple-element.60), channel_id=1, source_target_pairs={{0,12},{4,0},{8,4},{12,8},{1,13},{5,1},{9,5},{13,9},{2,14},{6,2},{... | collective-permute-start | bytes 516104 | tf_op jit(solution)/shard_map/ppermute | solution.py:277
  45.9 1.0 %copy-start.3 = (f32[528,256]{1,0:T(8,128)S(1)}, f32[528,256]{1,0:T(8,128)}, u32[]{:S(2)}) copy-start(f32[528,256]{1,0:T(8,128)} %copy-done.2) | copy-start | bytes 1622020
  49.3 2.4 %collective-permute-start.8 = (f32[336,128]{1,0:T(8,128)S(1)}, f32[336,128]{1,0:T(8,128)S(1)}, u32[]{:S(2)}, u32[]{:S(2)}) collective-permute-start(f32[336,128]{1,0:T(8,128)S(1)} %get-tuple-element.65), channel_id=1, source_target_pairs={{0,4},{4,8},{8,12},{12,0},{1,5},{5,9},{9,13},{13,1},{2,6},{6,10},{... | collective-permute-start | bytes 516104 | tf_op jit(solution)/shard_map/ppermute | solution.py:277
  49.4 5.8 %collective-permute-start.9 = (f32[336,128]{1,0:T(8,128)S(1)}, f32[336,128]{1,0:T(8,128)S(1)}, u32[]{:S(2)}, u32[]{:S(2)}) collective-permute-start(f32[336,128]{1,0:T(8,128)S(1)} %get-tuple-element.66), channel_id=1, source_target_pairs={{0,12},{4,0},{8,4},{12,8},{1,13},{5,1},{9,5},{13,9},{2,14},{6,2},{... | collective-permute-start | bytes 516104 | tf_op jit(solution)/shard_map/ppermute | solution.py:277
  55.2 10.1 %collective-permute-start.10 = (f32[336,128]{1,0:T(8,128)S(1)}, f32[336,128]{1,0:T(8,128)S(1)}, u32[]{:S(2)}, u32[]{:S(2)}) collective-permute-start(f32[336,128]{1,0:T(8,128)S(1)} %get-tuple-element.71.refs_4_), channel_id=1, source_target_pairs={{0,16},{16,32},{32,48},{48,64},{64,80},{80,96},{96,112},{112,128},... | collective-permute-start | bytes 516104 | tf_op jit(solution)/shard_map/ppermute | solution.py:277
  55.3 10.0 %collective-permute-start.11 = (f32[336,128]{1,0:T(8,128)S(1)}, f32[336,128]{1,0:T(8,128)S(1)}, u32[]{:S(2)}, u32[]{:S(2)}) collective-permute-start(f32[336,128]{1,0:T(8,128)S(1)} %get-tuple-element.70.refs_3_), channel_id=1, source_target_pairs={{0,240},{16,0},{32,16},{48,32},{64,48},{80,64},{96,80},{112,96},{1... | collective-permute-start | bytes 516104 | tf_op jit(solution)/shard_map/ppermute | solution.py:277
  67.5 10.3 %collective-permute-start.12 = (f32[288,128]{1,0:T(8,128)S(1)}, f32[288,128]{1,0:T(8,128)S(1)}, u32[]{:S(2)}, u32[]{:S(2)}) collective-permute-start(f32[288,128]{1,0:T(8,128)S(1)} %get-tuple-element.76), channel_id=1, source_target_pairs={{0,16},{16,32},{32,48},{48,64},{64,80},{80,96},{96,112},{112,128},... | collective-permute-start | bytes 442376 | tf_op jit(solution)/shard_map/ppermute | solution.py:277
  67.6 10.3 %collective-permute-start.13 = (f32[288,128]{1,0:T(8,128)S(1)}, f32[288,128]{1,0:T(8,128)S(1)}, u32[]{:S(2)}, u32[]{:S(2)}) collective-permute-start(f32[288,128]{1,0:T(8,128)S(1)} %get-tuple-element.77), channel_id=1, source_target_pairs={{0,4},{4,8},{8,12},{12,0},{1,5},{5,9},{9,13},{13,1},{2,6},{6,10},{... | collective-permute-start | bytes 442376 | tf_op jit(solution)/shard_map/ppermute | solution.py:277
  67.9 10.0 %collective-permute-start.14 = (f32[48,128]{1,0:T(8,128)S(1)}, f32[48,128]{1,0:T(8,128)S(1)}, u32[]{:S(2)}, u32[]{:S(2)}) collective-permute-start(f32[48,128]{1,0:T(8,128)S(1)} %get-tuple-element.78), channel_id=1, source_target_pairs={{0,20},{4,24},{8,28},{12,16},{16,36},{20,40},{24,44},{28,32},{32,5... | collective-permute-start | bytes 73736 | tf_op jit(solution)/shard_map/ppermute | solution.py:287

commit v3 on v2

v3 whole, which is shorter than its diff:
```python
import functools

import jax
import jax.numpy as jnp
import numpy as np
from jax import lax
from jax.experimental import pallas as pl
from jax.experimental.pallas import tpu as pltpu
from jax.sharding import PartitionSpec as P

ORDER = 6
SIDE = ORDER + 1
NZ = 24
LANES = 128
PARTS = 2
ROWS = 56
CELL_ROWS = SIDE * ROWS
KPAD = 400
LAYER = NZ * ROWS
XROWS = 3 * ORDER * ROWS + KPAD
YROWS = LAYER + ROWS
F32 = jnp.float32
BF16 = jnp.bfloat16
LIMIT = 16 * 1024 * 1024
WHOLE = 60 * 1024 * 1024

LINES1 = [(0, y) for y in range(6)] + [(x, 0) for x in range(1, 6)] + [(x, 1) for x in range(1, 4)]
LINES2 = [(x, 1) for x in (4, 5)] + [(x, y) for x in range(1, 6) for y in range(2, 6)]
OWNED = 36 * NZ
SET1 = len(LINES1) * NZ
SET2 = len(LINES2) * NZ
EDGE = 6 * NZ
PLANE = 7 * NZ
PLACES = {(x, y): x * 6 + y for x in range(6) for y in range(6)}
PLACES.update({(6, y): 36 + y for y in range(7)})
PLACES.update({(x, 6): 43 + x for x in range(6)})
CORNERS = ((0, 0), (6, 0), (0, 6), (6, 6))
CROWS = 8
CPAD = 64
CLAYER = NZ * CROWS
CXROWS = 3 * ORDER * CROWS + CPAD


def selection(places, rows, padded):
    chosen = np.zeros((padded, SIDE**3), np.float32)
    for (p, q), row in places:
        for r in range(SIDE):
            chosen[r * rows + row, (p * SIDE + q) * SIDE + r] = 1.0
    return chosen


def split(values):
    high = values.astype(BF16)
    return high, (values - high.astype(F32)).astype(BF16)


def dot(a, b):
    return jnp.dot(a, b, preferred_element_type=F32)


def line(index):
    return pl.ds(index * NZ, NZ)


def carry_out(copies):
    for copy in copies:
        copy.start()
    for copy in copies:
        copy.wait()


def lane_blocks(w, held, sems):
    return [
        pltpu.make_async_copy(
            w.at[:, pl.ds(part * LANES, LANES)], held.at[pl.ds(part * OWNED, OWNED)], sems.at[part]
        )
        for part in range(PARTS)
    ]


def pulls_kernel(w, pull_x, pull_y, pull_c, sems):
    copies = []

    def add(first, rows, out, start, part):
        copies.append(
            pltpu.make_async_copy(
                w.at[pl.ds(first, rows), pl.ds(part * LANES, LANES)],
                out.at[pl.ds(start, rows)],
                sems.at[len(copies)],
            )
        )

    for part in range(PARTS):
        add(0, EDGE, pull_x, part * EDGE, part)
        add(0, NZ, pull_c, part * NZ, part)
        for x in range(6):
            add(x * EDGE, NZ, pull_y, part * EDGE + x * NZ, part)
    carry_out(copies)


def cell_kernel(
    cell, chosen, chosen_t, corners_t, potential, center, halfwidth, k_high, k_low, c_high, c_low, local,
    cell_ref, chosen_ref, chosen_t_ref, corners_t_ref, sems,
):
    pairs = ((cell, cell_ref), (chosen, chosen_ref), (chosen_t, chosen_t_ref), (corners_t, corners_t_ref))
    copies = [pltpu.make_async_copy(source, target, sems.at[index]) for index, (source, target) in enumerate(pairs)]
    for copy in copies:
        copy.start()
    scale = 1.0 / jnp.full((1, LANES), halfwidth[0], F32)
    local[...] = jnp.zeros_like(local)
    for x in range(6):
        shifted = potential[x] - center[0]
        for z in range(NZ):
            local[pl.ds(z * ROWS + x * 6, 6)] = shifted[:, z : z + 1] * scale
    for copy in copies:
        copy.wait()
    for half, k_ref, c_ref in zip(split(cell_ref[...] * scale[:, 0:1]), (k_high, k_low), (c_high, c_low)):
        rows = dot(chosen_ref[...], half).astype(BF16)
        k_ref[...] = dot(rows, chosen_t_ref[...]).astype(BF16)
        c_ref[...] = dot(rows, corners_t_ref[...]).astype(BF16)


def rotation_kernel(me, rotation, r_high, r_low, far_high, far_low):
    for index, steps in enumerate((0, -1, 1, 2)):
        owner = lax.rem(me[0] + steps + 4, 4)
        high, low = split(rotation[pl.ds(pl.multiple_of(owner * 256, 256), 256)])
        if index < 3:
            r_high[pl.ds(index * 256, 256)] = high
            r_low[pl.ds(index * 256, 256)] = low
        else:
            far_high[...] = high
            far_low[...] = low


def turned(values, r_high, r_low):
    high, low = split(values)
    rh = r_high[...]
    return dot(high, rh) + (dot(low, rh) + dot(high, r_low[...]))


def side_by_side(stacked):
    rows = stacked.shape[0] // PARTS
    return [stacked[pl.ds(part * rows, rows)] for part in range(PARTS)]


def near_kernel(own, left, right, r_high, r_low, total):
    pieces = side_by_side(own) + side_by_side(left) + side_by_side(right)
    total[...] = turned(jnp.concatenate(pieces, 1), r_high, r_low)


def line_runs(lines):
    runs = []
    for index, (x, y) in enumerate(lines):
        there = x * 6 + y
        if runs and runs[-1][0] + runs[-1][2] == there:
            runs[-1][2] += 1
        else:
            runs.append([there, index, 1])
    return runs


def write_lines(lines, held, out, sems):
    carry_out(
        [
            pltpu.make_async_copy(
                held.at[pl.ds(here * NZ, count * NZ)], out.at[pl.ds(there * NZ, count * NZ)], sems.at[index]
            )
            for index, (there, here, count) in enumerate(line_runs(lines))
        ]
    )


def relay_kernel(left, right, left_part, right_part):
    rows = left_part.shape[0]
    left_part[...] = left[0:rows]
    right_part[...] = right[rows:]


def far_kernel(lines, total, far_a, far_b, far_high, far_low, *refs):
    out, held, sems = refs[-3:]
    held[...] = total[...] + turned(jnp.concatenate([far_a[...], far_b[...]], 1), far_high, far_low)
    write_lines(lines, held, out, sems)


def fence_kernel(*refs):
    pass


def cells_product(parts, x_ref, y_ref, xh_ref, xl_ref, k_high, k_low):
    kh = k_high[...]
    kl = k_low[...]
    step = ORDER * ROWS
    for part in range(parts):
        high, low = split(x_ref[part])
        xh_ref[...] = high
        xl_ref[...] = low
        y_ref[part] = jnp.zeros((YROWS, LANES), F32)
        for pair in range(2):
            first, second = 2 * pair * step, (2 * pair + 1) * step
            xh = jnp.concatenate([xh_ref[first : first + KPAD], xh_ref[second : second + KPAD]], 1)
            xl = jnp.concatenate([xl_ref[first : first + KPAD], xl_ref[second : second + KPAD]], 1)
            product = dot(kh, xh) + (dot(kh, xl) + dot(kl, xh))
            y_ref[part, first : first + CELL_ROWS] += product[:CELL_ROWS, :LANES]
            y_ref[part, second : second + CELL_ROWS] += product[:CELL_ROWS, LANES:]
        y_ref[part, 0:ROWS] += y_ref[part, LAYER:YROWS]


def every(start, count):
    return pl.ds(start, count, stride=NZ)


def first_kernel(
    w, gx, gy, gc, k_high, k_low, local, p_out, f0, f6, s0, s6, held, x_ref, y_ref, xh_ref, xl_ref, sems
):
    carry_out(lane_blocks(w, held, sems))
    for part in range(PARTS):
        xs = x_ref.at[part]
        xs[LAYER:] = jnp.zeros((XROWS - LAYER, LANES), F32)
        for z in range(NZ):
            at = z * ROWS
            xs[at : at + 36] = held[every(part * OWNED + z, 36)]
            xs[at + 36 : at + 42] = gx[every(part * EDGE + z, 6)]
            xs[at + 42 : at + 43] = gc[part * NZ + z : part * NZ + z + 1]
            xs[at + 43 : at + 49] = gy[every(part * EDGE + z, 6)]
            xs[at + 49 : at + 56] = jnp.zeros((7, LANES), F32)
        xs[LAYER:YROWS] = xs[0:ROWS]
    cells_product(PARTS, x_ref, y_ref, xh_ref, xl_ref, k_high, k_low)
    for part in range(PARTS):
        ps = p_out.at[part]
        ps[...] = y_ref[part, 0:LAYER] + local[...] * x_ref[part, 0:LAYER]
        base = part * PLANE
        for z in range(NZ):
            at = z * ROWS
            s6[every(base + z, 7)] = ps[at + 36 : at + 43]
            s0[every(base + z, 6)] = ps[at : at + 6]
            s0[base + EDGE + z : base + EDGE + z + 1] = ps[at + 43 : at + 44]
            f0[base + z : base + z + 1] = ps[at : at + 1]
            f0[every(base + NZ + z, 5)] = ps[pl.ds(at + 6, 5, stride=6)]
            f0[base + EDGE + z : base + EDGE + z + 1] = ps[at + 36 : at + 37]
            f6[every(base + z, 6)] = ps[at + 43 : at + 49]
            f6[base + EDGE + z : base + EDGE + z + 1] = ps[at + 42 : at + 43]


def cross_kernel(q0, q6, d0, d6):
    for part in range(PARTS):
        base, there = part * PLANE, part * 2 * NZ
        for index, q in enumerate((q0, q6)):
            d0[pl.ds(there + index * NZ, NZ)] = q[pl.ds(base, NZ)]
            d6[pl.ds(there + index * NZ, NZ)] = q[pl.ds(base + EDGE, NZ)]


def second_kernel(p_in, r0, r6, q0, q6, k_high, k_low, local, layers, x_ref, y_ref, xh_ref, xl_ref):
    for part in range(PARTS):
        xs = x_ref.at[part]
        xs[0:LAYER] = p_in[part]
        xs[LAYER:] = jnp.zeros((XROWS - LAYER, LANES), F32)
        base = part * PLANE
        for z in range(NZ):
            at = z * ROWS
            xs[at : at + 6] += q0[every(base + z, 6)]
            xs[at + 36 : at + 43] += q6[every(base + z, 7)]
            xs[at + 43 : at + 44] += q0[base + EDGE + z : base + EDGE + z + 1]
            xs[at : at + 1] += r0[base + z : base + z + 1]
            xs[pl.ds(at + 6, 5, stride=6)] += r0[every(base + NZ + z, 5)]
            xs[at + 36 : at + 37] += r0[base + EDGE + z : base + EDGE + z + 1]
            xs[at + 43 : at + 49] += r6[every(base + z, 6)]
            xs[at + 42 : at + 43] += r6[base + EDGE + z : base + EDGE + z + 1]
        xs[LAYER:YROWS] = xs[0:ROWS]
    cells_product(PARTS, x_ref, y_ref, xh_ref, xl_ref, k_high, k_low)
    for part in range(PARTS):
        layers[part] = 2.0 * (y_ref[part, 0:LAYER] + local[...] * x_ref[part, 0:LAYER])


def third_kernel(
    layers, d0, d6, w, c_high, c_low, local, set1, set2, push_x, push_y, push_c,
    held, c_ref, ch_ref, cl_ref, y_ref, sems,
):
    copies = lane_blocks(w, held, sems)
    for copy in copies:
        copy.start()
    ch, cl = c_high[...], c_low[...]
    step = ORDER * CROWS
    for part in range(PARTS):
        c_ref[...] = jnp.zeros_like(c_ref)
        base = part * 2 * NZ
        for z in range(NZ):
            at = z * CROWS
            c_ref[at : at + 2] = d0[every(base + z, 2)]
            c_ref[at + 2 : at + 4] = d6[every(base + z, 2)]
        c_ref[CLAYER : CLAYER + CROWS] = c_ref[0:CROWS]
        ch_ref[...], cl_ref[...] = split(2.0 * c_ref[...])
        ys = y_ref.at[part]
        ys[0:LAYER] = layers[part]
        ys[LAYER:YROWS] = jnp.zeros((ROWS, LANES), F32)
        for pair in range(2):
            first, second = 2 * pair, 2 * pair + 1
            high = jnp.concatenate([ch_ref[cell * step : cell * step + CPAD] for cell in (first, second)], 1)
            low = jnp.concatenate([cl_ref[cell * step : cell * step + CPAD] for cell in (first, second)], 1)
            product = dot(ch, high) + (dot(ch, low) + dot(cl, high))
            for index, cell in enumerate((first, second)):
                start = cell * ORDER * ROWS
                ys[start : start + CELL_ROWS] += product[:CELL_ROWS, index * LANES : (index + 1) * LANES]
        ys[0:ROWS] += ys[LAYER:YROWS]
        base1, base2 = part * SET1, part * SET2
        for z in range(NZ):
            at = z * ROWS
            ys[at : at + 1] += 2.0 * (local[at : at + 1] * c_ref[z * CROWS : z * CROWS + 1])
            set1[every(base1 + z, 6)] = ys[at : at + 6]
            set1[every(base1 + EDGE + z, 5)] = ys[pl.ds(at + 6, 5, stride=6)]
            set1[every(base1 + 11 * NZ + z, 3)] = ys[pl.ds(at + 7, 3, stride=6)]
            set2[every(base2 + z, 2)] = ys[pl.ds(at + 25, 2, stride=6)]
            for x in range(1, 6):
                set2[every(base2 + (4 * x - 2) * NZ + z, 4)] = ys[at + 6 * x + 2 : at + 6 * x + 6]
            push_x[every(part * EDGE + z, 6)] = ys[at + 36 : at + 42]
            push_c[part * NZ + z : part * NZ + z + 1] = ys[at + 42 : at + 43]
            push_y[every(part * EDGE + z, 6)] = ys[at + 43 : at + 49]
    for copy in copies:
        copy.wait()
    for part in range(PARTS):
        for lines, out in ((LINES1, set1), (LINES2, set2)):
            for index, (x, y) in enumerate(lines):
                out[line(part * len(lines) + index)] -= held[line(part * 36 + x * 6 + y)]


def finish_kernel(set1, rx, ry, rc, out):
    out[...] = set1[...]
    for part in range(PARTS):
        base, edge = part * SET1, part * EDGE
        out[pl.ds(base, EDGE)] += rx[pl.ds(edge, EDGE)]
        out[pl.ds(base, NZ)] += ry[pl.ds(edge, NZ)] + rc[pl.ds(part * NZ, NZ)]
        out[pl.ds(base + EDGE, 5 * NZ)] += ry[pl.ds(edge + NZ, 5 * NZ)]


VM = pl.BlockSpec(memory_space=pltpu.VMEM)
HB = pl.BlockSpec(memory_space=pltpu.HBM)
ANYWHERE = pl.BlockSpec(memory_space=pl.ANY)
SM = pl.BlockSpec(memory_space=pltpu.SMEM)


def call(kernel, name, in_specs, shapes, scratch=(), out=None, aliases=(), flops=10**11, limit=LIMIT, ordered=True):
    inputs, outputs = len(in_specs), len(shapes)
    tokens = 1 if ordered else 0

    def body(*refs):
        kernel(*refs[:inputs], *refs[inputs + tokens : inputs + tokens + outputs], *refs[inputs + outputs + 2 * tokens :])

    if out is None:
        results = [pltpu.VMEM(*shape) for shape in shapes]
    else:
        results = [jax.ShapeDtypeStruct(*shape) for shape in shapes]
    return pl.pallas_call(
        body,
        name=name,
        in_specs=in_specs + [ANYWHERE] * tokens,
        out_specs=[out or VM] * outputs + [ANYWHERE] * tokens,
        out_shape=results + [jax.ShapeDtypeStruct((8, LANES), F32)] * tokens,
        scratch_shapes=list(scratch),
        compiler_params=pltpu.CompilerParams(vmem_limit_bytes=limit),
        cost_estimate=pl.CostEstimate(flops=flops, bytes_accessed=1, transcendentals=0),
        input_output_aliases={**({inputs: outputs} if ordered else {}), **dict(aliases)},
    )


class Sequence:
    def __init__(self):
        self.token = jnp.zeros((8, LANES), F32)

    def __call__(self, kernel, *operands):
        *results, self.token = kernel(*operands, self.token)
        return results


def rows_of(count):
    return ((count, LANES), F32)


def passed_along(value, axis, steps):
    count = lax.axis_size(axis)
    return lax.ppermute(value, axis, [(s, (s + steps) % count) for s in range(count)])


def passed_diagonal(value, steps):
    slabs, faces = lax.axis_size("slab"), lax.axis_size("face")
    pairs = [
        (a * faces + b, ((a + steps) % slabs) * faces + (b + steps) % faces)
        for a in range(slabs)
        for b in range(faces)
    ]
    return lax.ppermute(value, ("slab", "face"), pairs)


def shards(wavefunctions, rotation, cell_matrix, potential, center, halfwidth):
    run = Sequence()
    places = PLACES.items()
    chosen = selection(places, ROWS, KPAD)
    corners_t = selection([(place, row) for row, place in enumerate(CORNERS)], CROWS, CPAD).T
    me = lax.axis_index("band").astype(jnp.int32).reshape(1)
    held = [pltpu.VMEM((PARTS * OWNED, LANES), F32)]
    operator_scratch = [
        pltpu.VMEM((PARTS, XROWS, LANES), F32),
        pltpu.VMEM((PARTS, YROWS, LANES), F32),
        pltpu.VMEM((XROWS, LANES), BF16),
        pltpu.VMEM((XROWS, LANES), BF16),
    ]
    two_copies = [pltpu.SemaphoreType.DMA((PARTS,))]
    edge, plane, corners = rows_of(PARTS * EDGE), rows_of(PARTS * PLANE), rows_of(PARTS * NZ)
    both = rows_of(PARTS * 2 * NZ)
    set1, set2 = rows_of(PARTS * SET1), rows_of(PARTS * SET2)
    wide1, wide2 = ((SET1, 256), F32), ((SET2, 256), F32)
    layer_shape = ((PARTS, LAYER, LANES), F32)
    field = wavefunctions.reshape(OWNED, 256)

    def left(value):
        return passed_along(value, "band", 1)

    def right(value):
        return passed_along(value, "band", -1)

    def fenced(name, *values):
        shapes = [(value.shape, value.dtype) for value in values]
        count = len(values)
        aliases = [(index, index) for index in range(count)]
        return run(call(fence_kernel, name, [ANYWHERE] * count, shapes, out=ANYWHERE, aliases=aliases), *values)

    pull_x, pull_y, pull_c = call(
        pulls_kernel,
        "pulls",
        [HB],
        [edge, edge, corners],
        [pltpu.SemaphoreType.DMA((8 * PARTS,))],
        limit=WHOLE,
        ordered=False,
    )(field)
    gy = passed_along(pull_y, "face", -1)
    gx = passed_along(pull_x, "slab", -1)
    (pull_c,) = fenced("fence_c", pull_c)
    gc = passed_diagonal(pull_c, -1)
    k_high, k_low, c_high, c_low, local = run(
        call(
            cell_kernel,
            "cell",
            [HB] * 4 + [VM] + [SM] * 2,
            [((KPAD, KPAD), BF16)] * 2 + [((KPAD, CPAD), BF16)] * 2 + [((LAYER, LANES), F32)],
            [
                pltpu.VMEM((SIDE**3, SIDE**3), F32),
                pltpu.VMEM((KPAD, SIDE**3), BF16),
                pltpu.VMEM((SIDE**3, KPAD), BF16),
                pltpu.VMEM((SIDE**3, CPAD), BF16),
                pltpu.SemaphoreType.DMA((4,)),
            ],
            flops=1,
        ),
        cell_matrix,
        jnp.asarray(chosen, BF16),
        jnp.asarray(chosen.T, BF16),
        jnp.asarray(corners_t, BF16),
        potential,
        center,
        halfwidth,
    )
    p, f0, f6, s0, s6 = run(
        call(
            first_kernel,
            "first",
            [HB] + [VM] * 6,
            [layer_shape] + [plane] * 4,
            held + operator_scratch + two_copies,
        ),
        field, gx, gy, gc, k_high, k_low, local,
    )
    r0 = passed_along(f6, "face", 1)
    r6 = passed_along(f0, "face", -1)
    q0 = passed_along(s6, "slab", 1)
    q6 = passed_along(s0, "slab", -1)
    r_high, r_low, far_high, far_low = run(
        call(
            rotation_kernel, "rotation", [SM, VM], [((768, 256), BF16)] * 2 + [((256, 256), BF16)] * 2
        ),
        me, rotation,
    )
    e0, e6 = run(call(cross_kernel, "cross", [VM] * 2, [both] * 2), q0, q6)
    d0 = passed_along(e6, "face", 1)
    d6 = passed_along(e0, "face", -1)
    (layers,) = run(
        call(second_kernel, "second", [VM] * 8, [layer_shape], operator_scratch), p, r0, r6, q0, q6, k_high, k_low, local
    )
    v1, v2, push_x, push_y, push_c = run(
        call(
            third_kernel,
            "third",
            [VM] * 3 + [HB] + [VM] * 3,
            [set1, set2, edge, edge, corners],
            held
            + [
                pltpu.VMEM((CXROWS, LANES), F32),
                pltpu.VMEM((CXROWS, LANES), BF16),
                pltpu.VMEM((CXROWS, LANES), BF16),
                pltpu.VMEM((PARTS, YROWS, LANES), F32),
            ]
            + two_copies,
        ),
        layers, d0, d6, field, c_high, c_low, local,
    )
    l2, r2 = left(v2), right(v2)
    push_x, push_y, push_c = fenced("fence_p", push_x, push_y, push_c)
    ry = passed_along(push_y, "face", 1)
    rx = passed_along(push_x, "slab", 1)
    rc = passed_diagonal(push_c, 1)
    (v1,) = run(call(finish_kernel, "finish", [VM] * 4, [set1], flops=1), v1, rx, ry, rc)
    l1, r1 = left(v1), right(v1)


    def relayed(name, from_left, from_right):
        rows = from_left.shape[0] // PARTS
        parts = run(call(relay_kernel, name, [VM] * 2, [rows_of(rows)] * 2), from_left, from_right)
        return left(parts[0]), right(parts[1])

    far2 = relayed("relay2", l2, r2)
    (total2,) = run(call(near_kernel, "near2", [VM] * 5, [wide2]), v2, l2, r2, r_high, r_low)
    far1 = relayed("relay1", l1, r1)
    (total1,) = run(call(near_kernel, "near1", [VM] * 5, [wide1]), v1, l1, r1, r_high, r_low)
    result_shape = [((OWNED, 256), F32)]

    def far_scratch(lines):
        return [pltpu.VMEM((len(lines) * NZ, 256), F32), pltpu.SemaphoreType.DMA((len(line_runs(lines)),))]

    (result,) = run(
        call(functools.partial(far_kernel, LINES2), "far2", [VM] * 5, result_shape, far_scratch(LINES2), out=HB),
        total2, *far2, far_high, far_low,
    )
    (result,) = run(
        call(
            functools.partial(far_kernel, LINES1),
            "last",
            [VM] * 5 + [HB],
            result_shape,
            far_scratch(LINES1),
            out=HB,
            aliases=((5, 0),),
        ),
        total1, *far1, far_high, far_low, result,
    )
    return result.reshape(6, 6, NZ, 256)


def solution(mesh):
    placed = (
        P("slab", "face", None, "band"),
        P(None, "band"),
        P(),
        P("slab", "face", None),
        P(),
        P(),
    )
    return jax.shard_map(
        shards,
        mesh=mesh,
        in_specs=placed,
        out_specs=P("slab", "face", None, "band"),
        check_vma=False,
    )
```

time: 79.3 us -> 75 us (0.946)
  the two profiles are of different devices: /device:TPU:1 before, /device:TPU:24 now
where the time goes in v3:
time: 75 us; the launch traced here: 74.7 us
  starting transfers between devices  30.4 us (41%)
  waiting for transfers between devices  21.3 us (28%)
  Pallas kernels  21.2 us (28%)
  between operations  1.73 us (2%)
    ppermute x18, starting transfers between devices, passed_along(): lax.ppermute(value, axis, [(s, (s + steps) % count) for s in range(count)])  29.5 us
    pallas_call x15, Pallas kernels, __call__(): *results, self.token = kernel(*operands, self.token)  20 us
    ppermute x18, waiting for transfers between devices, passed_along(): lax.ppermute(value, axis, [(s, (s + steps) % count) for s in range(count)])  13.6 us
    ppermute x2, waiting for transfers between devices, passed_diagonal(): return lax.ppermute(value, ('slab', 'face'), pairs)  7.71 us
  transfers between devices with their start and end apart: 20, of which 5 were waited for; matrix products, arithmetic and copies ran while one was open for 0% of the time, Pallas kernels for 18%

profile of v3, /device:TPU:24, one launch (start us, length us, event | category | flops | bytes accessed | tf_op | source)
XLA Modules:
  0.0 74.7 jit_solution(2777214134010590755)
XLA Ops:
  0.0 1.2 %pulls.1 = (f32[288,128]{1,0:T(8,128)S(1)}, f32[288,128]{1,0:T(8,128)S(1)}, f32[48,128]{1,0:T(8,128)S(1)}) custom-call(f32[864,256]{1,0:T(8,128)} %bitcast.3), custom_call_target="tpu_custom_call" | custom-call | flops 99999997952 | bytes 1 | tf_op jit(solution)/shard_map/pulls/pallas_call | solution.py:425
  1.2 8.4 %collective-permute-start = (f32[288,128]{1,0:T(8,128)S(1)}, f32[288,128]{1,0:T(8,128)S(1)}, u32[]{:S(2)}, u32[]{:S(2)}) collective-permute-start(f32[288,128]{1,0:T(8,128)S(1)} %get-tuple-element.57), channel_id=1, source_target_pairs={{0,240},{16,0},{32,16},{48,32},{64,48},{80,64},{96,80},{112,96},{1... | collective-permute-start | bytes 442376 | tf_op jit(solution)/shard_map/ppermute | solution.py:379
  9.6 0.0 collective-permute-start.1
  9.6 0.0 copy-start.2
  9.6 0.0 copy-start.3
  9.6 0.0 copy-start.4
  9.6 0.0 copy-start.6
  9.7 0.9 %collective-permute-start.2 = (f32[48,128]{1,0:T(8,128)S(1)}, f32[48,128]{1,0:T(8,128)S(1)}, u32[]{:S(2)}, u32[]{:S(2)}) collective-permute-start(f32[48,128]{1,0:T(8,128)S(1)} %get-tuple-element.60), channel_id=1, source_target_pairs={{0,252},{4,240},{8,244},{12,248},{16,12},{20,0},{24,4},{28,8},{32,... | collective-permute-start | bytes 73736 | tf_op jit(solution)/shard_map/ppermute | solution.py:389
  11.9 2.1 %cell.1 = (bf16[400,400]{1,0:T(8,128)(2,1)S(1)}, bf16[400,400]{1,0:T(8,128)(2,1)S(1)}, bf16[400,64]{1,0:T(8,128)(2,1)S(1)}, bf16[400,64]{1,0:T(8,128)(2,1)S(1)},...) custom-call(f32[343,343]{1,0:T(8,128)S(1)} %copy-done, ...), custom_call_target="tpu_custom_call", output_to_operand_aliasing={{5}: (7, {})} | custom-call | flops 1 | bytes 1 | tf_op jit(solution)/shard_map/cell/pallas_call | solution.py:369
  14.1 0.0 collective-permute-done.2.refs_3_
  14.1 0.0 collective-permute-done.refs_1_
  14.1 0.0 collective-permute-done.1.refs_2_
  14.1 0.0 copy-start.5
  14.1 2.8 %first.1 = (f32[2,1344,128]{2,1,0:T(8,128)S(1)}, f32[336,128]{1,0:T(8,128)}, f32[336,128]{1,0:T(8,128)}, f32[336,128]{1,0:T(8,128)S(1)}, f32[336,128]{1,0:T(8,128)S(1)}, /*index=5*/f32[8,128]{1,0:T(8,128)S(1)}) custom-call(f32[864,256]{1,0:T(8,128)S(1)} %bitcast.4, f32[288,128]{1,0:T(8,128)S(1)} %collective-permute-done.refs_1_, ...), custom_call_target="tpu_custom_call", output_to_operand_aliasing={{5}: (7, {})} | custom-call | flops 99999997952 | bytes 1 | tf_op jit(solution)/shard_map/first/pallas_call | solution.py:369
  17.0 0.7 collective-permute-start.3
  17.7 1.1 %collective-permute-start.4 = (f32[336,128]{1,0:T(8,128)}, f32[336,128]{1,0:T(8,128)}, u32[]{:S(2)}, u32[]{:S(2)}) collective-permute-start(f32[336,128]{1,0:T(8,128)} %get-tuple-element.68), channel_id=1, source_target_pairs={{0,12},{4,0},{8,4},{12,8},{1,13},{5,1},{9,5},{13,9},{2,14},{6,2},{... | collective-permute-start | bytes 516104 | tf_op jit(solution)/shard_map/ppermute | solution.py:379
  18.8 1.3 %collective-permute-start.5 = (f32[336,128]{1,0:T(8,128)S(1)}, f32[336,128]{1,0:T(8,128)S(1)}, u32[]{:S(2)}, u32[]{:S(2)}) collective-permute-start(f32[336,128]{1,0:T(8,128)S(1)} %get-tuple-element.69), channel_id=1, source_target_pairs={{0,16},{16,32},{32,48},{48,64},{64,80},{80,96},{96,112},{112,128},... | collective-permute-start | bytes 516104 | tf_op jit(solution)/shard_map/ppermute | solution.py:379
  20.1 4.3 %collective-permute-start.6 = (f32[336,128]{1,0:T(8,128)S(1)}, f32[336,128]{1,0:T(8,128)S(1)}, u32[]{:S(2)}, u32[]{:S(2)}) collective-permute-start(f32[336,128]{1,0:T(8,128)S(1)} %get-tuple-element.70), channel_id=1, source_target_pairs={{0,240},{16,0},{32,16},{48,32},{64,48},{80,64},{96,80},{112,96},{1... | collective-permute-start | bytes 516104 | tf_op jit(solution)/shard_map/ppermute | solution.py:379
  24.5 0.2 rotation.1
  24.6 3.5 %collective-permute-done.5.refs_0_.refs_3_ = f32[336,128]{1,0:T(8,128)S(1)} collective-permute-done((f32[336,128]{1,0:T(8,128)S(1)}, f32[336,128]{1,0:T(8,128)S(1)}, u32[]{:S(2)}, u32[]{:S(2)}) %collective-permute-start.5) | collective-permute-done | bytes 172064 | tf_op jit(solution)/shard_map/ppermute | solution.py:379
  28.1 0.0 collective-permute-done.6.refs_1_.refs_4_
  28.1 0.1 collective-permute-start.7
  28.2 1.7 %collective-permute-start.8 = (f32[96,128]{1,0:T(8,128)S(1)}, f32[96,128]{1,0:T(8,128)S(1)}, u32[]{:S(2)}, u32[]{:S(2)}) collective-permute-start(f32[96,128]{1,0:T(8,128)S(1)} %get-tuple-element.76), channel_id=1, source_target_pairs={{0,12},{4,0},{8,4},{12,8},{1,13},{5,1},{9,5},{13,9},{2,14},{6,2},{... | collective-permute-start | bytes 147464 | tf_op jit(solution)/shard_map/ppermute | solution.py:379
  29.9 3.1 %second.1 = (f32[2,1344,128]{2,1,0:T(8,128)S(1)}, f32[8,128]{1,0:T(8,128)S(1)}) custom-call(f32[2,1344,128]{2,1,0:T(8,128)S(1)} %get-tuple-element.66.refs_0_, f32[336,128]{1,0:T(8,128)} %collective-permute-done.3.refs_1_, f32[336,128]{1,0:T(8,128)} %collective-permute-done.4.refs_2_, ...), custom_call_target="tpu_custom_call", output_to_operand_aliasing={{1}: (8, {})} | custom-call | flops 99999997952 | bytes 1 | tf_op jit(solution)/shard_map/second/pallas_call | solution.py:369
  33.0 0.0 collective-permute-done.8.refs_2_
  33.0 1.4 %third.1 = (f32[672,128]{1,0:T(8,128)S(1)}, f32[1056,128]{1,0:T(8,128)S(1)}, f32[288,128]{1,0:T(8,128)S(1)}, f32[288,128]{1,0:T(8,128)S(1)}, f32[48,128]{1,0:T(8,128)S(1)}, /*index=5*/f32[8,128]{1,0:T(8,128)S(1)}) custom-call(f32[2,1344,128]{2,1,0:T(8,128)S(1)} %get-tuple-element.74.refs_0_, ...), custom_call_target="tpu_custom_call", output_to_operand_aliasing={{5}: (7, {})} | custom-call | flops 99999997952 | bytes 1 | tf_op jit(solution)/shard_map/third/pallas_call | solution.py:369
  34.4 0.8 %collective-permute-start.15 = (f32[1056,128]{1,0:T(8,128)S(1)}, f32[1056,128]{1,0:T(8,128)S(1)}, u32[]{:S(2)}, u32[]{:S(2)}) collective-permute-start(f32[1056,128]{1,0:T(8,128)S(1)} %get-tuple-element.92.refs_0_), channel_id=1, source_target_pairs={{0,3},{1,0},{2,1},{3,2},{4,7},{5,4},{6,5},{7,6},{8,11},{9,8},{10,9... | collective-permute-start | bytes 1622024 | tf_op jit(solution)/shard_map/ppermute | solution.py:379
  35.2 2.5 %collective-permute-start.14 = (f32[1056,128]{1,0:T(8,128)S(1)}, f32[1056,128]{1,0:T(8,128)S(1)}, u32[]{:S(2)}, u32[]{:S(2)}) collective-permute-start(f32[1056,128]{1,0:T(8,128)S(1)} %get-tuple-element.92.refs_0_), channel_id=1, source_target_pairs={{0,1},{1,2},{2,3},{3,0},{4,5},{5,6},{6,7},{7,4},{8,9},{9,10},{10,1... | collective-permute-start | bytes 1622024 | tf_op jit(solution)/shard_map/ppermute | solution.py:379
  37.7 0.0 collective-permute-start.9
  37.7 0.0 collective-permute-start.10
  37.7 0.0 collective-permute-start.11
  37.7 7.7 %collective-permute-done.11.refs_3_ = f32[48,128]{1,0:T(8,128)S(1)} collective-permute-done((f32[48,128]{1,0:T(8,128)S(1)}, f32[48,128]{1,0:T(8,128)S(1)}, u32[]{:S(2)}, u32[]{:S(2)}) %collective-permute-start.11) | collective-permute-done | bytes 24608 | tf_op jit(solution)/shard_map/ppermute | solution.py:389
  45.4 1.7 %collective-permute-done.9.refs_1_ = f32[288,128]{1,0:T(8,128)S(1)} collective-permute-done((f32[288,128]{1,0:T(8,128)S(1)}, f32[288,128]{1,0:T(8,128)S(1)}, u32[]{:S(2)}, u32[]{:S(2)}) %collective-permute-start.9) | collective-permute-done | bytes 147488 | tf_op jit(solution)/shard_map/ppermute | solution.py:379
  47.2 0.8 %finish.1 = (f32[672,128]{1,0:T(8,128)}, f32[8,128]{1,0:T(8,128)S(1)}) custom-call(f32[672,128]{1,0:T(8,128)S(1)} %get-tuple-element.80.refs_0_, f32[288,128]{1,0:T(8,128)S(1)} %collective-permute-done.9.refs_1_, f32[288,128]{1,0:T(8,128)S(1)} %collective-permute-done.10.refs_2_, ...), custom_call_target="tpu_custom_call", output_to_operand_aliasing={{1}: (4, {})} | custom-call | flops 1 | bytes 1 | tf_op jit(solution)/shard_map/finish/pallas_call | solution.py:369
  48.0 3.2 %collective-permute-start.12 = (f32[672,128]{1,0:T(8,128)}, f32[672,128]{1,0:T(8,128)}, u32[]{:S(2)}, u32[]{:S(2)}) collective-permute-start(f32[672,128]{1,0:T(8,128)} %get-tuple-element.89.refs_0_), channel_id=1, source_target_pairs={{0,1},{1,2},{2,3},{3,0},{4,5},{5,6},{6,7},{7,4},{8,9},{9,10},{10,1... | collective-permute-start | bytes 1032200 | tf_op jit(solution)/shard_map/ppermute | solution.py:379
  51.2 0.0 collective-permute-done.15.refs_1_.refs_2_
  51.2 0.0 collective-permute-done.14.refs_0_.refs_1_
  51.2 0.9 %relay2.1 = (f32[528,128]{1,0:T(8,128)}, f32[528,128]{1,0:T(8,128)}, f32[8,128]{1,0:T(8,128)S(1)}) custom-call(f32[1056,128]{1,0:T(8,128)S(1)} %collective-permute-done.14.refs_0_.refs_1_, f32[1056,128]{1,0:T(8,128)S(1)} %collective-permute-done.15.refs_1_.refs_2_, f32[8,128]{1,0:T(8,128)S(1)} %get-tuple-element.93.refs_2_), custom_call_target="tpu_custom_call", output_to_operand_aliasing={{2}: (2, {})} | custom-call | flops 99999997952 | bytes 1 | tf_op jit(solution)/shard_map/relay2/pallas_call | solution.py:369
  52.1 1.4 %collective-permute-start.18 = (f32[528,128]{1,0:T(8,128)}, f32[528,128]{1,0:T(8,128)}, u32[]{:S(2)}, u32[]{:S(2)}) collective-permute-start(f32[528,128]{1,0:T(8,128)} %get-tuple-element.103), channel_id=1, source_target_pairs={{0,1},{1,2},{2,3},{3,0},{4,5},{5,6},{6,7},{7,4},{8,9},{9,10},{10,1... | collective-permute-start | bytes 811016 | tf_op jit(solution)/shard_map/ppermute | solution.py:379
  53.5 0.6 collective-permute-start.19
  54.1 0.8 %near2.1 = (f32[528,256]{1,0:T(8,128)S(1)}, f32[8,128]{1,0:T(8,128)S(1)}) custom-call(f32[1056,128]{1,0:T(8,128)S(1)} %get-tuple-element.92.refs_0_, f32[1056,128]{1,0:T(8,128)S(1)} %collective-permute-done.14.refs_0_.refs_1_, f32[1056,128]{1,0:T(8,128)S(1)} %collective-permute-done.15.refs_1_.refs_2_, ...), custom_call_target="tpu_custom_call", output_to_operand_aliasing={{1}: (5, {})} | custom-call | flops 99999997952 | bytes 1 | tf_op jit(solution)/shard_map/near2/pallas_call | solution.py:369
  54.9 5.5 %collective-permute-done.13.refs_1_.refs_2_ = f32[672,128]{1,0:T(8,128)} collective-permute-done((f32[672,128]{1,0:T(8,128)}, f32[672,128]{1,0:T(8,128)}, u32[]{:S(2)}, u32[]{:S(2)}) %collective-permute-start.13) | collective-permute-done | bytes 344096 | tf_op jit(solution)/shard_map/ppermute | solution.py:379
  60.4 1.8 %relay1.1 = (f32[336,128]{1,0:T(8,128)}, f32[336,128]{1,0:T(8,128)}, f32[8,128]{1,0:T(8,128)S(1)}) custom-call(f32[672,128]{1,0:T(8,128)} %collective-permute-done.12.refs_0_.refs_1_, f32[672,128]{1,0:T(8,128)} %collective-permute-done.13.refs_1_.refs_2_, f32[8,128]{1,0:T(8,128)S(1)} %get-tuple-element.95.refs_2_), custom_call_target="tpu_custom_call", output_to_operand_aliasing={{2}: (2, {})} | custom-call | flops 99999997952 | bytes 1 | tf_op jit(solution)/shard_map/relay1/pallas_call | solution.py:369
  62.2 3.3 %collective-permute-start.16 = (f32[336,128]{1,0:T(8,128)}, f32[336,128]{1,0:T(8,128)}, u32[]{:S(2)}, u32[]{:S(2)}) collective-permute-start(f32[336,128]{1,0:T(8,128)} %get-tuple-element.98), channel_id=1, source_target_pairs={{0,1},{1,2},{2,3},{3,0},{4,5},{5,6},{6,7},{7,4},{8,9},{9,10},{10,1... | collective-permute-start | bytes 516104 | tf_op jit(solution)/shard_map/ppermute | solution.py:379
  65.5 1.8 %near1.1 = (f32[336,256]{1,0:T(8,128)S(1)}, f32[8,128]{1,0:T(8,128)S(1)}) custom-call(f32[672,128]{1,0:T(8,128)} %get-tuple-element.89.refs_0_, f32[672,128]{1,0:T(8,128)} %collective-permute-done.12.refs_0_.refs_1_, f32[672,128]{1,0:T(8,128)} %collective-permute-done.13.refs_1_.refs_2_, ...), custom_call_target="tpu_custom_call", output_to_operand_aliasing={{1}: (5, {})} | custom-call | flops 99999997952 | bytes 1 | tf_op jit(solution)/shard_map/near1/pallas_call | solution.py:369
  67.3 2.3 %far2.1 = (f32[864,256]{1,0:T(8,128)}, f32[8,128]{1,0:T(8,128)S(1)}) custom-call(f32[528,256]{1,0:T(8,128)S(1)} %get-tuple-element.102.refs_0_, f32[528,128]{1,0:T(8,128)} %collective-permute-done.18.refs_1_, f32[528,128]{1,0:T(8,128)} %collective-permute-done.19.refs_2_, ...), custom_call_target="tpu_custom_call", output_to_operand_aliasing={{1}: (5, {})} | custom-call | flops 99999997952 | bytes 1 | tf_op jit(solution)/shard_map/far2/pallas_call | solution.py:369
  69.6 2.8 %collective-permute-done.17.refs_2_ = f32[336,128]{1,0:T(8,128)} collective-permute-done((f32[336,128]{1,0:T(8,128)}, f32[336,128]{1,0:T(8,128)}, u32[]{:S(2)}, u32[]{:S(2)}) %collective-permute-start.17) | collective-permute-done | bytes 172064 | tf_op jit(solution)/shard_map/ppermute | solution.py:379
  72.4 2.1 %last.1 = (f32[864,256]{1,0:T(8,128)}, f32[8,128]{1,0:T(8,128)S(1)}) custom-call(f32[336,256]{1,0:T(8,128)S(1)} %get-tuple-element.97.refs_0_, f32[336,128]{1,0:T(8,128)} %collective-permute-done.16.refs_1_, f32[336,128]{1,0:T(8,128)} %collective-permute-done.17.refs_2_, ...), custom_call_target="tpu_custom_call", output_to_operand_aliasing={{1}: (6, {}), {0}: (5, {})} | custom-call | flops 99999997952 | bytes 1 | tf_op jit(solution)/shard_map/last/pallas_call | solution.py:369
  (23 shorter events, 0.1 us)
Async XLA Ops:
  1.2 12.9 %collective-permute-start = (f32[288,128]{1,0:T(8,128)S(1)}, f32[288,128]{1,0:T(8,128)S(1)}, u32[]{:S(2)}, u32[]{:S(2)}) collective-permute-start(f32[288,128]{1,0:T(8,128)S(1)} %get-tuple-element.57), channel_id=1, source_target_pairs={{0,240},{16,0},{32,16},{48,32},{64,48},{80,64},{96,80},{112,96},{1... | collective-permute-start | bytes 442376 | tf_op jit(solution)/shard_map/ppermute | solution.py:379
  9.6 4.5 %collective-permute-start.1 = (f32[288,128]{1,0:T(8,128)S(1)}, f32[288,128]{1,0:T(8,128)S(1)}, u32[]{:S(2)}, u32[]{:S(2)}) collective-permute-start(f32[288,128]{1,0:T(8,128)S(1)} %get-tuple-element.58), channel_id=1, source_target_pairs={{0,12},{4,0},{8,4},{12,8},{1,13},{5,1},{9,5},{13,9},{2,14},{6,2},{... | collective-permute-start | bytes 442376 | tf_op jit(solution)/shard_map/ppermute | solution.py:379
  9.6 2.3 %copy-start = (f32[343,343]{1,0:T(8,128)S(1)}, f32[343,343]{1,0:T(8,128)}, u32[]{:S(2)}) copy-start(f32[343,343]{1,0:T(8,128)} %refs_0_.1) | copy-start | bytes 1411792
  9.6 2.3 %copy-start.1 = (bf16[343,400]{1,0:T(8,128)(2,1)S(1)}, bf16[343,400]{1,0:T(8,128)(2,1)}, u32[]{:S(2)}) copy-start(bf16[343,400]{1,0:T(8,128)(2,1)} %constant.13.clone.refs_2_) | copy-start | bytes 823204
  9.6 2.3 %copy-start.2 = (bf16[400,343]{1,0:T(8,128)(2,1)S(1)}, bf16[400,343]{1,0:T(8,128)(2,1)}, u32[]{:S(2)}) copy-start(bf16[400,343]{1,0:T(8,128)(2,1)} %constant.12.clone.refs_1_) | copy-start | bytes 823204
  9.6 2.3 %copy-start.3 = (bf16[343,64]{1,0:T(8,128)(2,1)S(1)}, bf16[343,64]{1,0:T(8,128)(2,1)}, u32[]{:S(2)}) copy-start(bf16[343,64]{1,0:T(8,128)(2,1)} %constant.14.clone.refs_3_) | copy-start | bytes 131716
  9.6 2.3 %copy-start.4 = (f32[6,6,24]{2,1,0:T(8,128)S(1)}, f32[6,6,24]{2,1,0:T(8,128)}, u32[]{:S(2)}) copy-start(f32[6,6,24]{2,1,0:T(8,128)} %refs_4_.1) | copy-start | bytes 10372
  9.6 4.5 %copy-start.6 = (f32[6,6,24,256]{3,2,1,0:T(8,128)S(1)}, f32[6,6,24,256]{3,2,1,0:T(8,128)}, u32[]{:S(2)}) copy-start(f32[6,6,24,256]{3,2,1,0:T(8,128)} %param.9) | copy-start | bytes 2654212
  9.7 4.4 %collective-permute-start.2 = (f32[48,128]{1,0:T(8,128)S(1)}, f32[48,128]{1,0:T(8,128)S(1)}, u32[]{:S(2)}, u32[]{:S(2)}) collective-permute-start(f32[48,128]{1,0:T(8,128)S(1)} %get-tuple-element.60), channel_id=1, source_target_pairs={{0,252},{4,240},{8,244},{12,248},{16,12},{20,0},{24,4},{28,8},{32,... | collective-permute-start | bytes 73736 | tf_op jit(solution)/shard_map/ppermute | solution.py:389
  14.1 10.3 %copy-start.5 = (f32[1024,256]{1,0:T(8,128)S(1)}, f32[1024,256]{1,0:T(8,128)}, u32[]{:S(2)}) copy-start(f32[1024,256]{1,0:T(8,128)} %refs_1_.2) | copy-start | bytes 3145732
  17.0 12.9 %collective-permute-start.3 = (f32[336,128]{1,0:T(8,128)}, f32[336,128]{1,0:T(8,128)}, u32[]{:S(2)}, u32[]{:S(2)}) collective-permute-start(f32[336,128]{1,0:T(8,128)} %get-tuple-element.67), channel_id=1, source_target_pairs={{0,4},{4,8},{8,12},{12,0},{1,5},{5,9},{9,13},{13,1},{2,6},{6,10},{... | collective-permute-start | bytes 516104 | tf_op jit(solution)/shard_map/ppermute | solution.py:379
  17.7 12.2 %collective-permute-start.4 = (f32[336,128]{1,0:T(8,128)}, f32[336,128]{1,0:T(8,128)}, u32[]{:S(2)}, u32[]{:S(2)}) collective-permute-start(f32[336,128]{1,0:T(8,128)} %get-tuple-element.68), channel_id=1, source_target_pairs={{0,12},{4,0},{8,4},{12,8},{1,13},{5,1},{9,5},{13,9},{2,14},{6,2},{... | collective-permute-start | bytes 516104 | tf_op jit(solution)/shard_map/ppermute | solution.py:379
  18.8 9.3 %collective-permute-start.5 = (f32[336,128]{1,0:T(8,128)S(1)}, f32[336,128]{1,0:T(8,128)S(1)}, u32[]{:S(2)}, u32[]{:S(2)}) collective-permute-start(f32[336,128]{1,0:T(8,128)S(1)} %get-tuple-element.69), channel_id=1, source_target_pairs={{0,16},{16,32},{32,48},{48,64},{64,80},{80,96},{96,112},{112,128},... | collective-permute-start | bytes 516104 | tf_op jit(solution)/shard_map/ppermute | solution.py:379
  20.1 8.0 %collective-permute-start.6 = (f32[336,128]{1,0:T(8,128)S(1)}, f32[336,128]{1,0:T(8,128)S(1)}, u32[]{:S(2)}, u32[]{:S(2)}) collective-permute-start(f32[336,128]{1,0:T(8,128)S(1)} %get-tuple-element.70), channel_id=1, source_target_pairs={{0,240},{16,0},{32,16},{48,32},{64,48},{80,64},{96,80},{112,96},{1... | collective-permute-start | bytes 516104 | tf_op jit(solution)/shard_map/ppermute | solution.py:379
  28.1 4.9 %collective-permute-start.7 = (f32[96,128]{1,0:T(8,128)S(1)}, f32[96,128]{1,0:T(8,128)S(1)}, u32[]{:S(2)}, u32[]{:S(2)}) collective-permute-start(f32[96,128]{1,0:T(8,128)S(1)} %get-tuple-element.75), channel_id=1, source_target_pairs={{0,4},{4,8},{8,12},{12,0},{1,5},{5,9},{9,13},{13,1},{2,6},{6,10},{... | collective-permute-start | bytes 147464 | tf_op jit(solution)/shard_map/ppermute | solution.py:379
  28.2 4.8 %collective-permute-start.8 = (f32[96,128]{1,0:T(8,128)S(1)}, f32[96,128]{1,0:T(8,128)S(1)}, u32[]{:S(2)}, u32[]{:S(2)}) collective-permute-start(f32[96,128]{1,0:T(8,128)S(1)} %get-tuple-element.76), channel_id=1, source_target_pairs={{0,12},{4,0},{8,4},{12,8},{1,13},{5,1},{9,5},{13,9},{2,14},{6,2},{... | collective-permute-start | bytes 147464 | tf_op jit(solution)/shard_map/ppermute | solution.py:379
  34.4 16.8 %collective-permute-start.15 = (f32[1056,128]{1,0:T(8,128)S(1)}, f32[1056,128]{1,0:T(8,128)S(1)}, u32[]{:S(2)}, u32[]{:S(2)}) collective-permute-start(f32[1056,128]{1,0:T(8,128)S(1)} %get-tuple-element.92.refs_0_), channel_id=1, source_target_pairs={{0,3},{1,0},{2,1},{3,2},{4,7},{5,4},{6,5},{7,6},{8,11},{9,8},{10,9... | collective-permute-start | bytes 1622024 | tf_op jit(solution)/shard_map/ppermute | solution.py:379
  35.2 16.0 %collective-permute-start.14 = (f32[1056,128]{1,0:T(8,128)S(1)}, f32[1056,128]{1,0:T(8,128)S(1)}, u32[]{:S(2)}, u32[]{:S(2)}) collective-permute-start(f32[1056,128]{1,0:T(8,128)S(1)} %get-tuple-element.92.refs_0_), channel_id=1, source_target_pairs={{0,1},{1,2},{2,3},{3,0},{4,5},{5,6},{6,7},{7,4},{8,9},{9,10},{10,1... | collective-permute-start | bytes 1622024 | tf_op jit(solution)/shard_map/ppermute | solution.py:379
  37.7 9.5 %collective-permute-start.9 = (f32[288,128]{1,0:T(8,128)S(1)}, f32[288,128]{1,0:T(8,128)S(1)}, u32[]{:S(2)}, u32[]{:S(2)}) collective-permute-start(f32[288,128]{1,0:T(8,128)S(1)} %get-tuple-element.85), channel_id=1, source_target_pairs={{0,16},{16,32},{32,48},{48,64},{64,80},{80,96},{96,112},{112,128},... | collective-permute-start | bytes 442376 | tf_op jit(solution)/shard_map/ppermute | solution.py:379
  37.7 9.5 %collective-permute-start.10 = (f32[288,128]{1,0:T(8,128)S(1)}, f32[288,128]{1,0:T(8,128)S(1)}, u32[]{:S(2)}, u32[]{:S(2)}) collective-permute-start(f32[288,128]{1,0:T(8,128)S(1)} %get-tuple-element.86), channel_id=1, source_target_pairs={{0,4},{4,8},{8,12},{12,0},{1,5},{5,9},{9,13},{13,1},{2,6},{6,10},{... | collective-permute-start | bytes 442376 | tf_op jit(solution)/shard_map/ppermute | solution.py:379
  37.7 7.7 %collective-permute-start.11 = (f32[48,128]{1,0:T(8,128)S(1)}, f32[48,128]{1,0:T(8,128)S(1)}, u32[]{:S(2)}, u32[]{:S(2)}) collective-permute-start(f32[48,128]{1,0:T(8,128)S(1)} %get-tuple-element.87), channel_id=1, source_target_pairs={{0,20},{4,24},{8,28},{12,16},{16,36},{20,40},{24,44},{28,32},{32,5... | collective-permute-start | bytes 73736 | tf_op jit(solution)/shard_map/ppermute | solution.py:389
  48.0 12.4 %collective-permute-start.13 = (f32[672,128]{1,0:T(8,128)}, f32[672,128]{1,0:T(8,128)}, u32[]{:S(2)}, u32[]{:S(2)}) collective-permute-start(f32[672,128]{1,0:T(8,128)} %get-tuple-element.89.refs_0_), channel_id=1, source_target_pairs={{0,3},{1,0},{2,1},{3,2},{4,7},{5,4},{6,5},{7,6},{8,11},{9,8},{10,9... | collective-permute-start | bytes 1032200 | tf_op jit(solution)/shard_map/ppermute | solution.py:379
  48.0 12.4 %collective-permute-start.12 = (f32[672,128]{1,0:T(8,128)}, f32[672,128]{1,0:T(8,128)}, u32[]{:S(2)}, u32[]{:S(2)}) collective-permute-start(f32[672,128]{1,0:T(8,128)} %get-tuple-element.89.refs_0_), channel_id=1, source_target_pairs={{0,1},{1,2},{2,3},{3,0},{4,5},{5,6},{6,7},{7,4},{8,9},{9,10},{10,1... | collective-permute-start | bytes 1032200 | tf_op jit(solution)/shard_map/ppermute | solution.py:379
  52.1 15.2 %collective-permute-start.18 = (f32[528,128]{1,0:T(8,128)}, f32[528,128]{1,0:T(8,128)}, u32[]{:S(2)}, u32[]{:S(2)}) collective-permute-start(f32[528,128]{1,0:T(8,128)} %get-tuple-element.103), channel_id=1, source_target_pairs={{0,1},{1,2},{2,3},{3,0},{4,5},{5,6},{6,7},{7,4},{8,9},{9,10},{10,1... | collective-permute-start | bytes 811016 | tf_op jit(solution)/shard_map/ppermute | solution.py:379
  53.5 13.8 %collective-permute-start.19 = (f32[528,128]{1,0:T(8,128)}, f32[528,128]{1,0:T(8,128)}, u32[]{:S(2)}, u32[]{:S(2)}) collective-permute-start(f32[528,128]{1,0:T(8,128)} %get-tuple-element.104), channel_id=1, source_target_pairs={{0,3},{1,0},{2,1},{3,2},{4,7},{5,4},{6,5},{7,6},{8,11},{9,8},{10,9... | collective-permute-start | bytes 811016 | tf_op jit(solution)/shard_map/ppermute | solution.py:379
  62.2 7.4 %collective-permute-start.16 = (f32[336,128]{1,0:T(8,128)}, f32[336,128]{1,0:T(8,128)}, u32[]{:S(2)}, u32[]{:S(2)}) collective-permute-start(f32[336,128]{1,0:T(8,128)} %get-tuple-element.98), channel_id=1, source_target_pairs={{0,1},{1,2},{2,3},{3,0},{4,5},{5,6},{6,7},{7,4},{8,9},{9,10},{10,1... | collective-permute-start | bytes 516104 | tf_op jit(solution)/shard_map/ppermute | solution.py:379
  65.5 6.9 %collective-permute-start.17 = (f32[336,128]{1,0:T(8,128)}, f32[336,128]{1,0:T(8,128)}, u32[]{:S(2)}, u32[]{:S(2)}) collective-permute-start(f32[336,128]{1,0:T(8,128)} %get-tuple-element.99), channel_id=1, source_target_pairs={{0,3},{1,0},{2,1},{3,2},{4,7},{5,4},{6,5},{7,6},{8,11},{9,8},{10,9... | collective-permute-start | bytes 516104 | tf_op jit(solution)/shard_map/ppermute | solution.py:379

commit v4 on v3

--- a/solution.py
+++ b/solution.py
@@ -24,8 +24,8 @@
 LIMIT = 16 * 1024 * 1024
 WHOLE = 60 * 1024 * 1024
 
-LINES1 = [(0, y) for y in range(6)] + [(x, 0) for x in range(1, 6)] + [(x, 1) for x in range(1, 4)]
-LINES2 = [(x, 1) for x in (4, 5)] + [(x, y) for x in range(1, 6) for y in range(2, 6)]
+LINES1 = [(0, y) for y in range(6)] + [(x, 0) for x in range(1, 6)]
+LINES2 = [(x, y) for x in range(1, 6) for y in range(1, 6)]
 OWNED = 36 * NZ
 SET1 = len(LINES1) * NZ
 SET2 = len(LINES2) * NZ
@@ -307,10 +307,8 @@
             ys[at : at + 1] += 2.0 * (local[at : at + 1] * c_ref[z * CROWS : z * CROWS + 1])
             set1[every(base1 + z, 6)] = ys[at : at + 6]
             set1[every(base1 + EDGE + z, 5)] = ys[pl.ds(at + 6, 5, stride=6)]
-            set1[every(base1 + 11 * NZ + z, 3)] = ys[pl.ds(at + 7, 3, stride=6)]
-            set2[every(base2 + z, 2)] = ys[pl.ds(at + 25, 2, stride=6)]
             for x in range(1, 6):
-                set2[every(base2 + (4 * x - 2) * NZ + z, 4)] = ys[at + 6 * x + 2 : at + 6 * x + 6]
+                set2[every(base2 + 5 * (x - 1) * NZ + z, 5)] = ys[at + 6 * x + 1 : at + 6 * x + 6]
             push_x[every(part * EDGE + z, 6)] = ys[at + 36 : at + 42]
             push_c[part * NZ + z : part * NZ + z + 1] = ys[at + 42 : at + 43]
             push_y[every(part * EDGE + z, 6)] = ys[at + 43 : at + 49]
@@ -518,7 +516,6 @@
     far2 = relayed("relay2", l2, r2)
     (total2,) = run(call(near_kernel, "near2", [VM] * 5, [wide2]), v2, l2, r2, r_high, r_low)
     far1 = relayed("relay1", l1, r1)
-    (total1,) = run(call(near_kernel, "near1", [VM] * 5, [wide1]), v1, l1, r1, r_high, r_low)
     result_shape = [((OWNED, 256), F32)]
 
     def far_scratch(lines):
@@ -528,6 +525,7 @@
         call(functools.partial(far_kernel, LINES2), "far2", [VM] * 5, result_shape, far_scratch(LINES2), out=HB),
         total2, *far2, far_high, far_low,
     )
+    (total1,) = run(call(near_kernel, "near1", [VM] * 5, [wide1]), v1, l1, r1, r_high, r_low)
     (result,) = run(
         call(
             functools.partial(far_kernel, LINES1),

time: 75 us -> 74 us (0.987)
  the two profiles are of different devices: /device:TPU:24 before, /device:TPU:1 now
where the time goes in v4:
time: 74 us; the launch traced here: 73.5 us
  starting transfers between devices  31.8 us (43%)
  Pallas kernels  21.1 us (29%)
  waiting for transfers between devices  18.8 us (25%)
  between operations  1.71 us (2%)
    ppermute x18, starting transfers between devices, passed_along(): lax.ppermute(value, axis, [(s, (s + steps) % count) for s in range(count)])  30.8 us
    pallas_call x15, Pallas kernels, __call__(): *results, self.token = kernel(*operands, self.token)  19.9 us
    ppermute x18, waiting for transfers between devices, passed_along(): lax.ppermute(value, axis, [(s, (s + steps) % count) for s in range(count)])  10.1 us
    ppermute x2, waiting for transfers between devices, passed_diagonal(): return lax.ppermute(value, ('slab', 'face'), pairs)  8.73 us
  transfers between devices with their start and end apart: 20, of which 6 were waited for; matrix products, arithmetic and copies ran while one was open for 0% of the time, Pallas kernels for 19%

profile of v4, /device:TPU:1, one launch (start us, length us, event | category | flops | bytes accessed | tf_op | source)
XLA Modules:
  0.0 73.5 jit_solution(341444361301677404)
XLA Ops:
  0.0 1.2 %pulls.1 = (f32[288,128]{1,0:T(8,128)S(1)}, f32[288,128]{1,0:T(8,128)S(1)}, f32[48,128]{1,0:T(8,128)S(1)}) custom-call(f32[864,256]{1,0:T(8,128)} %bitcast.3), custom_call_target="tpu_custom_call" | custom-call | flops 99999997952 | bytes 1 | tf_op jit(solution)/shard_map/pulls/pallas_call | solution.py:423
  1.2 8.9 %collective-permute-start = (f32[288,128]{1,0:T(8,128)S(1)}, f32[288,128]{1,0:T(8,128)S(1)}, u32[]{:S(2)}, u32[]{:S(2)}) collective-permute-start(f32[288,128]{1,0:T(8,128)S(1)} %get-tuple-element.57), channel_id=1, source_target_pairs={{0,240},{16,0},{32,16},{48,32},{64,48},{80,64},{96,80},{112,96},{1... | collective-permute-start | bytes 442376 | tf_op jit(solution)/shard_map/ppermute | solution.py:377
  10.1 1.0 %collective-permute-start.1 = (f32[288,128]{1,0:T(8,128)S(1)}, f32[288,128]{1,0:T(8,128)S(1)}, u32[]{:S(2)}, u32[]{:S(2)}) collective-permute-start(f32[288,128]{1,0:T(8,128)S(1)} %get-tuple-element.58), channel_id=1, source_target_pairs={{0,12},{4,0},{8,4},{12,8},{1,13},{5,1},{9,5},{13,9},{2,14},{6,2},{... | collective-permute-start | bytes 442376 | tf_op jit(solution)/shard_map/ppermute | solution.py:377
  11.1 0.0 copy-start.3
  11.1 0.0 copy-start.4
  11.1 0.0 copy-start.6
  11.2 1.0 %collective-permute-start.2 = (f32[48,128]{1,0:T(8,128)S(1)}, f32[48,128]{1,0:T(8,128)S(1)}, u32[]{:S(2)}, u32[]{:S(2)}) collective-permute-start(f32[48,128]{1,0:T(8,128)S(1)} %get-tuple-element.60), channel_id=1, source_target_pairs={{0,252},{4,240},{8,244},{12,248},{16,12},{20,0},{24,4},{28,8},{32,... | collective-permute-start | bytes 73736 | tf_op jit(solution)/shard_map/ppermute | solution.py:387
  13.6 2.1 %cell.1 = (bf16[400,400]{1,0:T(8,128)(2,1)S(1)}, bf16[400,400]{1,0:T(8,128)(2,1)S(1)}, bf16[400,64]{1,0:T(8,128)(2,1)S(1)}, bf16[400,64]{1,0:T(8,128)(2,1)S(1)},...) custom-call(f32[343,343]{1,0:T(8,128)S(1)} %copy-done, ...), custom_call_target="tpu_custom_call", output_to_operand_aliasing={{5}: (7, {})} | custom-call | flops 1 | bytes 1 | tf_op jit(solution)/shard_map/cell/pallas_call | solution.py:367
  15.7 0.0 collective-permute-done.2.refs_3_
  15.7 0.0 collective-permute-done.1.refs_2_
  15.7 0.0 copy-start.5
  15.8 2.8 %first.1 = (f32[2,1344,128]{2,1,0:T(8,128)S(1)}, f32[336,128]{1,0:T(8,128)}, f32[336,128]{1,0:T(8,128)}, f32[336,128]{1,0:T(8,128)S(1)}, f32[336,128]{1,0:T(8,128)S(1)}, /*index=5*/f32[8,128]{1,0:T(8,128)S(1)}) custom-call(f32[864,256]{1,0:T(8,128)S(1)} %bitcast.4, f32[288,128]{1,0:T(8,128)S(1)} %collective-permute-done.refs_1_, ...), custom_call_target="tpu_custom_call", output_to_operand_aliasing={{5}: (7, {})} | custom-call | flops 99999997952 | bytes 1 | tf_op jit(solution)/shard_map/first/pallas_call | solution.py:367
  18.6 0.1 collective-permute-start.3
  18.7 0.5 collective-permute-start.4
  19.2 1.4 %collective-permute-start.5 = (f32[336,128]{1,0:T(8,128)S(1)}, f32[336,128]{1,0:T(8,128)S(1)}, u32[]{:S(2)}, u32[]{:S(2)}) collective-permute-start(f32[336,128]{1,0:T(8,128)S(1)} %get-tuple-element.69), channel_id=1, source_target_pairs={{0,16},{16,32},{32,48},{48,64},{64,80},{80,96},{96,112},{112,128},... | collective-permute-start | bytes 516104 | tf_op jit(solution)/shard_map/ppermute | solution.py:377
  20.6 3.6 %collective-permute-start.6 = (f32[336,128]{1,0:T(8,128)S(1)}, f32[336,128]{1,0:T(8,128)S(1)}, u32[]{:S(2)}, u32[]{:S(2)}) collective-permute-start(f32[336,128]{1,0:T(8,128)S(1)} %get-tuple-element.70), channel_id=1, source_target_pairs={{0,240},{16,0},{32,16},{48,32},{64,48},{80,64},{96,80},{112,96},{1... | collective-permute-start | bytes 516104 | tf_op jit(solution)/shard_map/ppermute | solution.py:377
  24.3 0.2 rotation.1
  24.4 3.1 %collective-permute-done.5.refs_0_.refs_3_ = f32[336,128]{1,0:T(8,128)S(1)} collective-permute-done((f32[336,128]{1,0:T(8,128)S(1)}, f32[336,128]{1,0:T(8,128)S(1)}, u32[]{:S(2)}, u32[]{:S(2)}) %collective-permute-start.5) | collective-permute-done | bytes 172064 | tf_op jit(solution)/shard_map/ppermute | solution.py:377
  27.6 0.0 collective-permute-done.6.refs_1_.refs_4_
  27.6 2.7 %collective-permute-start.7 = (f32[96,128]{1,0:T(8,128)S(1)}, f32[96,128]{1,0:T(8,128)S(1)}, u32[]{:S(2)}, u32[]{:S(2)}) collective-permute-start(f32[96,128]{1,0:T(8,128)S(1)} %get-tuple-element.75), channel_id=1, source_target_pairs={{0,4},{4,8},{8,12},{12,0},{1,5},{5,9},{9,13},{13,1},{2,6},{6,10},{... | collective-permute-start | bytes 147464 | tf_op jit(solution)/shard_map/ppermute | solution.py:377
  30.3 0.0 collective-permute-start.8
  30.3 0.0 collective-permute-done.3.refs_1_
  30.3 0.0 collective-permute-done.4.refs_2_
  30.3 3.1 %second.1 = (f32[2,1344,128]{2,1,0:T(8,128)S(1)}, f32[8,128]{1,0:T(8,128)S(1)}) custom-call(f32[2,1344,128]{2,1,0:T(8,128)S(1)} %get-tuple-element.66.refs_0_, f32[336,128]{1,0:T(8,128)} %collective-permute-done.3.refs_1_, f32[336,128]{1,0:T(8,128)} %collective-permute-done.4.refs_2_, ...), custom_call_target="tpu_custom_call", output_to_operand_aliasing={{1}: (8, {})} | custom-call | flops 99999997952 | bytes 1 | tf_op jit(solution)/shard_map/second/pallas_call | solution.py:367
  33.4 0.0 collective-permute-done.7.refs_1_
  33.4 0.4 collective-permute-done.8.refs_2_
  33.8 1.4 %third.1 = (f32[528,128]{1,0:T(8,128)S(1)}, f32[1200,128]{1,0:T(8,128)S(1)}, f32[288,128]{1,0:T(8,128)S(1)}, f32[288,128]{1,0:T(8,128)S(1)}, f32[48,128]{1,0:T(8,128)S(1)}, /*index=5*/f32[8,128]{1,0:T(8,128)S(1)}) custom-call(f32[2,1344,128]{2,1,0:T(8,128)S(1)} %get-tuple-element.74.refs_0_, ...), custom_call_target="tpu_custom_call", output_to_operand_aliasing={{5}: (7, {})} | custom-call | flops 99999997952 | bytes 1 | tf_op jit(solution)/shard_map/third/pallas_call | solution.py:367
  35.2 2.8 %collective-permute-start.15 = (f32[1200,128]{1,0:T(8,128)S(1)}, f32[1200,128]{1,0:T(8,128)S(1)}, u32[]{:S(2)}, u32[]{:S(2)}) collective-permute-start(f32[1200,128]{1,0:T(8,128)S(1)} %get-tuple-element.92.refs_0_), channel_id=1, source_target_pairs={{0,3},{1,0},{2,1},{3,2},{4,7},{5,4},{6,5},{7,6},{8,11},{9,8},{10,9... | collective-permute-start | bytes 1843208 | tf_op jit(solution)/shard_map/ppermute | solution.py:377
  38.0 0.0 collective-permute-start.14
  38.0 1.6 %collective-permute-start.10 = (f32[288,128]{1,0:T(8,128)S(1)}, f32[288,128]{1,0:T(8,128)S(1)}, u32[]{:S(2)}, u32[]{:S(2)}) collective-permute-start(f32[288,128]{1,0:T(8,128)S(1)} %get-tuple-element.86), channel_id=1, source_target_pairs={{0,4},{4,8},{8,12},{12,0},{1,5},{5,9},{9,13},{13,1},{2,6},{6,10},{... | collective-permute-start | bytes 442376 | tf_op jit(solution)/shard_map/ppermute | solution.py:377
  39.7 8.7 %collective-permute-done.11.refs_3_ = f32[48,128]{1,0:T(8,128)S(1)} collective-permute-done((f32[48,128]{1,0:T(8,128)S(1)}, f32[48,128]{1,0:T(8,128)S(1)}, u32[]{:S(2)}, u32[]{:S(2)}) %collective-permute-start.11) | collective-permute-done | bytes 24608 | tf_op jit(solution)/shard_map/ppermute | solution.py:387
  48.4 0.0 collective-permute-done.10.refs_2_
  48.4 0.8 %finish.1 = (f32[528,128]{1,0:T(8,128)}, f32[8,128]{1,0:T(8,128)S(1)}) custom-call(f32[528,128]{1,0:T(8,128)S(1)} %get-tuple-element.80.refs_0_, f32[288,128]{1,0:T(8,128)S(1)} %collective-permute-done.9.refs_1_, f32[288,128]{1,0:T(8,128)S(1)} %collective-permute-done.10.refs_2_, ...), custom_call_target="tpu_custom_call", output_to_operand_aliasing={{1}: (4, {})} | custom-call | flops 1 | bytes 1 | tf_op jit(solution)/shard_map/finish/pallas_call | solution.py:367
  49.1 2.7 %collective-permute-start.13 = (f32[528,128]{1,0:T(8,128)}, f32[528,128]{1,0:T(8,128)}, u32[]{:S(2)}, u32[]{:S(2)}) collective-permute-start(f32[528,128]{1,0:T(8,128)} %get-tuple-element.89.refs_0_), channel_id=1, source_target_pairs={{0,3},{1,0},{2,1},{3,2},{4,7},{5,4},{6,5},{7,6},{8,11},{9,8},{10,9... | collective-permute-start | bytes 811016 | tf_op jit(solution)/shard_map/ppermute | solution.py:377
  51.8 1.8 %collective-permute-done.14.refs_0_.refs_1_ = f32[1200,128]{1,0:T(8,128)S(1)} collective-permute-done((f32[1200,128]{1,0:T(8,128)S(1)}, f32[1200,128]{1,0:T(8,128)S(1)}, u32[]{:S(2)}, u32[]{:S(2)}) %collective-permute-start.14) | collective-permute-done | bytes 614432 | tf_op jit(solution)/shard_map/ppermute | solution.py:377
  53.6 0.9 %relay2.1 = (f32[600,128]{1,0:T(8,128)}, f32[600,128]{1,0:T(8,128)}, f32[8,128]{1,0:T(8,128)S(1)}) custom-call(f32[1200,128]{1,0:T(8,128)S(1)} %collective-permute-done.14.refs_0_.refs_1_, f32[1200,128]{1,0:T(8,128)S(1)} %collective-permute-done.15.refs_1_.refs_2_, f32[8,128]{1,0:T(8,128)S(1)} %get-tuple-element.93.refs_2_), custom_call_target="tpu_custom_call", output_to_operand_aliasing={{2}: (2, {})} | custom-call | flops 99999997952 | bytes 1 | tf_op jit(solution)/shard_map/relay2/pallas_call | solution.py:367
  54.5 0.0 collective-permute-start.16
  54.5 2.7 %collective-permute-start.17 = (f32[600,128]{1,0:T(8,128)}, f32[600,128]{1,0:T(8,128)}, u32[]{:S(2)}, u32[]{:S(2)}) collective-permute-start(f32[600,128]{1,0:T(8,128)} %get-tuple-element.97), channel_id=1, source_target_pairs={{0,3},{1,0},{2,1},{3,2},{4,7},{5,4},{6,5},{7,6},{8,11},{9,8},{10,9... | collective-permute-start | bytes 921608 | tf_op jit(solution)/shard_map/ppermute | solution.py:377
  57.1 0.9 %near2.1 = (f32[600,256]{1,0:T(8,128)S(1)}, f32[8,128]{1,0:T(8,128)S(1)}) custom-call(f32[1200,128]{1,0:T(8,128)S(1)} %get-tuple-element.92.refs_0_, f32[1200,128]{1,0:T(8,128)S(1)} %collective-permute-done.14.refs_0_.refs_1_, f32[1200,128]{1,0:T(8,128)S(1)} %collective-permute-done.15.refs_1_.refs_2_, ...), custom_call_target="tpu_custom_call", output_to_operand_aliasing={{1}: (5, {})} | custom-call | flops 99999997952 | bytes 1 | tf_op jit(solution)/shard_map/near2/pallas_call | solution.py:367
  58.1 0.0 collective-permute-done.13.refs_1_.refs_2_
  58.1 2.6 %collective-permute-done.12.refs_0_.refs_1_ = f32[528,128]{1,0:T(8,128)} collective-permute-done((f32[528,128]{1,0:T(8,128)}, f32[528,128]{1,0:T(8,128)}, u32[]{:S(2)}, u32[]{:S(2)}) %collective-permute-start.12) | collective-permute-done | bytes 270368 | tf_op jit(solution)/shard_map/ppermute | solution.py:377
  60.7 1.8 %relay1.1 = (f32[264,128]{1,0:T(8,128)}, f32[264,128]{1,0:T(8,128)}, f32[8,128]{1,0:T(8,128)S(1)}) custom-call(f32[528,128]{1,0:T(8,128)} %collective-permute-done.12.refs_0_.refs_1_, f32[528,128]{1,0:T(8,128)} %collective-permute-done.13.refs_1_.refs_2_, f32[8,128]{1,0:T(8,128)S(1)} %get-tuple-element.100.refs_2_), custom_call_target="tpu_custom_call", output_to_operand_aliasing={{2}: (2, {})} | custom-call | flops 99999997952 | bytes 1 | tf_op jit(solution)/shard_map/relay1/pallas_call | solution.py:367
  62.5 2.7 %collective-permute-start.19 = (f32[264,128]{1,0:T(8,128)}, f32[264,128]{1,0:T(8,128)}, u32[]{:S(2)}, u32[]{:S(2)}) collective-permute-start(f32[264,128]{1,0:T(8,128)} %get-tuple-element.105), channel_id=1, source_target_pairs={{0,3},{1,0},{2,1},{3,2},{4,7},{5,4},{6,5},{7,6},{8,11},{9,8},{10,9... | collective-permute-start | bytes 405512 | tf_op jit(solution)/shard_map/ppermute | solution.py:377
  65.1 2.2 %collective-permute-done.16.refs_1_ = f32[600,128]{1,0:T(8,128)} collective-permute-done((f32[600,128]{1,0:T(8,128)}, f32[600,128]{1,0:T(8,128)}, u32[]{:S(2)}, u32[]{:S(2)}) %collective-permute-start.16) | collective-permute-done | bytes 307232 | tf_op jit(solution)/shard_map/ppermute | solution.py:377
  67.3 2.3 %far2.1 = (f32[864,256]{1,0:T(8,128)}, f32[8,128]{1,0:T(8,128)S(1)}) custom-call(f32[600,256]{1,0:T(8,128)S(1)} %get-tuple-element.95.refs_0_, f32[600,128]{1,0:T(8,128)} %collective-permute-done.16.refs_1_, f32[600,128]{1,0:T(8,128)} %collective-permute-done.17.refs_2_, ...), custom_call_target="tpu_custom_call", output_to_operand_aliasing={{1}: (5, {})} | custom-call | flops 99999997952 | bytes 1 | tf_op jit(solution)/shard_map/far2/pallas_call | solution.py:367
  69.6 1.6 %near1.1 = (f32[264,256]{1,0:T(8,128)S(1)}, f32[8,128]{1,0:T(8,128)S(1)}) custom-call(f32[528,128]{1,0:T(8,128)} %get-tuple-element.89.refs_0_, f32[528,128]{1,0:T(8,128)} %collective-permute-done.12.refs_0_.refs_1_, f32[528,128]{1,0:T(8,128)} %collective-permute-done.13.refs_1_.refs_2_, ...), custom_call_target="tpu_custom_call", output_to_operand_aliasing={{1}: (5, {})} | custom-call | flops 99999997952 | bytes 1 | tf_op jit(solution)/shard_map/near1/pallas_call | solution.py:367
  71.3 0.0 collective-permute-done.19.refs_2_
  71.3 2.0 %last.1 = (f32[864,256]{1,0:T(8,128)}, f32[8,128]{1,0:T(8,128)S(1)}) custom-call(f32[264,256]{1,0:T(8,128)S(1)} %get-tuple-element.103.refs_0_, f32[264,128]{1,0:T(8,128)} %collective-permute-done.18.refs_1_, f32[264,128]{1,0:T(8,128)} %collective-permute-done.19.refs_2_, ...), custom_call_target="tpu_custom_call", output_to_operand_aliasing={{1}: (6, {}), {0}: (5, {})} | custom-call | flops 99999997952 | bytes 1 | tf_op jit(solution)/shard_map/last/pallas_call | solution.py:367
  (23 shorter events, 0.1 us)
Async XLA Ops:
  1.2 14.5 %collective-permute-start = (f32[288,128]{1,0:T(8,128)S(1)}, f32[288,128]{1,0:T(8,128)S(1)}, u32[]{:S(2)}, u32[]{:S(2)}) collective-permute-start(f32[288,128]{1,0:T(8,128)S(1)} %get-tuple-element.57), channel_id=1, source_target_pairs={{0,240},{16,0},{32,16},{48,32},{64,48},{80,64},{96,80},{112,96},{1... | collective-permute-start | bytes 442376 | tf_op jit(solution)/shard_map/ppermute | solution.py:377
  10.1 5.6 %collective-permute-start.1 = (f32[288,128]{1,0:T(8,128)S(1)}, f32[288,128]{1,0:T(8,128)S(1)}, u32[]{:S(2)}, u32[]{:S(2)}) collective-permute-start(f32[288,128]{1,0:T(8,128)S(1)} %get-tuple-element.58), channel_id=1, source_target_pairs={{0,12},{4,0},{8,4},{12,8},{1,13},{5,1},{9,5},{13,9},{2,14},{6,2},{... | collective-permute-start | bytes 442376 | tf_op jit(solution)/shard_map/ppermute | solution.py:377
  11.1 2.4 %copy-start = (f32[343,343]{1,0:T(8,128)S(1)}, f32[343,343]{1,0:T(8,128)}, u32[]{:S(2)}) copy-start(f32[343,343]{1,0:T(8,128)} %refs_0_.1) | copy-start | bytes 1411792
  11.1 2.4 %copy-start.1 = (bf16[343,400]{1,0:T(8,128)(2,1)S(1)}, bf16[343,400]{1,0:T(8,128)(2,1)}, u32[]{:S(2)}) copy-start(bf16[343,400]{1,0:T(8,128)(2,1)} %constant.13.clone.refs_2_) | copy-start | bytes 823204
  11.1 2.4 %copy-start.2 = (bf16[400,343]{1,0:T(8,128)(2,1)S(1)}, bf16[400,343]{1,0:T(8,128)(2,1)}, u32[]{:S(2)}) copy-start(bf16[400,343]{1,0:T(8,128)(2,1)} %constant.12.clone.refs_1_) | copy-start | bytes 823204
  11.1 2.4 %copy-start.3 = (bf16[343,64]{1,0:T(8,128)(2,1)S(1)}, bf16[343,64]{1,0:T(8,128)(2,1)}, u32[]{:S(2)}) copy-start(bf16[343,64]{1,0:T(8,128)(2,1)} %constant.14.clone.refs_3_) | copy-start | bytes 131716
  11.1 2.4 %copy-start.4 = (f32[6,6,24]{2,1,0:T(8,128)S(1)}, f32[6,6,24]{2,1,0:T(8,128)}, u32[]{:S(2)}) copy-start(f32[6,6,24]{2,1,0:T(8,128)} %refs_4_.1) | copy-start | bytes 10372
  11.1 4.6 %copy-start.6 = (f32[6,6,24,256]{3,2,1,0:T(8,128)S(1)}, f32[6,6,24,256]{3,2,1,0:T(8,128)}, u32[]{:S(2)}) copy-start(f32[6,6,24,256]{3,2,1,0:T(8,128)} %param.9) | copy-start | bytes 2654212
  11.2 4.5 %collective-permute-start.2 = (f32[48,128]{1,0:T(8,128)S(1)}, f32[48,128]{1,0:T(8,128)S(1)}, u32[]{:S(2)}, u32[]{:S(2)}) collective-permute-start(f32[48,128]{1,0:T(8,128)S(1)} %get-tuple-element.60), channel_id=1, source_target_pairs={{0,252},{4,240},{8,244},{12,248},{16,12},{20,0},{24,4},{28,8},{32,... | collective-permute-start | bytes 73736 | tf_op jit(solution)/shard_map/ppermute | solution.py:387
  15.7 8.5 %copy-start.5 = (f32[1024,256]{1,0:T(8,128)S(1)}, f32[1024,256]{1,0:T(8,128)}, u32[]{:S(2)}) copy-start(f32[1024,256]{1,0:T(8,128)} %refs_1_.2) | copy-start | bytes 3145732
  18.6 11.7 %collective-permute-start.3 = (f32[336,128]{1,0:T(8,128)}, f32[336,128]{1,0:T(8,128)}, u32[]{:S(2)}, u32[]{:S(2)}) collective-permute-start(f32[336,128]{1,0:T(8,128)} %get-tuple-element.67), channel_id=1, source_target_pairs={{0,4},{4,8},{8,12},{12,0},{1,5},{5,9},{9,13},{13,1},{2,6},{6,10},{... | collective-permute-start | bytes 516104 | tf_op jit(solution)/shard_map/ppermute | solution.py:377
  18.7 11.6 %collective-permute-start.4 = (f32[336,128]{1,0:T(8,128)}, f32[336,128]{1,0:T(8,128)}, u32[]{:S(2)}, u32[]{:S(2)}) collective-permute-start(f32[336,128]{1,0:T(8,128)} %get-tuple-element.68), channel_id=1, source_target_pairs={{0,12},{4,0},{8,4},{12,8},{1,13},{5,1},{9,5},{13,9},{2,14},{6,2},{... | collective-permute-start | bytes 516104 | tf_op jit(solution)/shard_map/ppermute | solution.py:377
  19.2 8.4 %collective-permute-start.5 = (f32[336,128]{1,0:T(8,128)S(1)}, f32[336,128]{1,0:T(8,128)S(1)}, u32[]{:S(2)}, u32[]{:S(2)}) collective-permute-start(f32[336,128]{1,0:T(8,128)S(1)} %get-tuple-element.69), channel_id=1, source_target_pairs={{0,16},{16,32},{32,48},{48,64},{64,80},{80,96},{96,112},{112,128},... | collective-permute-start | bytes 516104 | tf_op jit(solution)/shard_map/ppermute | solution.py:377
  20.6 6.9 %collective-permute-start.6 = (f32[336,128]{1,0:T(8,128)S(1)}, f32[336,128]{1,0:T(8,128)S(1)}, u32[]{:S(2)}, u32[]{:S(2)}) collective-permute-start(f32[336,128]{1,0:T(8,128)S(1)} %get-tuple-element.70), channel_id=1, source_target_pairs={{0,240},{16,0},{32,16},{48,32},{64,48},{80,64},{96,80},{112,96},{1... | collective-permute-start | bytes 516104 | tf_op jit(solution)/shard_map/ppermute | solution.py:377
  27.6 5.8 %collective-permute-start.7 = (f32[96,128]{1,0:T(8,128)S(1)}, f32[96,128]{1,0:T(8,128)S(1)}, u32[]{:S(2)}, u32[]{:S(2)}) collective-permute-start(f32[96,128]{1,0:T(8,128)S(1)} %get-tuple-element.75), channel_id=1, source_target_pairs={{0,4},{4,8},{8,12},{12,0},{1,5},{5,9},{9,13},{13,1},{2,6},{6,10},{... | collective-permute-start | bytes 147464 | tf_op jit(solution)/shard_map/ppermute | solution.py:377
  30.3 3.5 %collective-permute-start.8 = (f32[96,128]{1,0:T(8,128)S(1)}, f32[96,128]{1,0:T(8,128)S(1)}, u32[]{:S(2)}, u32[]{:S(2)}) collective-permute-start(f32[96,128]{1,0:T(8,128)S(1)} %get-tuple-element.76), channel_id=1, source_target_pairs={{0,12},{4,0},{8,4},{12,8},{1,13},{5,1},{9,5},{13,9},{2,14},{6,2},{... | collective-permute-start | bytes 147464 | tf_op jit(solution)/shard_map/ppermute | solution.py:377
  35.2 16.6 %collective-permute-start.15 = (f32[1200,128]{1,0:T(8,128)S(1)}, f32[1200,128]{1,0:T(8,128)S(1)}, u32[]{:S(2)}, u32[]{:S(2)}) collective-permute-start(f32[1200,128]{1,0:T(8,128)S(1)} %get-tuple-element.92.refs_0_), channel_id=1, source_target_pairs={{0,3},{1,0},{2,1},{3,2},{4,7},{5,4},{6,5},{7,6},{8,11},{9,8},{10,9... | collective-permute-start | bytes 1843208 | tf_op jit(solution)/shard_map/ppermute | solution.py:377
  38.0 15.6 %collective-permute-start.14 = (f32[1200,128]{1,0:T(8,128)S(1)}, f32[1200,128]{1,0:T(8,128)S(1)}, u32[]{:S(2)}, u32[]{:S(2)}) collective-permute-start(f32[1200,128]{1,0:T(8,128)S(1)} %get-tuple-element.92.refs_0_), channel_id=1, source_target_pairs={{0,1},{1,2},{2,3},{3,0},{4,5},{5,6},{6,7},{7,4},{8,9},{9,10},{10,1... | collective-permute-start | bytes 1843208 | tf_op jit(solution)/shard_map/ppermute | solution.py:377
  38.0 10.4 %collective-permute-start.9 = (f32[288,128]{1,0:T(8,128)S(1)}, f32[288,128]{1,0:T(8,128)S(1)}, u32[]{:S(2)}, u32[]{:S(2)}) collective-permute-start(f32[288,128]{1,0:T(8,128)S(1)} %get-tuple-element.85), channel_id=1, source_target_pairs={{0,16},{16,32},{32,48},{48,64},{64,80},{80,96},{96,112},{112,128},... | collective-permute-start | bytes 442376 | tf_op jit(solution)/shard_map/ppermute | solution.py:377
  38.0 10.4 %collective-permute-start.10 = (f32[288,128]{1,0:T(8,128)S(1)}, f32[288,128]{1,0:T(8,128)S(1)}, u32[]{:S(2)}, u32[]{:S(2)}) collective-permute-start(f32[288,128]{1,0:T(8,128)S(1)} %get-tuple-element.86), channel_id=1, source_target_pairs={{0,4},{4,8},{8,12},{12,0},{1,5},{5,9},{9,13},{13,1},{2,6},{6,10},{... | collective-permute-start | bytes 442376 | tf_op jit(solution)/shard_map/ppermute | solution.py:377
  39.7 8.7 %collective-permute-start.11 = (f32[48,128]{1,0:T(8,128)S(1)}, f32[48,128]{1,0:T(8,128)S(1)}, u32[]{:S(2)}, u32[]{:S(2)}) collective-permute-start(f32[48,128]{1,0:T(8,128)S(1)} %get-tuple-element.87), channel_id=1, source_target_pairs={{0,20},{4,24},{8,28},{12,16},{16,36},{20,40},{24,44},{28,32},{32,5... | collective-permute-start | bytes 73736 | tf_op jit(solution)/shard_map/ppermute | solution.py:387
  49.1 8.9 %collective-permute-start.13 = (f32[528,128]{1,0:T(8,128)}, f32[528,128]{1,0:T(8,128)}, u32[]{:S(2)}, u32[]{:S(2)}) collective-permute-start(f32[528,128]{1,0:T(8,128)} %get-tuple-element.89.refs_0_), channel_id=1, source_target_pairs={{0,3},{1,0},{2,1},{3,2},{4,7},{5,4},{6,5},{7,6},{8,11},{9,8},{10,9... | collective-permute-start | bytes 811016 | tf_op jit(solution)/shard_map/ppermute | solution.py:377
  51.8 8.9 %collective-permute-start.12 = (f32[528,128]{1,0:T(8,128)}, f32[528,128]{1,0:T(8,128)}, u32[]{:S(2)}, u32[]{:S(2)}) collective-permute-start(f32[528,128]{1,0:T(8,128)} %get-tuple-element.89.refs_0_), channel_id=1, source_target_pairs={{0,1},{1,2},{2,3},{3,0},{4,5},{5,6},{6,7},{7,4},{8,9},{9,10},{10,1... | collective-permute-start | bytes 811016 | tf_op jit(solution)/shard_map/ppermute | solution.py:377
  54.5 12.8 %collective-permute-start.16 = (f32[600,128]{1,0:T(8,128)}, f32[600,128]{1,0:T(8,128)}, u32[]{:S(2)}, u32[]{:S(2)}) collective-permute-start(f32[600,128]{1,0:T(8,128)} %get-tuple-element.96), channel_id=1, source_target_pairs={{0,1},{1,2},{2,3},{3,0},{4,5},{5,6},{6,7},{7,4},{8,9},{9,10},{10,1... | collective-permute-start | bytes 921608 | tf_op jit(solution)/shard_map/ppermute | solution.py:377
  54.5 12.8 %collective-permute-start.17 = (f32[600,128]{1,0:T(8,128)}, f32[600,128]{1,0:T(8,128)}, u32[]{:S(2)}, u32[]{:S(2)}) collective-permute-start(f32[600,128]{1,0:T(8,128)} %get-tuple-element.97), channel_id=1, source_target_pairs={{0,3},{1,0},{2,1},{3,2},{4,7},{5,4},{6,5},{7,6},{8,11},{9,8},{10,9... | collective-permute-start | bytes 921608 | tf_op jit(solution)/shard_map/ppermute | solution.py:377
  62.5 8.8 %collective-permute-start.18 = (f32[264,128]{1,0:T(8,128)}, f32[264,128]{1,0:T(8,128)}, u32[]{:S(2)}, u32[]{:S(2)}) collective-permute-start(f32[264,128]{1,0:T(8,128)} %get-tuple-element.104), channel_id=1, source_target_pairs={{0,1},{1,2},{2,3},{3,0},{4,5},{5,6},{6,7},{7,4},{8,9},{9,10},{10,1... | collective-permute-start | bytes 405512 | tf_op jit(solution)/shard_map/ppermute | solution.py:377
  62.5 8.8 %collective-permute-start.19 = (f32[264,128]{1,0:T(8,128)}, f32[264,128]{1,0:T(8,128)}, u32[]{:S(2)}, u32[]{:S(2)}) collective-permute-start(f32[264,128]{1,0:T(8,128)} %get-tuple-element.105), channel_id=1, source_target_pairs={{0,3},{1,0},{2,1},{3,2},{4,7},{5,4},{6,5},{7,6},{8,11},{9,8},{10,9... | collective-permute-start | bytes 405512 | tf_op jit(solution)/shard_map/ppermute | solution.py:377

commit v5 on v4

--- a/solution.py
+++ b/solution.py
@@ -335,7 +335,7 @@
 SM = pl.BlockSpec(memory_space=pltpu.SMEM)
 
 
-def call(kernel, name, in_specs, shapes, scratch=(), out=None, aliases=(), flops=10**11, limit=LIMIT, ordered=True):
+def call(kernel, name, in_specs, shapes, scratch=(), out=None, aliases=(), flops=10**10, limit=LIMIT, ordered=True):
     inputs, outputs = len(in_specs), len(shapes)
     tokens = 1 if ordered else 0
 

time: 74 us -> 69.9 us (0.945)
  Pallas kernels: 21.1 us -> 12.9 us
  waiting for transfers between devices: 18.8 us -> 23.9 us
    pallas_call x15, Pallas kernels: 19.9 us -> 11.7 us  [__call__(): *results, self.token = kernel(*operands, self.token)]
    ppermute x18, waiting for transfers between devices: 10.1 us -> 14.3 us  [passed_along(): lax.ppermute(value, axis, [(s, (s + steps) % count) for s in range(count)])]
    ppermute x2, waiting for transfers between devices: 8.73 us -> 9.55 us  [passed_diagonal(): return lax.ppermute(value, ('slab', 'face'), pairs)]
  transfers between devices with their start and end apart: 20 -> 20, of which waited for: 6 -> 8; matrix products, arithmetic and copies ran while one was open for 0% -> 0% of each run, Pallas kernels for 19% -> 10%
where the time goes in v5:
time: 69.9 us; the launch traced here: 69.7 us
  starting transfers between devices  31.2 us (45%)
  waiting for transfers between devices  23.9 us (34%)
  Pallas kernels  12.9 us (18%)
  between operations  1.72 us (2%)
    ppermute x18, starting transfers between devices, passed_along(): lax.ppermute(value, axis, [(s, (s + steps) % count) for s in range(count)])  30.1 us
    ppermute x18, waiting for transfers between devices, passed_along(): lax.ppermute(value, axis, [(s, (s + steps) % count) for s in range(count)])  14.3 us
    pallas_call x15, Pallas kernels, __call__(): *results, self.token = kernel(*operands, self.token)  11.7 us
    ppermute x2, waiting for transfers between devices, passed_diagonal(): return lax.ppermute(value, ('slab', 'face'), pairs)  9.55 us
  transfers between devices with their start and end apart: 20, of which 8 were waited for; matrix products, arithmetic and copies ran while one was open for 0% of the time, Pallas kernels for 10%

profile of v5, /device:TPU:1, one launch (start us, length us, event | category | flops | bytes accessed | tf_op | source)
XLA Modules:
  0.0 69.7 jit_solution(3175909100680675414)
XLA Ops:
  0.0 1.2 %pulls.1 = (f32[288,128]{1,0:T(8,128)S(1)}, f32[288,128]{1,0:T(8,128)S(1)}, f32[48,128]{1,0:T(8,128)S(1)}) custom-call(f32[864,256]{1,0:T(8,128)} %bitcast.3), custom_call_target="tpu_custom_call" | custom-call | flops 10000000000 | bytes 1 | tf_op jit(solution)/shard_map/pulls/pallas_call | solution.py:423
  1.2 8.9 %collective-permute-start = (f32[288,128]{1,0:T(8,128)S(1)}, f32[288,128]{1,0:T(8,128)S(1)}, u32[]{:S(2)}, u32[]{:S(2)}) collective-permute-start(f32[288,128]{1,0:T(8,128)S(1)} %get-tuple-element.57), channel_id=1, source_target_pairs={{0,240},{16,0},{32,16},{48,32},{64,48},{80,64},{96,80},{112,96},{1... | collective-permute-start | bytes 442376 | tf_op jit(solution)/shard_map/ppermute | solution.py:377
  10.1 1.0 %collective-permute-start.1 = (f32[288,128]{1,0:T(8,128)S(1)}, f32[288,128]{1,0:T(8,128)S(1)}, u32[]{:S(2)}, u32[]{:S(2)}) collective-permute-start(f32[288,128]{1,0:T(8,128)S(1)} %get-tuple-element.58), channel_id=1, source_target_pairs={{0,12},{4,0},{8,4},{12,8},{1,13},{5,1},{9,5},{13,9},{2,14},{6,2},{... | collective-permute-start | bytes 442376 | tf_op jit(solution)/shard_map/ppermute | solution.py:377
  11.1 0.0 copy-start.3
  11.1 0.0 copy-start.4
  11.1 0.0 copy-start.6
  11.2 1.0 %collective-permute-start.2 = (f32[48,128]{1,0:T(8,128)S(1)}, f32[48,128]{1,0:T(8,128)S(1)}, u32[]{:S(2)}, u32[]{:S(2)}) collective-permute-start(f32[48,128]{1,0:T(8,128)S(1)} %get-tuple-element.60), channel_id=1, source_target_pairs={{0,252},{4,240},{8,244},{12,248},{16,12},{20,0},{24,4},{28,8},{32,... | collective-permute-start | bytes 73736 | tf_op jit(solution)/shard_map/ppermute | solution.py:387
  13.6 2.1 %cell.1 = (bf16[400,400]{1,0:T(8,128)(2,1)S(1)}, bf16[400,400]{1,0:T(8,128)(2,1)S(1)}, bf16[400,64]{1,0:T(8,128)(2,1)S(1)}, bf16[400,64]{1,0:T(8,128)(2,1)S(1)},...) custom-call(f32[343,343]{1,0:T(8,128)S(1)} %copy-done, ...), custom_call_target="tpu_custom_call", output_to_operand_aliasing={{5}: (7, {})} | custom-call | flops 1 | bytes 1 | tf_op jit(solution)/shard_map/cell/pallas_call | solution.py:367
  15.7 0.0 collective-permute-done.2.refs_3_
  15.7 0.0 copy-start.5
  15.8 2.1 %first.1 = (f32[2,1344,128]{2,1,0:T(8,128)S(1)}, f32[336,128]{1,0:T(8,128)S(1)}, f32[336,128]{1,0:T(8,128)S(1)}, f32[336,128]{1,0:T(8,128)S(1)}, f32[336,128]{1,0:T(8,128)S(1)}, /*index=5*/f32[8,128]{1,0:T(8,128)S(1)}) custom-call(f32[864,256]{1,0:T(8,128)S(1)} %bitcast.4, ...), custom_call_target="tpu_custom_call", output_to_operand_aliasing={{5}: (7, {})} | custom-call | flops 10000000000 | bytes 1 | tf_op jit(solution)/shard_map/first/pallas_call | solution.py:367
  17.9 0.1 collective-permute-start.3
  18.0 0.5 collective-permute-start.4
  18.5 1.4 %collective-permute-start.5 = (f32[336,128]{1,0:T(8,128)S(1)}, f32[336,128]{1,0:T(8,128)S(1)}, u32[]{:S(2)}, u32[]{:S(2)}) collective-permute-start(f32[336,128]{1,0:T(8,128)S(1)} %get-tuple-element.69), channel_id=1, source_target_pairs={{0,16},{16,32},{32,48},{48,64},{64,80},{80,96},{96,112},{112,128},... | collective-permute-start | bytes 516104 | tf_op jit(solution)/shard_map/ppermute | solution.py:377
  19.9 3.6 %collective-permute-start.6 = (f32[336,128]{1,0:T(8,128)S(1)}, f32[336,128]{1,0:T(8,128)S(1)}, u32[]{:S(2)}, u32[]{:S(2)}) collective-permute-start(f32[336,128]{1,0:T(8,128)S(1)} %get-tuple-element.70), channel_id=1, source_target_pairs={{0,240},{16,0},{32,16},{48,32},{64,48},{80,64},{96,80},{112,96},{1... | collective-permute-start | bytes 516104 | tf_op jit(solution)/shard_map/ppermute | solution.py:377
  23.6 0.2 rotation.1
  23.7 3.1 %collective-permute-done.5.refs_0_.refs_3_ = f32[336,128]{1,0:T(8,128)S(1)} collective-permute-done((f32[336,128]{1,0:T(8,128)S(1)}, f32[336,128]{1,0:T(8,128)S(1)}, u32[]{:S(2)}, u32[]{:S(2)}) %collective-permute-start.5) | collective-permute-done | bytes 172064 | tf_op jit(solution)/shard_map/ppermute | solution.py:377
  26.8 0.0 collective-permute-done.6.refs_1_.refs_4_
  26.8 2.7 %collective-permute-start.7 = (f32[96,128]{1,0:T(8,128)S(1)}, f32[96,128]{1,0:T(8,128)S(1)}, u32[]{:S(2)}, u32[]{:S(2)}) collective-permute-start(f32[96,128]{1,0:T(8,128)S(1)} %get-tuple-element.75), channel_id=1, source_target_pairs={{0,4},{4,8},{8,12},{12,0},{1,5},{5,9},{9,13},{13,1},{2,6},{6,10},{... | collective-permute-start | bytes 147464 | tf_op jit(solution)/shard_map/ppermute | solution.py:377
  29.6 0.0 collective-permute-start.8
  29.6 0.0 collective-permute-done.3.refs_1_
  29.6 0.0 collective-permute-done.4.refs_2_
  29.6 2.1 %second.1 = (f32[2,1344,128]{2,1,0:T(8,128)S(1)}, f32[8,128]{1,0:T(8,128)S(1)}) custom-call(f32[2,1344,128]{2,1,0:T(8,128)S(1)} %get-tuple-element.66.refs_0_, f32[336,128]{1,0:T(8,128)S(1)} %collective-permute-done.3.refs_1_, f32[336,128]{1,0:T(8,128)S(1)} %collective-permute-done.4.refs_2_, ...), custom_call_target="tpu_custom_call", output_to_operand_aliasing={{1}: (8, {})} | custom-call | flops 10000000000 | bytes 1 | tf_op jit(solution)/shard_map/second/pallas_call | solution.py:367
  31.7 1.4 %collective-permute-done.8.refs_2_ = f32[96,128]{1,0:T(8,128)S(1)} collective-permute-done((f32[96,128]{1,0:T(8,128)S(1)}, f32[96,128]{1,0:T(8,128)S(1)}, u32[]{:S(2)}, u32[]{:S(2)}) %collective-permute-start.8) | collective-permute-done | bytes 49184 | tf_op jit(solution)/shard_map/ppermute | solution.py:377
  33.1 1.4 %third.1 = (f32[528,128]{1,0:T(8,128)S(1)}, f32[1200,128]{1,0:T(8,128)S(1)}, f32[288,128]{1,0:T(8,128)S(1)}, f32[288,128]{1,0:T(8,128)S(1)}, f32[48,128]{1,0:T(8,128)S(1)}, /*index=5*/f32[8,128]{1,0:T(8,128)S(1)}) custom-call(f32[2,1344,128]{2,1,0:T(8,128)S(1)} %get-tuple-element.74.refs_0_, ...), custom_call_target="tpu_custom_call", output_to_operand_aliasing={{5}: (7, {})} | custom-call | flops 10000000000 | bytes 1 | tf_op jit(solution)/shard_map/third/pallas_call | solution.py:367
  34.5 2.8 %collective-permute-start.15 = (f32[1200,128]{1,0:T(8,128)S(1)}, f32[1200,128]{1,0:T(8,128)S(1)}, u32[]{:S(2)}, u32[]{:S(2)}) collective-permute-start(f32[1200,128]{1,0:T(8,128)S(1)} %get-tuple-element.92.refs_0_), channel_id=1, source_target_pairs={{0,3},{1,0},{2,1},{3,2},{4,7},{5,4},{6,5},{7,6},{8,11},{9,8},{10,9... | collective-permute-start | bytes 1843208 | tf_op jit(solution)/shard_map/ppermute | solution.py:377
  37.3 0.0 collective-permute-start.9
  37.3 0.6 collective-permute-start.10
  37.9 0.0 collective-permute-start.11
  37.9 9.6 %collective-permute-done.11.refs_3_ = f32[48,128]{1,0:T(8,128)S(1)} collective-permute-done((f32[48,128]{1,0:T(8,128)S(1)}, f32[48,128]{1,0:T(8,128)S(1)}, u32[]{:S(2)}, u32[]{:S(2)}) %collective-permute-start.11) | collective-permute-done | bytes 24608 | tf_op jit(solution)/shard_map/ppermute | solution.py:387
  47.5 0.0 collective-permute-done.9.refs_1_
  47.5 0.0 collective-permute-done.10.refs_2_
  47.5 2.9 %collective-permute-start.13 = (f32[528,128]{1,0:T(8,128)S(1)}, f32[528,128]{1,0:T(8,128)S(1)}, u32[]{:S(2)}, u32[]{:S(2)}) collective-permute-start(f32[528,128]{1,0:T(8,128)S(1)} %get-tuple-element.89.refs_0_), channel_id=1, source_target_pairs={{0,3},{1,0},{2,1},{3,2},{4,7},{5,4},{6,5},{7,6},{8,11},{9,8},{10,9... | collective-permute-start | bytes 811016 | tf_op jit(solution)/shard_map/ppermute | solution.py:377
  50.4 0.0 collective-permute-start.12
  50.4 0.4 collective-permute-done.15.refs_1_.refs_2_
  50.8 3.2 %collective-permute-done.14.refs_0_.refs_1_ = f32[1200,128]{1,0:T(8,128)S(1)} collective-permute-done((f32[1200,128]{1,0:T(8,128)S(1)}, f32[1200,128]{1,0:T(8,128)S(1)}, u32[]{:S(2)}, u32[]{:S(2)}) %collective-permute-start.14) | collective-permute-done | bytes 614432 | tf_op jit(solution)/shard_map/ppermute | solution.py:377
  54.1 0.1 collective-permute-start.16
  54.2 2.7 %collective-permute-start.17 = (f32[600,128]{1,0:T(8,128)S(1)}, f32[600,128]{1,0:T(8,128)S(1)}, u32[]{:S(2)}, u32[]{:S(2)}) collective-permute-start(f32[600,128]{1,0:T(8,128)S(1)} %get-tuple-element.97), channel_id=1, source_target_pairs={{0,3},{1,0},{2,1},{3,2},{4,7},{5,4},{6,5},{7,6},{8,11},{9,8},{10,9... | collective-permute-start | bytes 921608 | tf_op jit(solution)/shard_map/ppermute | solution.py:377
  56.8 0.9 %near2.1 = (f32[600,256]{1,0:T(8,128)S(1)}, f32[8,128]{1,0:T(8,128)S(1)}) custom-call(f32[1200,128]{1,0:T(8,128)S(1)} %get-tuple-element.92.refs_0_, f32[1200,128]{1,0:T(8,128)S(1)} %collective-permute-done.14.refs_0_.refs_1_, f32[1200,128]{1,0:T(8,128)S(1)} %collective-permute-done.15.refs_1_.refs_2_, ...), custom_call_target="tpu_custom_call", output_to_operand_aliasing={{1}: (5, {})} | custom-call | flops 10000000000 | bytes 1 | tf_op jit(solution)/shard_map/near2/pallas_call | solution.py:367
  57.7 0.0 collective-permute-done.13.refs_1_.refs_2_
  57.7 1.3 %collective-permute-done.12.refs_0_.refs_1_ = f32[528,128]{1,0:T(8,128)S(1)} collective-permute-done((f32[528,128]{1,0:T(8,128)S(1)}, f32[528,128]{1,0:T(8,128)S(1)}, u32[]{:S(2)}, u32[]{:S(2)}) %collective-permute-start.12) | collective-permute-done | bytes 270368 | tf_op jit(solution)/shard_map/ppermute | solution.py:377
  59.1 0.1 collective-permute-start.18
  59.2 2.7 %collective-permute-start.19 = (f32[264,128]{1,0:T(8,128)S(1)}, f32[264,128]{1,0:T(8,128)S(1)}, u32[]{:S(2)}, u32[]{:S(2)}) collective-permute-start(f32[264,128]{1,0:T(8,128)S(1)} %get-tuple-element.105), channel_id=1, source_target_pairs={{0,3},{1,0},{2,1},{3,2},{4,7},{5,4},{6,5},{7,6},{8,11},{9,8},{10,9... | collective-permute-start | bytes 405512 | tf_op jit(solution)/shard_map/ppermute | solution.py:377
  61.8 3.8 %collective-permute-done.16.refs_1_ = f32[600,128]{1,0:T(8,128)S(1)} collective-permute-done((f32[600,128]{1,0:T(8,128)S(1)}, f32[600,128]{1,0:T(8,128)S(1)}, u32[]{:S(2)}, u32[]{:S(2)}) %collective-permute-start.16) | collective-permute-done | bytes 307232 | tf_op jit(solution)/shard_map/ppermute | solution.py:377
  65.6 1.3 %far2.1 = (f32[864,256]{1,0:T(8,128)}, f32[8,128]{1,0:T(8,128)S(1)}) custom-call(f32[600,256]{1,0:T(8,128)S(1)} %get-tuple-element.95.refs_0_, f32[600,128]{1,0:T(8,128)S(1)} %collective-permute-done.16.refs_1_, f32[600,128]{1,0:T(8,128)S(1)} %collective-permute-done.17.refs_2_, ...), custom_call_target="tpu_custom_call", output_to_operand_aliasing={{1}: (5, {})} | custom-call | flops 10000000000 | bytes 1 | tf_op jit(solution)/shard_map/far2/pallas_call | solution.py:367
  66.9 0.5 near1.1
  67.4 1.1 %collective-permute-done.18.refs_1_ = f32[264,128]{1,0:T(8,128)S(1)} collective-permute-done((f32[264,128]{1,0:T(8,128)S(1)}, f32[264,128]{1,0:T(8,128)S(1)}, u32[]{:S(2)}, u32[]{:S(2)}) %collective-permute-start.18) | collective-permute-done | bytes 135200 | tf_op jit(solution)/shard_map/ppermute | solution.py:377
  68.5 1.0 %last.1 = (f32[864,256]{1,0:T(8,128)}, f32[8,128]{1,0:T(8,128)S(1)}) custom-call(f32[264,256]{1,0:T(8,128)S(1)} %get-tuple-element.103.refs_0_, f32[264,128]{1,0:T(8,128)S(1)} %collective-permute-done.18.refs_1_, f32[264,128]{1,0:T(8,128)S(1)} %collective-permute-done.19.refs_2_, ...), custom_call_target="tpu_custom_call", output_to_operand_aliasing={{1}: (6, {}), {0}: (5, {})} | custom-call | flops 10000000000 | bytes 1 | tf_op jit(solution)/shard_map/last/pallas_call | solution.py:367
  (23 shorter events, 0.1 us)
Async XLA Ops:
  1.2 14.5 %collective-permute-start = (f32[288,128]{1,0:T(8,128)S(1)}, f32[288,128]{1,0:T(8,128)S(1)}, u32[]{:S(2)}, u32[]{:S(2)}) collective-permute-start(f32[288,128]{1,0:T(8,128)S(1)} %get-tuple-element.57), channel_id=1, source_target_pairs={{0,240},{16,0},{32,16},{48,32},{64,48},{80,64},{96,80},{112,96},{1... | collective-permute-start | bytes 442376 | tf_op jit(solution)/shard_map/ppermute | solution.py:377
  10.1 5.6 %collective-permute-start.1 = (f32[288,128]{1,0:T(8,128)S(1)}, f32[288,128]{1,0:T(8,128)S(1)}, u32[]{:S(2)}, u32[]{:S(2)}) collective-permute-start(f32[288,128]{1,0:T(8,128)S(1)} %get-tuple-element.58), channel_id=1, source_target_pairs={{0,12},{4,0},{8,4},{12,8},{1,13},{5,1},{9,5},{13,9},{2,14},{6,2},{... | collective-permute-start | bytes 442376 | tf_op jit(solution)/shard_map/ppermute | solution.py:377
  11.1 2.4 %copy-start = (f32[343,343]{1,0:T(8,128)S(1)}, f32[343,343]{1,0:T(8,128)}, u32[]{:S(2)}) copy-start(f32[343,343]{1,0:T(8,128)} %refs_0_.1) | copy-start | bytes 1411792
  11.1 2.4 %copy-start.1 = (bf16[343,400]{1,0:T(8,128)(2,1)S(1)}, bf16[343,400]{1,0:T(8,128)(2,1)}, u32[]{:S(2)}) copy-start(bf16[343,400]{1,0:T(8,128)(2,1)} %constant.13.clone.refs_2_) | copy-start | bytes 823204
  11.1 2.4 %copy-start.2 = (bf16[400,343]{1,0:T(8,128)(2,1)S(1)}, bf16[400,343]{1,0:T(8,128)(2,1)}, u32[]{:S(2)}) copy-start(bf16[400,343]{1,0:T(8,128)(2,1)} %constant.12.clone.refs_1_) | copy-start | bytes 823204
  11.1 2.4 %copy-start.3 = (bf16[343,64]{1,0:T(8,128)(2,1)S(1)}, bf16[343,64]{1,0:T(8,128)(2,1)}, u32[]{:S(2)}) copy-start(bf16[343,64]{1,0:T(8,128)(2,1)} %constant.14.clone.refs_3_) | copy-start | bytes 131716
  11.1 2.4 %copy-start.4 = (f32[6,6,24]{2,1,0:T(8,128)S(1)}, f32[6,6,24]{2,1,0:T(8,128)}, u32[]{:S(2)}) copy-start(f32[6,6,24]{2,1,0:T(8,128)} %refs_4_.1) | copy-start | bytes 10372
  11.1 4.6 %copy-start.6 = (f32[6,6,24,256]{3,2,1,0:T(8,128)S(1)}, f32[6,6,24,256]{3,2,1,0:T(8,128)}, u32[]{:S(2)}) copy-start(f32[6,6,24,256]{3,2,1,0:T(8,128)} %param.9) | copy-start | bytes 2654212
  11.2 4.5 %collective-permute-start.2 = (f32[48,128]{1,0:T(8,128)S(1)}, f32[48,128]{1,0:T(8,128)S(1)}, u32[]{:S(2)}, u32[]{:S(2)}) collective-permute-start(f32[48,128]{1,0:T(8,128)S(1)} %get-tuple-element.60), channel_id=1, source_target_pairs={{0,252},{4,240},{8,244},{12,248},{16,12},{20,0},{24,4},{28,8},{32,... | collective-permute-start | bytes 73736 | tf_op jit(solution)/shard_map/ppermute | solution.py:387
  15.7 7.8 %copy-start.5 = (f32[1024,256]{1,0:T(8,128)S(1)}, f32[1024,256]{1,0:T(8,128)}, u32[]{:S(2)}) copy-start(f32[1024,256]{1,0:T(8,128)} %refs_1_.2) | copy-start | bytes 3145732
  17.9 11.7 %collective-permute-start.3 = (f32[336,128]{1,0:T(8,128)S(1)}, f32[336,128]{1,0:T(8,128)S(1)}, u32[]{:S(2)}, u32[]{:S(2)}) collective-permute-start(f32[336,128]{1,0:T(8,128)S(1)} %get-tuple-element.67), channel_id=1, source_target_pairs={{0,4},{4,8},{8,12},{12,0},{1,5},{5,9},{9,13},{13,1},{2,6},{6,10},{... | collective-permute-start | bytes 516104 | tf_op jit(solution)/shard_map/ppermute | solution.py:377
  18.0 11.6 %collective-permute-start.4 = (f32[336,128]{1,0:T(8,128)S(1)}, f32[336,128]{1,0:T(8,128)S(1)}, u32[]{:S(2)}, u32[]{:S(2)}) collective-permute-start(f32[336,128]{1,0:T(8,128)S(1)} %get-tuple-element.68), channel_id=1, source_target_pairs={{0,12},{4,0},{8,4},{12,8},{1,13},{5,1},{9,5},{13,9},{2,14},{6,2},{... | collective-permute-start | bytes 516104 | tf_op jit(solution)/shard_map/ppermute | solution.py:377
  18.5 8.4 %collective-permute-start.5 = (f32[336,128]{1,0:T(8,128)S(1)}, f32[336,128]{1,0:T(8,128)S(1)}, u32[]{:S(2)}, u32[]{:S(2)}) collective-permute-start(f32[336,128]{1,0:T(8,128)S(1)} %get-tuple-element.69), channel_id=1, source_target_pairs={{0,16},{16,32},{32,48},{48,64},{64,80},{80,96},{96,112},{112,128},... | collective-permute-start | bytes 516104 | tf_op jit(solution)/shard_map/ppermute | solution.py:377
  19.9 6.9 %collective-permute-start.6 = (f32[336,128]{1,0:T(8,128)S(1)}, f32[336,128]{1,0:T(8,128)S(1)}, u32[]{:S(2)}, u32[]{:S(2)}) collective-permute-start(f32[336,128]{1,0:T(8,128)S(1)} %get-tuple-element.70), channel_id=1, source_target_pairs={{0,240},{16,0},{32,16},{48,32},{64,48},{80,64},{96,80},{112,96},{1... | collective-permute-start | bytes 516104 | tf_op jit(solution)/shard_map/ppermute | solution.py:377
  26.8 4.8 %collective-permute-start.7 = (f32[96,128]{1,0:T(8,128)S(1)}, f32[96,128]{1,0:T(8,128)S(1)}, u32[]{:S(2)}, u32[]{:S(2)}) collective-permute-start(f32[96,128]{1,0:T(8,128)S(1)} %get-tuple-element.75), channel_id=1, source_target_pairs={{0,4},{4,8},{8,12},{12,0},{1,5},{5,9},{9,13},{13,1},{2,6},{6,10},{... | collective-permute-start | bytes 147464 | tf_op jit(solution)/shard_map/ppermute | solution.py:377
  29.6 3.5 %collective-permute-start.8 = (f32[96,128]{1,0:T(8,128)S(1)}, f32[96,128]{1,0:T(8,128)S(1)}, u32[]{:S(2)}, u32[]{:S(2)}) collective-permute-start(f32[96,128]{1,0:T(8,128)S(1)} %get-tuple-element.76), channel_id=1, source_target_pairs={{0,12},{4,0},{8,4},{12,8},{1,13},{5,1},{9,5},{13,9},{2,14},{6,2},{... | collective-permute-start | bytes 147464 | tf_op jit(solution)/shard_map/ppermute | solution.py:377
  34.5 16.3 %collective-permute-start.15 = (f32[1200,128]{1,0:T(8,128)S(1)}, f32[1200,128]{1,0:T(8,128)S(1)}, u32[]{:S(2)}, u32[]{:S(2)}) collective-permute-start(f32[1200,128]{1,0:T(8,128)S(1)} %get-tuple-element.92.refs_0_), channel_id=1, source_target_pairs={{0,3},{1,0},{2,1},{3,2},{4,7},{5,4},{6,5},{7,6},{8,11},{9,8},{10,9... | collective-permute-start | bytes 1843208 | tf_op jit(solution)/shard_map/ppermute | solution.py:377
  37.3 16.7 %collective-permute-start.14 = (f32[1200,128]{1,0:T(8,128)S(1)}, f32[1200,128]{1,0:T(8,128)S(1)}, u32[]{:S(2)}, u32[]{:S(2)}) collective-permute-start(f32[1200,128]{1,0:T(8,128)S(1)} %get-tuple-element.92.refs_0_), channel_id=1, source_target_pairs={{0,1},{1,2},{2,3},{3,0},{4,5},{5,6},{6,7},{7,4},{8,9},{9,10},{10,1... | collective-permute-start | bytes 1843208 | tf_op jit(solution)/shard_map/ppermute | solution.py:377
  37.3 10.2 %collective-permute-start.9 = (f32[288,128]{1,0:T(8,128)S(1)}, f32[288,128]{1,0:T(8,128)S(1)}, u32[]{:S(2)}, u32[]{:S(2)}) collective-permute-start(f32[288,128]{1,0:T(8,128)S(1)} %get-tuple-element.85), channel_id=1, source_target_pairs={{0,16},{16,32},{32,48},{48,64},{64,80},{80,96},{96,112},{112,128},... | collective-permute-start | bytes 442376 | tf_op jit(solution)/shard_map/ppermute | solution.py:377
  37.3 10.2 %collective-permute-start.10 = (f32[288,128]{1,0:T(8,128)S(1)}, f32[288,128]{1,0:T(8,128)S(1)}, u32[]{:S(2)}, u32[]{:S(2)}) collective-permute-start(f32[288,128]{1,0:T(8,128)S(1)} %get-tuple-element.86), channel_id=1, source_target_pairs={{0,4},{4,8},{8,12},{12,0},{1,5},{5,9},{9,13},{13,1},{2,6},{6,10},{... | collective-permute-start | bytes 442376 | tf_op jit(solution)/shard_map/ppermute | solution.py:377
  37.9 9.6 %collective-permute-start.11 = (f32[48,128]{1,0:T(8,128)S(1)}, f32[48,128]{1,0:T(8,128)S(1)}, u32[]{:S(2)}, u32[]{:S(2)}) collective-permute-start(f32[48,128]{1,0:T(8,128)S(1)} %get-tuple-element.87), channel_id=1, source_target_pairs={{0,20},{4,24},{8,28},{12,16},{16,36},{20,40},{24,44},{28,32},{32,5... | collective-permute-start | bytes 73736 | tf_op jit(solution)/shard_map/ppermute | solution.py:387
  47.5 10.2 %collective-permute-start.13 = (f32[528,128]{1,0:T(8,128)S(1)}, f32[528,128]{1,0:T(8,128)S(1)}, u32[]{:S(2)}, u32[]{:S(2)}) collective-permute-start(f32[528,128]{1,0:T(8,128)S(1)} %get-tuple-element.89.refs_0_), channel_id=1, source_target_pairs={{0,3},{1,0},{2,1},{3,2},{4,7},{5,4},{6,5},{7,6},{8,11},{9,8},{10,9... | collective-permute-start | bytes 811016 | tf_op jit(solution)/shard_map/ppermute | solution.py:377
  50.4 8.6 %collective-permute-start.12 = (f32[528,128]{1,0:T(8,128)S(1)}, f32[528,128]{1,0:T(8,128)S(1)}, u32[]{:S(2)}, u32[]{:S(2)}) collective-permute-start(f32[528,128]{1,0:T(8,128)S(1)} %get-tuple-element.89.refs_0_), channel_id=1, source_target_pairs={{0,1},{1,2},{2,3},{3,0},{4,5},{5,6},{6,7},{7,4},{8,9},{9,10},{10,1... | collective-permute-start | bytes 811016 | tf_op jit(solution)/shard_map/ppermute | solution.py:377
  54.1 11.6 %collective-permute-start.16 = (f32[600,128]{1,0:T(8,128)S(1)}, f32[600,128]{1,0:T(8,128)S(1)}, u32[]{:S(2)}, u32[]{:S(2)}) collective-permute-start(f32[600,128]{1,0:T(8,128)S(1)} %get-tuple-element.96), channel_id=1, source_target_pairs={{0,1},{1,2},{2,3},{3,0},{4,5},{5,6},{6,7},{7,4},{8,9},{9,10},{10,1... | collective-permute-start | bytes 921608 | tf_op jit(solution)/shard_map/ppermute | solution.py:377
  54.2 11.5 %collective-permute-start.17 = (f32[600,128]{1,0:T(8,128)S(1)}, f32[600,128]{1,0:T(8,128)S(1)}, u32[]{:S(2)}, u32[]{:S(2)}) collective-permute-start(f32[600,128]{1,0:T(8,128)S(1)} %get-tuple-element.97), channel_id=1, source_target_pairs={{0,3},{1,0},{2,1},{3,2},{4,7},{5,4},{6,5},{7,6},{8,11},{9,8},{10,9... | collective-permute-start | bytes 921608 | tf_op jit(solution)/shard_map/ppermute | solution.py:377
  59.1 9.5 %collective-permute-start.18 = (f32[264,128]{1,0:T(8,128)S(1)}, f32[264,128]{1,0:T(8,128)S(1)}, u32[]{:S(2)}, u32[]{:S(2)}) collective-permute-start(f32[264,128]{1,0:T(8,128)S(1)} %get-tuple-element.104), channel_id=1, source_target_pairs={{0,1},{1,2},{2,3},{3,0},{4,5},{5,6},{6,7},{7,4},{8,9},{9,10},{10,1... | collective-permute-start | bytes 405512 | tf_op jit(solution)/shard_map/ppermute | solution.py:377
  59.2 9.4 %collective-permute-start.19 = (f32[264,128]{1,0:T(8,128)S(1)}, f32[264,128]{1,0:T(8,128)S(1)}, u32[]{:S(2)}, u32[]{:S(2)}) collective-permute-start(f32[264,128]{1,0:T(8,128)S(1)} %get-tuple-element.105), channel_id=1, source_target_pairs={{0,3},{1,0},{2,1},{3,2},{4,7},{5,4},{6,5},{7,6},{8,11},{9,8},{10,9... | collective-permute-start | bytes 405512 | tf_op jit(solution)/shard_map/ppermute | solution.py:377

commit v6 on v5

--- a/solution.py
+++ b/solution.py
@@ -99,28 +99,27 @@
 
 
 def cell_kernel(
-    cell, chosen, chosen_t, corners_t, potential, center, halfwidth, k_high, k_low, c_high, c_low, local,
-    cell_ref, chosen_ref, chosen_t_ref, corners_t_ref, sems,
+    cell, chosen, chosen_t, potential, center, halfwidth, k_high, k_low, local, cell_ref, chosen_ref, chosen_t_ref, sems
 ):
-    pairs = ((cell, cell_ref), (chosen, chosen_ref), (chosen_t, chosen_t_ref), (corners_t, corners_t_ref))
+    pairs = ((cell, cell_ref), (chosen, chosen_ref), (chosen_t, chosen_t_ref))
     copies = [pltpu.make_async_copy(source, target, sems.at[index]) for index, (source, target) in enumerate(pairs)]
     for copy in copies:
         copy.start()
-    scale = 1.0 / jnp.full((1, LANES), halfwidth[0], F32)
+    scale = 1.0 / jnp.broadcast_to(halfwidth[...], (1, LANES))
     local[...] = jnp.zeros_like(local)
     for x in range(6):
-        shifted = potential[x] - center[0]
+        shifted = potential[x] - center[...]
         for z in range(NZ):
             local[pl.ds(z * ROWS + x * 6, 6)] = shifted[:, z : z + 1] * scale
     for copy in copies:
         copy.wait()
-    for half, k_ref, c_ref in zip(split(cell_ref[...] * scale[:, 0:1]), (k_high, k_low), (c_high, c_low)):
-        rows = dot(chosen_ref[...], half).astype(BF16)
-        k_ref[...] = dot(rows, chosen_t_ref[...]).astype(BF16)
-        c_ref[...] = dot(rows, corners_t_ref[...]).astype(BF16)
-
-
-def rotation_kernel(me, rotation, r_high, r_low, far_high, far_low):
+    for half, k_ref in zip(split(cell_ref[...] * scale[:, 0:1]), (k_high, k_low)):
+        k_ref[...] = dot(dot(chosen_ref[...], half).astype(BF16), chosen_t_ref[...]).astype(BF16)
+
+
+def rotation_kernel(me, rotation, k_high, k_low, columns, r_high, r_low, far_high, far_low, c_high, c_low):
+    c_high[...] = dot(k_high[...], columns[...]).astype(BF16)
+    c_low[...] = dot(k_low[...], columns[...]).astype(BF16)
     for index, steps in enumerate((0, -1, 1, 2)):
         owner = lax.rem(me[0] + steps + 4, 4)
         high, low = split(rotation[pl.ds(pl.multiple_of(owner * 256, 256), 256)])
@@ -391,7 +390,7 @@
     run = Sequence()
     places = PLACES.items()
     chosen = selection(places, ROWS, KPAD)
-    corners_t = selection([(place, row) for row, place in enumerate(CORNERS)], CROWS, CPAD).T
+    columns = chosen @ selection([(place, row) for row, place in enumerate(CORNERS)], CROWS, CPAD).T
     me = lax.axis_index("band").astype(jnp.int32).reshape(1)
     held = [pltpu.VMEM((PARTS * OWNED, LANES), F32)]
     operator_scratch = [
@@ -433,28 +432,26 @@
     gx = passed_along(pull_x, "slab", -1)
     (pull_c,) = fenced("fence_c", pull_c)
     gc = passed_diagonal(pull_c, -1)
-    k_high, k_low, c_high, c_low, local = run(
+    k_high, k_low, local = run(
         call(
             cell_kernel,
             "cell",
-            [HB] * 4 + [VM] + [SM] * 2,
-            [((KPAD, KPAD), BF16)] * 2 + [((KPAD, CPAD), BF16)] * 2 + [((LAYER, LANES), F32)],
+            [HB] * 3 + [VM] * 3,
+            [((KPAD, KPAD), BF16)] * 2 + [((LAYER, LANES), F32)],
             [
                 pltpu.VMEM((SIDE**3, SIDE**3), F32),
                 pltpu.VMEM((KPAD, SIDE**3), BF16),
                 pltpu.VMEM((SIDE**3, KPAD), BF16),
-                pltpu.VMEM((SIDE**3, CPAD), BF16),
-                pltpu.SemaphoreType.DMA((4,)),
+                pltpu.SemaphoreType.DMA((3,)),
             ],
             flops=1,
         ),
         cell_matrix,
         jnp.asarray(chosen, BF16),
         jnp.asarray(chosen.T, BF16),
-        jnp.asarray(corners_t, BF16),
         potential,
-        center,
-        halfwidth,
+        center.reshape(1, 1),
+        halfwidth.reshape(1, 1),
     )
     p, f0, f6, s0, s6 = run(
         call(
@@ -470,11 +467,14 @@
     r6 = passed_along(f0, "face", -1)
     q0 = passed_along(s6, "slab", 1)
     q6 = passed_along(s0, "slab", -1)
-    r_high, r_low, far_high, far_low = run(
+    r_high, r_low, far_high, far_low, c_high, c_low = run(
         call(
-            rotation_kernel, "rotation", [SM, VM], [((768, 256), BF16)] * 2 + [((256, 256), BF16)] * 2
+            rotation_kernel,
+            "rotation",
+            [SM] + [VM] * 4,
+            [((768, 256), BF16)] * 2 + [((256, 256), BF16)] * 2 + [((KPAD, CPAD), BF16)] * 2,
         ),
-        me, rotation,
+        me, rotation, k_high, k_low, jnp.asarray(columns, BF16),
     )
     e0, e6 = run(call(cross_kernel, "cross", [VM] * 2, [both] * 2), q0, q6)
     d0 = passed_along(e6, "face", 1)

time: 69.9 us -> 69.6 us (level)
  no operation moved by 1% of the time
where the time goes in v6:
time: 69.6 us; the launch traced here: 69.5 us
  starting transfers between devices  31.1 us (45%)
  waiting for transfers between devices  23.6 us (34%)
  Pallas kernels  13 us (19%)
  between operations  1.72 us (2%)
    ppermute x18, starting transfers between devices, passed_along(): lax.ppermute(value, axis, [(s, (s + steps) % count) for s in range(count)])  30 us
    ppermute x18, waiting for transfers between devices, passed_along(): lax.ppermute(value, axis, [(s, (s + steps) % count) for s in range(count)])  14 us
    pallas_call x15, Pallas kernels, __call__(): *results, self.token = kernel(*operands, self.token)  11.8 us
    ppermute x2, waiting for transfers between devices, passed_diagonal(): return lax.ppermute(value, ('slab', 'face'), pairs)  9.61 us
  transfers between devices with their start and end apart: 20, of which 8 were waited for; matrix products, arithmetic and copies ran while one was open for 0% of the time, Pallas kernels for 10%

profile of v6, /device:TPU:1, one launch (start us, length us, event | category | flops | bytes accessed | tf_op | source)
XLA Modules:
  0.0 69.5 jit_solution(4532702335180043462)
XLA Ops:
  0.0 1.2 %pulls.1 = (f32[288,128]{1,0:T(8,128)S(1)}, f32[288,128]{1,0:T(8,128)S(1)}, f32[48,128]{1,0:T(8,128)S(1)}) custom-call(f32[864,256]{1,0:T(8,128)} %bitcast.7), custom_call_target="tpu_custom_call" | custom-call | flops 10000000000 | bytes 1 | tf_op jit(solution)/shard_map/pulls/pallas_call | solution.py:422
  1.2 8.9 %collective-permute-start = (f32[288,128]{1,0:T(8,128)S(1)}, f32[288,128]{1,0:T(8,128)S(1)}, u32[]{:S(2)}, u32[]{:S(2)}) collective-permute-start(f32[288,128]{1,0:T(8,128)S(1)} %get-tuple-element.57), channel_id=1, source_target_pairs={{0,240},{16,0},{32,16},{48,32},{64,48},{80,64},{96,80},{112,96},{1... | collective-permute-start | bytes 442376 | tf_op jit(solution)/shard_map/ppermute | solution.py:376
  10.1 1.0 %collective-permute-start.1 = (f32[288,128]{1,0:T(8,128)S(1)}, f32[288,128]{1,0:T(8,128)S(1)}, u32[]{:S(2)}, u32[]{:S(2)}) collective-permute-start(f32[288,128]{1,0:T(8,128)S(1)} %get-tuple-element.58), channel_id=1, source_target_pairs={{0,12},{4,0},{8,4},{12,8},{1,13},{5,1},{9,5},{13,9},{2,14},{6,2},{... | collective-permute-start | bytes 442376 | tf_op jit(solution)/shard_map/ppermute | solution.py:376
  11.1 0.0 copy-start.3
  11.1 0.0 copy-start.5
  11.1 1.0 %collective-permute-start.2 = (f32[48,128]{1,0:T(8,128)S(1)}, f32[48,128]{1,0:T(8,128)S(1)}, u32[]{:S(2)}, u32[]{:S(2)}) collective-permute-start(f32[48,128]{1,0:T(8,128)S(1)} %get-tuple-element.60), channel_id=1, source_target_pairs={{0,252},{4,240},{8,244},{12,248},{16,12},{20,0},{24,4},{28,8},{32,... | collective-permute-start | bytes 73736 | tf_op jit(solution)/shard_map/ppermute | solution.py:386
  13.5 1.9 %cell.1 = (bf16[400,400]{1,0:T(8,128)(2,1)S(1)}, bf16[400,400]{1,0:T(8,128)(2,1)S(1)}, f32[1344,128]{1,0:T(8,128)S(1)}, f32[8,128]{1,0:T(8,128)S(1)}) custom-call(f32[343,343]{1,0:T(8,128)S(1)} %copy-done, bf16[400,343]{1,0:T(8,128)(2,1)S(1)} %copy-done.2, bf16[343,400]{1,0:T(8,128)(2,1)S(1)} %copy-done.1, ...), custom_call_target="tpu_custom_call", output_to_operand_aliasing={{3}: (6, {})} | custom-call | flops 1 | bytes 1 | tf_op jit(solution)/shard_map/cell/pallas_call | solution.py:366
  15.4 0.0 collective-permute-done.2.refs_3_
  15.4 0.0 collective-permute-done.refs_1_
  15.5 0.0 copy-start.4
  15.5 0.0 copy-start.6
  15.5 2.1 %first.1 = (f32[2,1344,128]{2,1,0:T(8,128)S(1)}, f32[336,128]{1,0:T(8,128)S(1)}, f32[336,128]{1,0:T(8,128)S(1)}, f32[336,128]{1,0:T(8,128)S(1)}, f32[336,128]{1,0:T(8,128)S(1)}, /*index=5*/f32[8,128]{1,0:T(8,128)S(1)}) custom-call(f32[864,256]{1,0:T(8,128)S(1)} %bitcast.8, ...), custom_call_target="tpu_custom_call", output_to_operand_aliasing={{5}: (7, {})} | custom-call | flops 10000000000 | bytes 1 | tf_op jit(solution)/shard_map/first/pallas_call | solution.py:366
  17.6 0.1 collective-permute-start.3
  17.7 0.5 collective-permute-start.4
  18.2 1.5 %collective-permute-start.5 = (f32[336,128]{1,0:T(8,128)S(1)}, f32[336,128]{1,0:T(8,128)S(1)}, u32[]{:S(2)}, u32[]{:S(2)}) collective-permute-start(f32[336,128]{1,0:T(8,128)S(1)} %get-tuple-element.69), channel_id=1, source_target_pairs={{0,16},{16,32},{32,48},{48,64},{64,80},{80,96},{96,112},{112,128},... | collective-permute-start | bytes 516104 | tf_op jit(solution)/shard_map/ppermute | solution.py:376
  19.7 3.7 %collective-permute-start.6 = (f32[336,128]{1,0:T(8,128)S(1)}, f32[336,128]{1,0:T(8,128)S(1)}, u32[]{:S(2)}, u32[]{:S(2)}) collective-permute-start(f32[336,128]{1,0:T(8,128)S(1)} %get-tuple-element.70), channel_id=1, source_target_pairs={{0,240},{16,0},{32,16},{48,32},{64,48},{80,64},{96,80},{112,96},{1... | collective-permute-start | bytes 516104 | tf_op jit(solution)/shard_map/ppermute | solution.py:376
  23.4 0.5 rotation.1
  23.9 2.8 %collective-permute-done.5.refs_0_.refs_3_ = f32[336,128]{1,0:T(8,128)S(1)} collective-permute-done((f32[336,128]{1,0:T(8,128)S(1)}, f32[336,128]{1,0:T(8,128)S(1)}, u32[]{:S(2)}, u32[]{:S(2)}) %collective-permute-start.5) | collective-permute-done | bytes 172064 | tf_op jit(solution)/shard_map/ppermute | solution.py:376
  26.7 0.0 collective-permute-done.6.refs_1_.refs_4_
  26.7 2.6 %collective-permute-start.7 = (f32[96,128]{1,0:T(8,128)S(1)}, f32[96,128]{1,0:T(8,128)S(1)}, u32[]{:S(2)}, u32[]{:S(2)}) collective-permute-start(f32[96,128]{1,0:T(8,128)S(1)} %get-tuple-element.75), channel_id=1, source_target_pairs={{0,4},{4,8},{8,12},{12,0},{1,5},{5,9},{9,13},{13,1},{2,6},{6,10},{... | collective-permute-start | bytes 147464 | tf_op jit(solution)/shard_map/ppermute | solution.py:376
  29.3 0.0 collective-permute-start.8
  29.3 0.0 collective-permute-done.3.refs_1_
  29.3 0.0 collective-permute-done.4.refs_2_
  29.3 2.1 %second.1 = (f32[2,1344,128]{2,1,0:T(8,128)S(1)}, f32[8,128]{1,0:T(8,128)S(1)}) custom-call(f32[2,1344,128]{2,1,0:T(8,128)S(1)} %get-tuple-element.66.refs_0_, f32[336,128]{1,0:T(8,128)S(1)} %collective-permute-done.3.refs_1_, f32[336,128]{1,0:T(8,128)S(1)} %collective-permute-done.4.refs_2_, ...), custom_call_target="tpu_custom_call", output_to_operand_aliasing={{1}: (8, {})} | custom-call | flops 10000000000 | bytes 1 | tf_op jit(solution)/shard_map/second/pallas_call | solution.py:366
  31.4 1.4 %collective-permute-done.8.refs_2_ = f32[96,128]{1,0:T(8,128)S(1)} collective-permute-done((f32[96,128]{1,0:T(8,128)S(1)}, f32[96,128]{1,0:T(8,128)S(1)}, u32[]{:S(2)}, u32[]{:S(2)}) %collective-permute-start.8) | collective-permute-done | bytes 49184 | tf_op jit(solution)/shard_map/ppermute | solution.py:376
  32.8 1.4 %third.1 = (f32[528,128]{1,0:T(8,128)S(1)}, f32[1200,128]{1,0:T(8,128)S(1)}, f32[288,128]{1,0:T(8,128)S(1)}, f32[288,128]{1,0:T(8,128)S(1)}, f32[48,128]{1,0:T(8,128)S(1)}, /*index=5*/f32[8,128]{1,0:T(8,128)S(1)}) custom-call(f32[2,1344,128]{2,1,0:T(8,128)S(1)} %get-tuple-element.74.refs_0_, ...), custom_call_target="tpu_custom_call", output_to_operand_aliasing={{5}: (7, {})} | custom-call | flops 10000000000 | bytes 1 | tf_op jit(solution)/shard_map/third/pallas_call | solution.py:366
  34.2 2.8 %collective-permute-start.15 = (f32[1200,128]{1,0:T(8,128)S(1)}, f32[1200,128]{1,0:T(8,128)S(1)}, u32[]{:S(2)}, u32[]{:S(2)}) collective-permute-start(f32[1200,128]{1,0:T(8,128)S(1)} %get-tuple-element.92.refs_0_), channel_id=1, source_target_pairs={{0,3},{1,0},{2,1},{3,2},{4,7},{5,4},{6,5},{7,6},{8,11},{9,8},{10,9... | collective-permute-start | bytes 1843208 | tf_op jit(solution)/shard_map/ppermute | solution.py:376
  37.1 0.0 collective-permute-start.14
  37.1 0.6 collective-permute-start.10
  37.7 0.0 collective-permute-start.11
  37.7 9.6 %collective-permute-done.11.refs_3_ = f32[48,128]{1,0:T(8,128)S(1)} collective-permute-done((f32[48,128]{1,0:T(8,128)S(1)}, f32[48,128]{1,0:T(8,128)S(1)}, u32[]{:S(2)}, u32[]{:S(2)}) %collective-permute-start.11) | collective-permute-done | bytes 24608 | tf_op jit(solution)/shard_map/ppermute | solution.py:386
  47.3 0.0 collective-permute-done.9.refs_1_
  47.3 0.0 collective-permute-done.10.refs_2_
  47.4 2.8 %collective-permute-start.13 = (f32[528,128]{1,0:T(8,128)S(1)}, f32[528,128]{1,0:T(8,128)S(1)}, u32[]{:S(2)}, u32[]{:S(2)}) collective-permute-start(f32[528,128]{1,0:T(8,128)S(1)} %get-tuple-element.89.refs_0_), channel_id=1, source_target_pairs={{0,3},{1,0},{2,1},{3,2},{4,7},{5,4},{6,5},{7,6},{8,11},{9,8},{10,9... | collective-permute-start | bytes 811016 | tf_op jit(solution)/shard_map/ppermute | solution.py:376
  50.2 0.3 collective-permute-done.15.refs_1_.refs_2_
  50.5 3.2 %collective-permute-done.14.refs_0_.refs_1_ = f32[1200,128]{1,0:T(8,128)S(1)} collective-permute-done((f32[1200,128]{1,0:T(8,128)S(1)}, f32[1200,128]{1,0:T(8,128)S(1)}, u32[]{:S(2)}, u32[]{:S(2)}) %collective-permute-start.14) | collective-permute-done | bytes 614432 | tf_op jit(solution)/shard_map/ppermute | solution.py:376
  53.7 0.1 collective-permute-start.16
  53.8 2.7 %collective-permute-start.17 = (f32[600,128]{1,0:T(8,128)S(1)}, f32[600,128]{1,0:T(8,128)S(1)}, u32[]{:S(2)}, u32[]{:S(2)}) collective-permute-start(f32[600,128]{1,0:T(8,128)S(1)} %get-tuple-element.97), channel_id=1, source_target_pairs={{0,3},{1,0},{2,1},{3,2},{4,7},{5,4},{6,5},{7,6},{8,11},{9,8},{10,9... | collective-permute-start | bytes 921608 | tf_op jit(solution)/shard_map/ppermute | solution.py:376
  56.5 0.9 %near2.1 = (f32[600,256]{1,0:T(8,128)S(1)}, f32[8,128]{1,0:T(8,128)S(1)}) custom-call(f32[1200,128]{1,0:T(8,128)S(1)} %get-tuple-element.92.refs_0_, f32[1200,128]{1,0:T(8,128)S(1)} %collective-permute-done.14.refs_0_.refs_1_, f32[1200,128]{1,0:T(8,128)S(1)} %collective-permute-done.15.refs_1_.refs_2_, ...), custom_call_target="tpu_custom_call", output_to_operand_aliasing={{1}: (5, {})} | custom-call | flops 10000000000 | bytes 1 | tf_op jit(solution)/shard_map/near2/pallas_call | solution.py:366
  57.4 1.4 %collective-permute-done.12.refs_0_.refs_1_ = f32[528,128]{1,0:T(8,128)S(1)} collective-permute-done((f32[528,128]{1,0:T(8,128)S(1)}, f32[528,128]{1,0:T(8,128)S(1)}, u32[]{:S(2)}, u32[]{:S(2)}) %collective-permute-start.12) | collective-permute-done | bytes 270368 | tf_op jit(solution)/shard_map/ppermute | solution.py:376
  58.8 0.1 collective-permute-start.18
  58.9 2.7 %collective-permute-start.19 = (f32[264,128]{1,0:T(8,128)S(1)}, f32[264,128]{1,0:T(8,128)S(1)}, u32[]{:S(2)}, u32[]{:S(2)}) collective-permute-start(f32[264,128]{1,0:T(8,128)S(1)} %get-tuple-element.105), channel_id=1, source_target_pairs={{0,3},{1,0},{2,1},{3,2},{4,7},{5,4},{6,5},{7,6},{8,11},{9,8},{10,9... | collective-permute-start | bytes 405512 | tf_op jit(solution)/shard_map/ppermute | solution.py:376
  61.6 3.8 %collective-permute-done.16.refs_1_ = f32[600,128]{1,0:T(8,128)S(1)} collective-permute-done((f32[600,128]{1,0:T(8,128)S(1)}, f32[600,128]{1,0:T(8,128)S(1)}, u32[]{:S(2)}, u32[]{:S(2)}) %collective-permute-start.16) | collective-permute-done | bytes 307232 | tf_op jit(solution)/shard_map/ppermute | solution.py:376
  65.4 0.0 collective-permute-done.17.refs_2_
  65.4 1.3 %far2.1 = (f32[864,256]{1,0:T(8,128)}, f32[8,128]{1,0:T(8,128)S(1)}) custom-call(f32[600,256]{1,0:T(8,128)S(1)} %get-tuple-element.95.refs_0_, f32[600,128]{1,0:T(8,128)S(1)} %collective-permute-done.16.refs_1_, f32[600,128]{1,0:T(8,128)S(1)} %collective-permute-done.17.refs_2_, ...), custom_call_target="tpu_custom_call", output_to_operand_aliasing={{1}: (5, {})} | custom-call | flops 10000000000 | bytes 1 | tf_op jit(solution)/shard_map/far2/pallas_call | solution.py:366
  66.7 0.5 near1.1
  67.2 1.1 %collective-permute-done.18.refs_1_ = f32[264,128]{1,0:T(8,128)S(1)} collective-permute-done((f32[264,128]{1,0:T(8,128)S(1)}, f32[264,128]{1,0:T(8,128)S(1)}, u32[]{:S(2)}, u32[]{:S(2)}) %collective-permute-start.18) | collective-permute-done | bytes 135200 | tf_op jit(solution)/shard_map/ppermute | solution.py:376
  68.3 1.0 %last.1 = (f32[864,256]{1,0:T(8,128)}, f32[8,128]{1,0:T(8,128)S(1)}) custom-call(f32[264,256]{1,0:T(8,128)S(1)} %get-tuple-element.103.refs_0_, f32[264,128]{1,0:T(8,128)S(1)} %collective-permute-done.18.refs_1_, f32[264,128]{1,0:T(8,128)S(1)} %collective-permute-done.19.refs_2_, ...), custom_call_target="tpu_custom_call", output_to_operand_aliasing={{1}: (6, {}), {0}: (5, {})} | custom-call | flops 10000000000 | bytes 1 | tf_op jit(solution)/shard_map/last/pallas_call | solution.py:366
  (23 shorter events, 0.1 us)
Async XLA Ops:
  1.2 14.2 %collective-permute-start = (f32[288,128]{1,0:T(8,128)S(1)}, f32[288,128]{1,0:T(8,128)S(1)}, u32[]{:S(2)}, u32[]{:S(2)}) collective-permute-start(f32[288,128]{1,0:T(8,128)S(1)} %get-tuple-element.57), channel_id=1, source_target_pairs={{0,240},{16,0},{32,16},{48,32},{64,48},{80,64},{96,80},{112,96},{1... | collective-permute-start | bytes 442376 | tf_op jit(solution)/shard_map/ppermute | solution.py:376
  10.1 5.3 %collective-permute-start.1 = (f32[288,128]{1,0:T(8,128)S(1)}, f32[288,128]{1,0:T(8,128)S(1)}, u32[]{:S(2)}, u32[]{:S(2)}) collective-permute-start(f32[288,128]{1,0:T(8,128)S(1)} %get-tuple-element.58), channel_id=1, source_target_pairs={{0,12},{4,0},{8,4},{12,8},{1,13},{5,1},{9,5},{13,9},{2,14},{6,2},{... | collective-permute-start | bytes 442376 | tf_op jit(solution)/shard_map/ppermute | solution.py:376
  11.1 2.4 %copy-start = (f32[343,343]{1,0:T(8,128)S(1)}, f32[343,343]{1,0:T(8,128)}, u32[]{:S(2)}) copy-start(f32[343,343]{1,0:T(8,128)} %refs_0_.1) | copy-start | bytes 1411792
  11.1 2.4 %copy-start.1 = (bf16[343,400]{1,0:T(8,128)(2,1)S(1)}, bf16[343,400]{1,0:T(8,128)(2,1)}, u32[]{:S(2)}) copy-start(bf16[343,400]{1,0:T(8,128)(2,1)} %constant.13.clone.refs_2_) | copy-start | bytes 823204
  11.1 2.4 %copy-start.2 = (bf16[400,343]{1,0:T(8,128)(2,1)S(1)}, bf16[400,343]{1,0:T(8,128)(2,1)}, u32[]{:S(2)}) copy-start(bf16[400,343]{1,0:T(8,128)(2,1)} %constant.12.clone.refs_1_) | copy-start | bytes 823204
  11.1 2.4 %copy-start.3 = (f32[6,6,24]{2,1,0:T(8,128)S(1)}, f32[6,6,24]{2,1,0:T(8,128)}, u32[]{:S(2)}) copy-start(f32[6,6,24]{2,1,0:T(8,128)} %refs_3_.1) | copy-start | bytes 10372
  11.1 4.3 %copy-start.5 = (f32[6,6,24,256]{3,2,1,0:T(8,128)S(1)}, f32[6,6,24,256]{3,2,1,0:T(8,128)}, u32[]{:S(2)}) copy-start(f32[6,6,24,256]{3,2,1,0:T(8,128)} %param.9) | copy-start | bytes 2654212
  11.1 4.3 %collective-permute-start.2 = (f32[48,128]{1,0:T(8,128)S(1)}, f32[48,128]{1,0:T(8,128)S(1)}, u32[]{:S(2)}, u32[]{:S(2)}) collective-permute-start(f32[48,128]{1,0:T(8,128)S(1)} %get-tuple-element.60), channel_id=1, source_target_pairs={{0,252},{4,240},{8,244},{12,248},{16,12},{20,0},{24,4},{28,8},{32,... | collective-permute-start | bytes 73736 | tf_op jit(solution)/shard_map/ppermute | solution.py:386
  15.5 7.9 %copy-start.4 = (f32[1024,256]{1,0:T(8,128)S(1)}, f32[1024,256]{1,0:T(8,128)}, u32[]{:S(2)}) copy-start(f32[1024,256]{1,0:T(8,128)} %refs_1_.2) | copy-start | bytes 3145732
  15.5 7.9 %copy-start.6 = (bf16[400,64]{1,0:T(8,128)(2,1)S(1)}, bf16[400,64]{1,0:T(8,128)(2,1)}, u32[]{:S(2)}) copy-start(bf16[400,64]{1,0:T(8,128)(2,1)} %constant.14.clone.refs_4_) | copy-start | bytes 153604
  17.6 11.7 %collective-permute-start.3 = (f32[336,128]{1,0:T(8,128)S(1)}, f32[336,128]{1,0:T(8,128)S(1)}, u32[]{:S(2)}, u32[]{:S(2)}) collective-permute-start(f32[336,128]{1,0:T(8,128)S(1)} %get-tuple-element.67), channel_id=1, source_target_pairs={{0,4},{4,8},{8,12},{12,0},{1,5},{5,9},{9,13},{13,1},{2,6},{6,10},{... | collective-permute-start | bytes 516104 | tf_op jit(solution)/shard_map/ppermute | solution.py:376
  17.7 11.6 %collective-permute-start.4 = (f32[336,128]{1,0:T(8,128)S(1)}, f32[336,128]{1,0:T(8,128)S(1)}, u32[]{:S(2)}, u32[]{:S(2)}) collective-permute-start(f32[336,128]{1,0:T(8,128)S(1)} %get-tuple-element.68), channel_id=1, source_target_pairs={{0,12},{4,0},{8,4},{12,8},{1,13},{5,1},{9,5},{13,9},{2,14},{6,2},{... | collective-permute-start | bytes 516104 | tf_op jit(solution)/shard_map/ppermute | solution.py:376
  18.2 8.5 %collective-permute-start.5 = (f32[336,128]{1,0:T(8,128)S(1)}, f32[336,128]{1,0:T(8,128)S(1)}, u32[]{:S(2)}, u32[]{:S(2)}) collective-permute-start(f32[336,128]{1,0:T(8,128)S(1)} %get-tuple-element.69), channel_id=1, source_target_pairs={{0,16},{16,32},{32,48},{48,64},{64,80},{80,96},{96,112},{112,128},... | collective-permute-start | bytes 516104 | tf_op jit(solution)/shard_map/ppermute | solution.py:376
  19.7 7.0 %collective-permute-start.6 = (f32[336,128]{1,0:T(8,128)S(1)}, f32[336,128]{1,0:T(8,128)S(1)}, u32[]{:S(2)}, u32[]{:S(2)}) collective-permute-start(f32[336,128]{1,0:T(8,128)S(1)} %get-tuple-element.70), channel_id=1, source_target_pairs={{0,240},{16,0},{32,16},{48,32},{64,48},{80,64},{96,80},{112,96},{1... | collective-permute-start | bytes 516104 | tf_op jit(solution)/shard_map/ppermute | solution.py:376
  26.7 4.7 %collective-permute-start.7 = (f32[96,128]{1,0:T(8,128)S(1)}, f32[96,128]{1,0:T(8,128)S(1)}, u32[]{:S(2)}, u32[]{:S(2)}) collective-permute-start(f32[96,128]{1,0:T(8,128)S(1)} %get-tuple-element.75), channel_id=1, source_target_pairs={{0,4},{4,8},{8,12},{12,0},{1,5},{5,9},{9,13},{13,1},{2,6},{6,10},{... | collective-permute-start | bytes 147464 | tf_op jit(solution)/shard_map/ppermute | solution.py:376
  29.3 3.5 %collective-permute-start.8 = (f32[96,128]{1,0:T(8,128)S(1)}, f32[96,128]{1,0:T(8,128)S(1)}, u32[]{:S(2)}, u32[]{:S(2)}) collective-permute-start(f32[96,128]{1,0:T(8,128)S(1)} %get-tuple-element.76), channel_id=1, source_target_pairs={{0,12},{4,0},{8,4},{12,8},{1,13},{5,1},{9,5},{13,9},{2,14},{6,2},{... | collective-permute-start | bytes 147464 | tf_op jit(solution)/shard_map/ppermute | solution.py:376
  34.2 16.2 %collective-permute-start.15 = (f32[1200,128]{1,0:T(8,128)S(1)}, f32[1200,128]{1,0:T(8,128)S(1)}, u32[]{:S(2)}, u32[]{:S(2)}) collective-permute-start(f32[1200,128]{1,0:T(8,128)S(1)} %get-tuple-element.92.refs_0_), channel_id=1, source_target_pairs={{0,3},{1,0},{2,1},{3,2},{4,7},{5,4},{6,5},{7,6},{8,11},{9,8},{10,9... | collective-permute-start | bytes 1843208 | tf_op jit(solution)/shard_map/ppermute | solution.py:376
  37.1 16.6 %collective-permute-start.14 = (f32[1200,128]{1,0:T(8,128)S(1)}, f32[1200,128]{1,0:T(8,128)S(1)}, u32[]{:S(2)}, u32[]{:S(2)}) collective-permute-start(f32[1200,128]{1,0:T(8,128)S(1)} %get-tuple-element.92.refs_0_), channel_id=1, source_target_pairs={{0,1},{1,2},{2,3},{3,0},{4,5},{5,6},{6,7},{7,4},{8,9},{9,10},{10,1... | collective-permute-start | bytes 1843208 | tf_op jit(solution)/shard_map/ppermute | solution.py:376
  37.1 10.2 %collective-permute-start.9 = (f32[288,128]{1,0:T(8,128)S(1)}, f32[288,128]{1,0:T(8,128)S(1)}, u32[]{:S(2)}, u32[]{:S(2)}) collective-permute-start(f32[288,128]{1,0:T(8,128)S(1)} %get-tuple-element.85), channel_id=1, source_target_pairs={{0,16},{16,32},{32,48},{48,64},{64,80},{80,96},{96,112},{112,128},... | collective-permute-start | bytes 442376 | tf_op jit(solution)/shard_map/ppermute | solution.py:376
  37.1 10.2 %collective-permute-start.10 = (f32[288,128]{1,0:T(8,128)S(1)}, f32[288,128]{1,0:T(8,128)S(1)}, u32[]{:S(2)}, u32[]{:S(2)}) collective-permute-start(f32[288,128]{1,0:T(8,128)S(1)} %get-tuple-element.86), channel_id=1, source_target_pairs={{0,4},{4,8},{8,12},{12,0},{1,5},{5,9},{9,13},{13,1},{2,6},{6,10},{... | collective-permute-start | bytes 442376 | tf_op jit(solution)/shard_map/ppermute | solution.py:376
  37.7 9.6 %collective-permute-start.11 = (f32[48,128]{1,0:T(8,128)S(1)}, f32[48,128]{1,0:T(8,128)S(1)}, u32[]{:S(2)}, u32[]{:S(2)}) collective-permute-start(f32[48,128]{1,0:T(8,128)S(1)} %get-tuple-element.87), channel_id=1, source_target_pairs={{0,20},{4,24},{8,28},{12,16},{16,36},{20,40},{24,44},{28,32},{32,5... | collective-permute-start | bytes 73736 | tf_op jit(solution)/shard_map/ppermute | solution.py:386
  47.4 10.1 %collective-permute-start.13 = (f32[528,128]{1,0:T(8,128)S(1)}, f32[528,128]{1,0:T(8,128)S(1)}, u32[]{:S(2)}, u32[]{:S(2)}) collective-permute-start(f32[528,128]{1,0:T(8,128)S(1)} %get-tuple-element.89.refs_0_), channel_id=1, source_target_pairs={{0,3},{1,0},{2,1},{3,2},{4,7},{5,4},{6,5},{7,6},{8,11},{9,8},{10,9... | collective-permute-start | bytes 811016 | tf_op jit(solution)/shard_map/ppermute | solution.py:376
  50.2 8.6 %collective-permute-start.12 = (f32[528,128]{1,0:T(8,128)S(1)}, f32[528,128]{1,0:T(8,128)S(1)}, u32[]{:S(2)}, u32[]{:S(2)}) collective-permute-start(f32[528,128]{1,0:T(8,128)S(1)} %get-tuple-element.89.refs_0_), channel_id=1, source_target_pairs={{0,1},{1,2},{2,3},{3,0},{4,5},{5,6},{6,7},{7,4},{8,9},{9,10},{10,1... | collective-permute-start | bytes 811016 | tf_op jit(solution)/shard_map/ppermute | solution.py:376
  53.7 11.6 %collective-permute-start.16 = (f32[600,128]{1,0:T(8,128)S(1)}, f32[600,128]{1,0:T(8,128)S(1)}, u32[]{:S(2)}, u32[]{:S(2)}) collective-permute-start(f32[600,128]{1,0:T(8,128)S(1)} %get-tuple-element.96), channel_id=1, source_target_pairs={{0,1},{1,2},{2,3},{3,0},{4,5},{5,6},{6,7},{7,4},{8,9},{9,10},{10,1... | collective-permute-start | bytes 921608 | tf_op jit(solution)/shard_map/ppermute | solution.py:376
  53.8 11.6 %collective-permute-start.17 = (f32[600,128]{1,0:T(8,128)S(1)}, f32[600,128]{1,0:T(8,128)S(1)}, u32[]{:S(2)}, u32[]{:S(2)}) collective-permute-start(f32[600,128]{1,0:T(8,128)S(1)} %get-tuple-element.97), channel_id=1, source_target_pairs={{0,3},{1,0},{2,1},{3,2},{4,7},{5,4},{6,5},{7,6},{8,11},{9,8},{10,9... | collective-permute-start | bytes 921608 | tf_op jit(solution)/shard_map/ppermute | solution.py:376
  58.8 9.5 %collective-permute-start.18 = (f32[264,128]{1,0:T(8,128)S(1)}, f32[264,128]{1,0:T(8,128)S(1)}, u32[]{:S(2)}, u32[]{:S(2)}) collective-permute-start(f32[264,128]{1,0:T(8,128)S(1)} %get-tuple-element.104), channel_id=1, source_target_pairs={{0,1},{1,2},{2,3},{3,0},{4,5},{5,6},{6,7},{7,4},{8,9},{9,10},{10,1... | collective-permute-start | bytes 405512 | tf_op jit(solution)/shard_map/ppermute | solution.py:376
  58.9 9.4 %collective-permute-start.19 = (f32[264,128]{1,0:T(8,128)S(1)}, f32[264,128]{1,0:T(8,128)S(1)}, u32[]{:S(2)}, u32[]{:S(2)}) collective-permute-start(f32[264,128]{1,0:T(8,128)S(1)} %get-tuple-element.105), channel_id=1, source_target_pairs={{0,3},{1,0},{2,1},{3,2},{4,7},{5,4},{6,5},{7,6},{8,11},{9,8},{10,9... | collective-permute-start | bytes 405512 | tf_op jit(solution)/shard_map/ppermute | solution.py:376

commit v7 on v6

--- a/solution.py
+++ b/solution.py
@@ -117,9 +117,8 @@
         k_ref[...] = dot(dot(chosen_ref[...], half).astype(BF16), chosen_t_ref[...]).astype(BF16)
 
 
-def rotation_kernel(me, rotation, k_high, k_low, columns, r_high, r_low, far_high, far_low, c_high, c_low):
-    c_high[...] = dot(k_high[...], columns[...]).astype(BF16)
-    c_low[...] = dot(k_low[...], columns[...]).astype(BF16)
+def rotation_kernel(me, rotation, k_high, k_low, columns_high, columns_low, r_high, r_low, far_high, far_low, c_terms):
+    c_terms[...] = (dot(k_high[...], columns_high[...]) + dot(k_low[...], columns_low[...])).astype(BF16)
     for index, steps in enumerate((0, -1, 1, 2)):
         owner = lax.rem(me[0] + steps + 4, 4)
         high, low = split(rotation[pl.ds(pl.multiple_of(owner * 256, 256), 256)])
@@ -271,13 +270,13 @@
 
 
 def third_kernel(
-    layers, d0, d6, w, c_high, c_low, local, set1, set2, push_x, push_y, push_c,
+    layers, d0, d6, w, c_terms, local, set1, set2, push_x, push_y, push_c,
     held, c_ref, ch_ref, cl_ref, y_ref, sems,
 ):
     copies = lane_blocks(w, held, sems)
     for copy in copies:
         copy.start()
-    ch, cl = c_high[...], c_low[...]
+    terms = c_terms[...]
     step = ORDER * CROWS
     for part in range(PARTS):
         c_ref[...] = jnp.zeros_like(c_ref)
@@ -295,7 +294,7 @@
             first, second = 2 * pair, 2 * pair + 1
             high = jnp.concatenate([ch_ref[cell * step : cell * step + CPAD] for cell in (first, second)], 1)
             low = jnp.concatenate([cl_ref[cell * step : cell * step + CPAD] for cell in (first, second)], 1)
-            product = dot(ch, high) + (dot(ch, low) + dot(cl, high))
+            product = dot(terms, jnp.concatenate([high, low, high], 0))
             for index, cell in enumerate((first, second)):
                 start = cell * ORDER * ROWS
                 ys[start : start + CELL_ROWS] += product[:CELL_ROWS, index * LANES : (index + 1) * LANES]
@@ -391,6 +390,8 @@
     places = PLACES.items()
     chosen = selection(places, ROWS, KPAD)
     columns = chosen @ selection([(place, row) for row, place in enumerate(CORNERS)], CROWS, CPAD).T
+    columns_high = np.concatenate([columns, columns, 0 * columns], 1)
+    columns_low = np.concatenate([0 * columns, 0 * columns, columns], 1)
     me = lax.axis_index("band").astype(jnp.int32).reshape(1)
     held = [pltpu.VMEM((PARTS * OWNED, LANES), F32)]
     operator_scratch = [
@@ -467,14 +468,14 @@
     r6 = passed_along(f0, "face", -1)
     q0 = passed_along(s6, "slab", 1)
     q6 = passed_along(s0, "slab", -1)
-    r_high, r_low, far_high, far_low, c_high, c_low = run(
+    r_high, r_low, far_high, far_low, c_terms = run(
         call(
             rotation_kernel,
             "rotation",
-            [SM] + [VM] * 4,
-            [((768, 256), BF16)] * 2 + [((256, 256), BF16)] * 2 + [((KPAD, CPAD), BF16)] * 2,
+            [SM] + [VM] * 5,
+            [((768, 256), BF16)] * 2 + [((256, 256), BF16)] * 2 + [((KPAD, 3 * CPAD), BF16)],
         ),
-        me, rotation, k_high, k_low, jnp.asarray(columns, BF16),
+        me, rotation, k_high, k_low, jnp.asarray(columns_high, BF16), jnp.asarray(columns_low, BF16),
     )
     e0, e6 = run(call(cross_kernel, "cross", [VM] * 2, [both] * 2), q0, q6)
     d0 = passed_along(e6, "face", 1)
@@ -486,7 +487,7 @@
         call(
             third_kernel,
             "third",
-            [VM] * 3 + [HB] + [VM] * 3,
+            [VM] * 3 + [HB] + [VM] * 2,
             [set1, set2, edge, edge, corners],
             held
             + [
@@ -497,7 +498,7 @@
             ]
             + two_copies,
         ),
-        layers, d0, d6, field, c_high, c_low, local,
+        layers, d0, d6, field, c_terms, local,
     )
     l2, r2 = left(v2), right(v2)
     push_x, push_y, push_c = fenced("fence_p", push_x, push_y, push_c)

time: 69.6 us -> 69.2 us (level)
  transfers between devices with their start and end apart: 20 -> 20, of which waited for: 8 -> 8; matrix products, arithmetic and copies ran while one was open for 0% -> 0% of each run, Pallas kernels for 10% -> 11%
where the time goes in v7:
time: 69.2 us; the launch traced here: 69 us
  starting transfers between devices  31.1 us (45%)
  waiting for transfers between devices  23.6 us (34%)
  Pallas kernels  12.6 us (18%)
  between operations  1.73 us (2%)
    ppermute x18, starting transfers between devices, passed_along(): lax.ppermute(value, axis, [(s, (s + steps) % count) for s in range(count)])  30 us
    ppermute x18, waiting for transfers between devices, passed_along(): lax.ppermute(value, axis, [(s, (s + steps) % count) for s in range(count)])  14 us
    pallas_call x15, Pallas kernels, __call__(): *results, self.token = kernel(*operands, self.token)  11.4 us
    ppermute x2, waiting for transfers between devices, passed_diagonal(): return lax.ppermute(value, ('slab', 'face'), pairs)  9.61 us
  transfers between devices with their start and end apart: 20, of which 8 were waited for; matrix products, arithmetic and copies ran while one was open for 0% of the time, Pallas kernels for 11%

profile of v7, /device:TPU:1, one launch (start us, length us, event | category | flops | bytes accessed | tf_op | source)
XLA Modules:
  0.0 69.0 jit_solution(6746880934870601025)
XLA Ops:
  0.0 1.2 %pulls.1 = (f32[288,128]{1,0:T(8,128)S(1)}, f32[288,128]{1,0:T(8,128)S(1)}, f32[48,128]{1,0:T(8,128)S(1)}) custom-call(f32[864,256]{1,0:T(8,128)} %bitcast.7), custom_call_target="tpu_custom_call" | custom-call | flops 10000000000 | bytes 1 | tf_op jit(solution)/shard_map/pulls/pallas_call | solution.py:423
  1.2 8.9 %collective-permute-start = (f32[288,128]{1,0:T(8,128)S(1)}, f32[288,128]{1,0:T(8,128)S(1)}, u32[]{:S(2)}, u32[]{:S(2)}) collective-permute-start(f32[288,128]{1,0:T(8,128)S(1)} %get-tuple-element.56), channel_id=1, source_target_pairs={{0,240},{16,0},{32,16},{48,32},{64,48},{80,64},{96,80},{112,96},{1... | collective-permute-start | bytes 442376 | tf_op jit(solution)/shard_map/ppermute | solution.py:375
  10.1 1.0 %collective-permute-start.1 = (f32[288,128]{1,0:T(8,128)S(1)}, f32[288,128]{1,0:T(8,128)S(1)}, u32[]{:S(2)}, u32[]{:S(2)}) collective-permute-start(f32[288,128]{1,0:T(8,128)S(1)} %get-tuple-element.57), channel_id=1, source_target_pairs={{0,12},{4,0},{8,4},{12,8},{1,13},{5,1},{9,5},{13,9},{2,14},{6,2},{... | collective-permute-start | bytes 442376 | tf_op jit(solution)/shard_map/ppermute | solution.py:375
  11.1 0.0 copy-start.3
  11.1 0.0 copy-start.5
  11.1 1.0 %collective-permute-start.2 = (f32[48,128]{1,0:T(8,128)S(1)}, f32[48,128]{1,0:T(8,128)S(1)}, u32[]{:S(2)}, u32[]{:S(2)}) collective-permute-start(f32[48,128]{1,0:T(8,128)S(1)} %get-tuple-element.59), channel_id=1, source_target_pairs={{0,252},{4,240},{8,244},{12,248},{16,12},{20,0},{24,4},{28,8},{32,... | collective-permute-start | bytes 73736 | tf_op jit(solution)/shard_map/ppermute | solution.py:385
  13.5 1.9 %cell.1 = (bf16[400,400]{1,0:T(8,128)(2,1)S(1)}, bf16[400,400]{1,0:T(8,128)(2,1)S(1)}, f32[1344,128]{1,0:T(8,128)S(1)}, f32[8,128]{1,0:T(8,128)S(1)}) custom-call(f32[343,343]{1,0:T(8,128)S(1)} %copy-done, bf16[400,343]{1,0:T(8,128)(2,1)S(1)} %copy-done.2, bf16[343,400]{1,0:T(8,128)(2,1)S(1)} %copy-done.1, ...), custom_call_target="tpu_custom_call", output_to_operand_aliasing={{3}: (6, {})} | custom-call | flops 1 | bytes 1 | tf_op jit(solution)/shard_map/cell/pallas_call | solution.py:365
  15.4 0.0 collective-permute-done.2.refs_3_
  15.4 0.0 collective-permute-done.1.refs_2_
  15.5 0.0 copy-start.4
  15.5 0.0 copy-start.6
  15.5 0.0 copy-start.7
  15.5 2.1 %first.1 = (f32[2,1344,128]{2,1,0:T(8,128)S(1)}, f32[336,128]{1,0:T(8,128)S(1)}, f32[336,128]{1,0:T(8,128)S(1)}, f32[336,128]{1,0:T(8,128)S(1)}, f32[336,128]{1,0:T(8,128)S(1)}, /*index=5*/f32[8,128]{1,0:T(8,128)S(1)}) custom-call(f32[864,256]{1,0:T(8,128)S(1)} %bitcast.8, ...), custom_call_target="tpu_custom_call", output_to_operand_aliasing={{5}: (7, {})} | custom-call | flops 10000000000 | bytes 1 | tf_op jit(solution)/shard_map/first/pallas_call | solution.py:365
  17.6 0.1 collective-permute-start.3
  17.7 0.5 collective-permute-start.4
  18.2 1.5 %collective-permute-start.5 = (f32[336,128]{1,0:T(8,128)S(1)}, f32[336,128]{1,0:T(8,128)S(1)}, u32[]{:S(2)}, u32[]{:S(2)}) collective-permute-start(f32[336,128]{1,0:T(8,128)S(1)} %get-tuple-element.68), channel_id=1, source_target_pairs={{0,16},{16,32},{32,48},{48,64},{64,80},{80,96},{96,112},{112,128},... | collective-permute-start | bytes 516104 | tf_op jit(solution)/shard_map/ppermute | solution.py:375
  19.7 3.7 %collective-permute-start.6 = (f32[336,128]{1,0:T(8,128)S(1)}, f32[336,128]{1,0:T(8,128)S(1)}, u32[]{:S(2)}, u32[]{:S(2)}) collective-permute-start(f32[336,128]{1,0:T(8,128)S(1)} %get-tuple-element.69), channel_id=1, source_target_pairs={{0,240},{16,0},{32,16},{48,32},{64,48},{80,64},{96,80},{112,96},{1... | collective-permute-start | bytes 516104 | tf_op jit(solution)/shard_map/ppermute | solution.py:375
  23.4 0.5 rotation.1
  23.9 2.8 %collective-permute-done.5.refs_0_.refs_3_ = f32[336,128]{1,0:T(8,128)S(1)} collective-permute-done((f32[336,128]{1,0:T(8,128)S(1)}, f32[336,128]{1,0:T(8,128)S(1)}, u32[]{:S(2)}, u32[]{:S(2)}) %collective-permute-start.5) | collective-permute-done | bytes 172064 | tf_op jit(solution)/shard_map/ppermute | solution.py:375
  26.7 0.0 collective-permute-done.6.refs_1_.refs_4_
  26.7 2.6 %collective-permute-start.7 = (f32[96,128]{1,0:T(8,128)S(1)}, f32[96,128]{1,0:T(8,128)S(1)}, u32[]{:S(2)}, u32[]{:S(2)}) collective-permute-start(f32[96,128]{1,0:T(8,128)S(1)} %get-tuple-element.74), channel_id=1, source_target_pairs={{0,4},{4,8},{8,12},{12,0},{1,5},{5,9},{9,13},{13,1},{2,6},{6,10},{... | collective-permute-start | bytes 147464 | tf_op jit(solution)/shard_map/ppermute | solution.py:375
  29.3 0.0 collective-permute-start.8
  29.3 0.0 collective-permute-done.4.refs_2_
  29.3 2.1 %second.1 = (f32[2,1344,128]{2,1,0:T(8,128)S(1)}, f32[8,128]{1,0:T(8,128)S(1)}) custom-call(f32[2,1344,128]{2,1,0:T(8,128)S(1)} %get-tuple-element.65.refs_0_, f32[336,128]{1,0:T(8,128)S(1)} %collective-permute-done.3.refs_1_, f32[336,128]{1,0:T(8,128)S(1)} %collective-permute-done.4.refs_2_, ...), custom_call_target="tpu_custom_call", output_to_operand_aliasing={{1}: (8, {})} | custom-call | flops 10000000000 | bytes 1 | tf_op jit(solution)/shard_map/second/pallas_call | solution.py:365
  31.4 1.4 %collective-permute-done.8.refs_2_ = f32[96,128]{1,0:T(8,128)S(1)} collective-permute-done((f32[96,128]{1,0:T(8,128)S(1)}, f32[96,128]{1,0:T(8,128)S(1)}, u32[]{:S(2)}, u32[]{:S(2)}) %collective-permute-start.8) | collective-permute-done | bytes 49184 | tf_op jit(solution)/shard_map/ppermute | solution.py:375
  32.8 1.0 %third.1 = (f32[528,128]{1,0:T(8,128)S(1)}, f32[1200,128]{1,0:T(8,128)S(1)}, f32[288,128]{1,0:T(8,128)S(1)}, f32[288,128]{1,0:T(8,128)S(1)}, f32[48,128]{1,0:T(8,128)S(1)}, /*index=5*/f32[8,128]{1,0:T(8,128)S(1)}) custom-call(f32[2,1344,128]{2,1,0:T(8,128)S(1)} %get-tuple-element.73.refs_0_, ...), custom_call_target="tpu_custom_call", output_to_operand_aliasing={{5}: (6, {})} | custom-call | flops 10000000000 | bytes 1 | tf_op jit(solution)/shard_map/third/pallas_call | solution.py:365
  33.8 2.8 %collective-permute-start.15 = (f32[1200,128]{1,0:T(8,128)S(1)}, f32[1200,128]{1,0:T(8,128)S(1)}, u32[]{:S(2)}, u32[]{:S(2)}) collective-permute-start(f32[1200,128]{1,0:T(8,128)S(1)} %get-tuple-element.90.refs_0_), channel_id=1, source_target_pairs={{0,3},{1,0},{2,1},{3,2},{4,7},{5,4},{6,5},{7,6},{8,11},{9,8},{10,9... | collective-permute-start | bytes 1843208 | tf_op jit(solution)/shard_map/ppermute | solution.py:375
  36.6 0.0 collective-permute-start.14
  36.7 0.0 collective-permute-start.9
  36.7 0.6 collective-permute-start.10
  37.3 0.0 collective-permute-start.11
  37.3 9.6 %collective-permute-done.11.refs_3_ = f32[48,128]{1,0:T(8,128)S(1)} collective-permute-done((f32[48,128]{1,0:T(8,128)S(1)}, f32[48,128]{1,0:T(8,128)S(1)}, u32[]{:S(2)}, u32[]{:S(2)}) %collective-permute-start.11) | collective-permute-done | bytes 24608 | tf_op jit(solution)/shard_map/ppermute | solution.py:385
  46.9 2.8 %collective-permute-start.13 = (f32[528,128]{1,0:T(8,128)S(1)}, f32[528,128]{1,0:T(8,128)S(1)}, u32[]{:S(2)}, u32[]{:S(2)}) collective-permute-start(f32[528,128]{1,0:T(8,128)S(1)} %get-tuple-element.87.refs_0_), channel_id=1, source_target_pairs={{0,3},{1,0},{2,1},{3,2},{4,7},{5,4},{6,5},{7,6},{8,11},{9,8},{10,9... | collective-permute-start | bytes 811016 | tf_op jit(solution)/shard_map/ppermute | solution.py:375
  49.8 0.0 collective-permute-start.12
  49.8 0.3 collective-permute-done.15.refs_1_.refs_2_
  50.1 3.2 %collective-permute-done.14.refs_0_.refs_1_ = f32[1200,128]{1,0:T(8,128)S(1)} collective-permute-done((f32[1200,128]{1,0:T(8,128)S(1)}, f32[1200,128]{1,0:T(8,128)S(1)}, u32[]{:S(2)}, u32[]{:S(2)}) %collective-permute-start.14) | collective-permute-done | bytes 614432 | tf_op jit(solution)/shard_map/ppermute | solution.py:375
  53.3 0.1 collective-permute-start.16
  53.4 2.7 %collective-permute-start.17 = (f32[600,128]{1,0:T(8,128)S(1)}, f32[600,128]{1,0:T(8,128)S(1)}, u32[]{:S(2)}, u32[]{:S(2)}) collective-permute-start(f32[600,128]{1,0:T(8,128)S(1)} %get-tuple-element.95), channel_id=1, source_target_pairs={{0,3},{1,0},{2,1},{3,2},{4,7},{5,4},{6,5},{7,6},{8,11},{9,8},{10,9... | collective-permute-start | bytes 921608 | tf_op jit(solution)/shard_map/ppermute | solution.py:375
  56.1 0.9 %near2.1 = (f32[600,256]{1,0:T(8,128)S(1)}, f32[8,128]{1,0:T(8,128)S(1)}) custom-call(f32[1200,128]{1,0:T(8,128)S(1)} %get-tuple-element.90.refs_0_, f32[1200,128]{1,0:T(8,128)S(1)} %collective-permute-done.14.refs_0_.refs_1_, f32[1200,128]{1,0:T(8,128)S(1)} %collective-permute-done.15.refs_1_.refs_2_, ...), custom_call_target="tpu_custom_call", output_to_operand_aliasing={{1}: (5, {})} | custom-call | flops 10000000000 | bytes 1 | tf_op jit(solution)/shard_map/near2/pallas_call | solution.py:365
  57.0 0.0 collective-permute-done.13.refs_1_.refs_2_
  57.0 1.4 %collective-permute-done.12.refs_0_.refs_1_ = f32[528,128]{1,0:T(8,128)S(1)} collective-permute-done((f32[528,128]{1,0:T(8,128)S(1)}, f32[528,128]{1,0:T(8,128)S(1)}, u32[]{:S(2)}, u32[]{:S(2)}) %collective-permute-start.12) | collective-permute-done | bytes 270368 | tf_op jit(solution)/shard_map/ppermute | solution.py:375
  58.4 0.1 collective-permute-start.18
  58.5 2.7 %collective-permute-start.19 = (f32[264,128]{1,0:T(8,128)S(1)}, f32[264,128]{1,0:T(8,128)S(1)}, u32[]{:S(2)}, u32[]{:S(2)}) collective-permute-start(f32[264,128]{1,0:T(8,128)S(1)} %get-tuple-element.103), channel_id=1, source_target_pairs={{0,3},{1,0},{2,1},{3,2},{4,7},{5,4},{6,5},{7,6},{8,11},{9,8},{10,9... | collective-permute-start | bytes 405512 | tf_op jit(solution)/shard_map/ppermute | solution.py:375
  61.2 3.8 %collective-permute-done.16.refs_1_ = f32[600,128]{1,0:T(8,128)S(1)} collective-permute-done((f32[600,128]{1,0:T(8,128)S(1)}, f32[600,128]{1,0:T(8,128)S(1)}, u32[]{:S(2)}, u32[]{:S(2)}) %collective-permute-start.16) | collective-permute-done | bytes 307232 | tf_op jit(solution)/shard_map/ppermute | solution.py:375
  65.0 1.3 %far2.1 = (f32[864,256]{1,0:T(8,128)}, f32[8,128]{1,0:T(8,128)S(1)}) custom-call(f32[600,256]{1,0:T(8,128)S(1)} %get-tuple-element.93.refs_0_, f32[600,128]{1,0:T(8,128)S(1)} %collective-permute-done.16.refs_1_, f32[600,128]{1,0:T(8,128)S(1)} %collective-permute-done.17.refs_2_, ...), custom_call_target="tpu_custom_call", output_to_operand_aliasing={{1}: (5, {})} | custom-call | flops 10000000000 | bytes 1 | tf_op jit(solution)/shard_map/far2/pallas_call | solution.py:365
  66.3 0.5 near1.1
  66.8 1.1 %collective-permute-done.18.refs_1_ = f32[264,128]{1,0:T(8,128)S(1)} collective-permute-done((f32[264,128]{1,0:T(8,128)S(1)}, f32[264,128]{1,0:T(8,128)S(1)}, u32[]{:S(2)}, u32[]{:S(2)}) %collective-permute-start.18) | collective-permute-done | bytes 135200 | tf_op jit(solution)/shard_map/ppermute | solution.py:375
  67.9 1.0 %last.1 = (f32[864,256]{1,0:T(8,128)}, f32[8,128]{1,0:T(8,128)S(1)}) custom-call(f32[264,256]{1,0:T(8,128)S(1)} %get-tuple-element.101.refs_0_, f32[264,128]{1,0:T(8,128)S(1)} %collective-permute-done.18.refs_1_, f32[264,128]{1,0:T(8,128)S(1)} %collective-permute-done.19.refs_2_, ...), custom_call_target="tpu_custom_call", output_to_operand_aliasing={{1}: (6, {}), {0}: (5, {})} | custom-call | flops 10000000000 | bytes 1 | tf_op jit(solution)/shard_map/last/pallas_call | solution.py:365
  (25 shorter events, 0.1 us)
Async XLA Ops:
  1.2 14.2 %collective-permute-start = (f32[288,128]{1,0:T(8,128)S(1)}, f32[288,128]{1,0:T(8,128)S(1)}, u32[]{:S(2)}, u32[]{:S(2)}) collective-permute-start(f32[288,128]{1,0:T(8,128)S(1)} %get-tuple-element.56), channel_id=1, source_target_pairs={{0,240},{16,0},{32,16},{48,32},{64,48},{80,64},{96,80},{112,96},{1... | collective-permute-start | bytes 442376 | tf_op jit(solution)/shard_map/ppermute | solution.py:375
  10.1 5.3 %collective-permute-start.1 = (f32[288,128]{1,0:T(8,128)S(1)}, f32[288,128]{1,0:T(8,128)S(1)}, u32[]{:S(2)}, u32[]{:S(2)}) collective-permute-start(f32[288,128]{1,0:T(8,128)S(1)} %get-tuple-element.57), channel_id=1, source_target_pairs={{0,12},{4,0},{8,4},{12,8},{1,13},{5,1},{9,5},{13,9},{2,14},{6,2},{... | collective-permute-start | bytes 442376 | tf_op jit(solution)/shard_map/ppermute | solution.py:375
  11.1 2.4 %copy-start = (f32[343,343]{1,0:T(8,128)S(1)}, f32[343,343]{1,0:T(8,128)}, u32[]{:S(2)}) copy-start(f32[343,343]{1,0:T(8,128)} %refs_0_.1) | copy-start | bytes 1411792
  11.1 2.4 %copy-start.1 = (bf16[343,400]{1,0:T(8,128)(2,1)S(1)}, bf16[343,400]{1,0:T(8,128)(2,1)}, u32[]{:S(2)}) copy-start(bf16[343,400]{1,0:T(8,128)(2,1)} %constant.15.clone.refs_2_) | copy-start | bytes 823204
  11.1 2.4 %copy-start.2 = (bf16[400,343]{1,0:T(8,128)(2,1)S(1)}, bf16[400,343]{1,0:T(8,128)(2,1)}, u32[]{:S(2)}) copy-start(bf16[400,343]{1,0:T(8,128)(2,1)} %constant.14.clone.refs_1_) | copy-start | bytes 823204
  11.1 2.4 %copy-start.3 = (f32[6,6,24]{2,1,0:T(8,128)S(1)}, f32[6,6,24]{2,1,0:T(8,128)}, u32[]{:S(2)}) copy-start(f32[6,6,24]{2,1,0:T(8,128)} %refs_3_.1) | copy-start | bytes 10372
  11.1 4.3 %copy-start.5 = (f32[6,6,24,256]{3,2,1,0:T(8,128)S(1)}, f32[6,6,24,256]{3,2,1,0:T(8,128)}, u32[]{:S(2)}) copy-start(f32[6,6,24,256]{3,2,1,0:T(8,128)} %param.10) | copy-start | bytes 2654212
  11.1 4.3 %collective-permute-start.2 = (f32[48,128]{1,0:T(8,128)S(1)}, f32[48,128]{1,0:T(8,128)S(1)}, u32[]{:S(2)}, u32[]{:S(2)}) collective-permute-start(f32[48,128]{1,0:T(8,128)S(1)} %get-tuple-element.59), channel_id=1, source_target_pairs={{0,252},{4,240},{8,244},{12,248},{16,12},{20,0},{24,4},{28,8},{32,... | collective-permute-start | bytes 73736 | tf_op jit(solution)/shard_map/ppermute | solution.py:385
  15.5 7.9 %copy-start.4 = (f32[1024,256]{1,0:T(8,128)S(1)}, f32[1024,256]{1,0:T(8,128)}, u32[]{:S(2)}) copy-start(f32[1024,256]{1,0:T(8,128)} %refs_1_.2) | copy-start | bytes 3145732
  15.5 7.9 %copy-start.6 = (bf16[400,192]{1,0:T(8,128)(2,1)S(1)}, bf16[400,192]{1,0:T(8,128)(2,1)}, u32[]{:S(2)}) copy-start(bf16[400,192]{1,0:T(8,128)(2,1)} %constant.17.clone.refs_5_) | copy-start | bytes 460804
  15.5 7.9 %copy-start.7 = (bf16[400,192]{1,0:T(8,128)(2,1)S(1)}, bf16[400,192]{1,0:T(8,128)(2,1)}, u32[]{:S(2)}) copy-start(bf16[400,192]{1,0:T(8,128)(2,1)} %constant.16.clone.refs_4_) | copy-start | bytes 460804
  17.6 11.7 %collective-permute-start.3 = (f32[336,128]{1,0:T(8,128)S(1)}, f32[336,128]{1,0:T(8,128)S(1)}, u32[]{:S(2)}, u32[]{:S(2)}) collective-permute-start(f32[336,128]{1,0:T(8,128)S(1)} %get-tuple-element.66), channel_id=1, source_target_pairs={{0,4},{4,8},{8,12},{12,0},{1,5},{5,9},{9,13},{13,1},{2,6},{6,10},{... | collective-permute-start | bytes 516104 | tf_op jit(solution)/shard_map/ppermute | solution.py:375
  17.7 11.6 %collective-permute-start.4 = (f32[336,128]{1,0:T(8,128)S(1)}, f32[336,128]{1,0:T(8,128)S(1)}, u32[]{:S(2)}, u32[]{:S(2)}) collective-permute-start(f32[336,128]{1,0:T(8,128)S(1)} %get-tuple-element.67), channel_id=1, source_target_pairs={{0,12},{4,0},{8,4},{12,8},{1,13},{5,1},{9,5},{13,9},{2,14},{6,2},{... | collective-permute-start | bytes 516104 | tf_op jit(solution)/shard_map/ppermute | solution.py:375
  18.2 8.5 %collective-permute-start.5 = (f32[336,128]{1,0:T(8,128)S(1)}, f32[336,128]{1,0:T(8,128)S(1)}, u32[]{:S(2)}, u32[]{:S(2)}) collective-permute-start(f32[336,128]{1,0:T(8,128)S(1)} %get-tuple-element.68), channel_id=1, source_target_pairs={{0,16},{16,32},{32,48},{48,64},{64,80},{80,96},{96,112},{112,128},... | collective-permute-start | bytes 516104 | tf_op jit(solution)/shard_map/ppermute | solution.py:375
  19.7 7.0 %collective-permute-start.6 = (f32[336,128]{1,0:T(8,128)S(1)}, f32[336,128]{1,0:T(8,128)S(1)}, u32[]{:S(2)}, u32[]{:S(2)}) collective-permute-start(f32[336,128]{1,0:T(8,128)S(1)} %get-tuple-element.69), channel_id=1, source_target_pairs={{0,240},{16,0},{32,16},{48,32},{64,48},{80,64},{96,80},{112,96},{1... | collective-permute-start | bytes 516104 | tf_op jit(solution)/shard_map/ppermute | solution.py:375
  26.7 4.7 %collective-permute-start.7 = (f32[96,128]{1,0:T(8,128)S(1)}, f32[96,128]{1,0:T(8,128)S(1)}, u32[]{:S(2)}, u32[]{:S(2)}) collective-permute-start(f32[96,128]{1,0:T(8,128)S(1)} %get-tuple-element.74), channel_id=1, source_target_pairs={{0,4},{4,8},{8,12},{12,0},{1,5},{5,9},{9,13},{13,1},{2,6},{6,10},{... | collective-permute-start | bytes 147464 | tf_op jit(solution)/shard_map/ppermute | solution.py:375
  29.3 3.5 %collective-permute-start.8 = (f32[96,128]{1,0:T(8,128)S(1)}, f32[96,128]{1,0:T(8,128)S(1)}, u32[]{:S(2)}, u32[]{:S(2)}) collective-permute-start(f32[96,128]{1,0:T(8,128)S(1)} %get-tuple-element.75), channel_id=1, source_target_pairs={{0,12},{4,0},{8,4},{12,8},{1,13},{5,1},{9,5},{13,9},{2,14},{6,2},{... | collective-permute-start | bytes 147464 | tf_op jit(solution)/shard_map/ppermute | solution.py:375
  33.8 16.3 %collective-permute-start.15 = (f32[1200,128]{1,0:T(8,128)S(1)}, f32[1200,128]{1,0:T(8,128)S(1)}, u32[]{:S(2)}, u32[]{:S(2)}) collective-permute-start(f32[1200,128]{1,0:T(8,128)S(1)} %get-tuple-element.90.refs_0_), channel_id=1, source_target_pairs={{0,3},{1,0},{2,1},{3,2},{4,7},{5,4},{6,5},{7,6},{8,11},{9,8},{10,9... | collective-permute-start | bytes 1843208 | tf_op jit(solution)/shard_map/ppermute | solution.py:375
  36.6 16.6 %collective-permute-start.14 = (f32[1200,128]{1,0:T(8,128)S(1)}, f32[1200,128]{1,0:T(8,128)S(1)}, u32[]{:S(2)}, u32[]{:S(2)}) collective-permute-start(f32[1200,128]{1,0:T(8,128)S(1)} %get-tuple-element.90.refs_0_), channel_id=1, source_target_pairs={{0,1},{1,2},{2,3},{3,0},{4,5},{5,6},{6,7},{7,4},{8,9},{9,10},{10,1... | collective-permute-start | bytes 1843208 | tf_op jit(solution)/shard_map/ppermute | solution.py:375
  36.7 10.2 %collective-permute-start.9 = (f32[288,128]{1,0:T(8,128)S(1)}, f32[288,128]{1,0:T(8,128)S(1)}, u32[]{:S(2)}, u32[]{:S(2)}) collective-permute-start(f32[288,128]{1,0:T(8,128)S(1)} %get-tuple-element.83), channel_id=1, source_target_pairs={{0,16},{16,32},{32,48},{48,64},{64,80},{80,96},{96,112},{112,128},... | collective-permute-start | bytes 442376 | tf_op jit(solution)/shard_map/ppermute | solution.py:375
  36.7 10.2 %collective-permute-start.10 = (f32[288,128]{1,0:T(8,128)S(1)}, f32[288,128]{1,0:T(8,128)S(1)}, u32[]{:S(2)}, u32[]{:S(2)}) collective-permute-start(f32[288,128]{1,0:T(8,128)S(1)} %get-tuple-element.84), channel_id=1, source_target_pairs={{0,4},{4,8},{8,12},{12,0},{1,5},{5,9},{9,13},{13,1},{2,6},{6,10},{... | collective-permute-start | bytes 442376 | tf_op jit(solution)/shard_map/ppermute | solution.py:375
  37.3 9.6 %collective-permute-start.11 = (f32[48,128]{1,0:T(8,128)S(1)}, f32[48,128]{1,0:T(8,128)S(1)}, u32[]{:S(2)}, u32[]{:S(2)}) collective-permute-start(f32[48,128]{1,0:T(8,128)S(1)} %get-tuple-element.85), channel_id=1, source_target_pairs={{0,20},{4,24},{8,28},{12,16},{16,36},{20,40},{24,44},{28,32},{32,5... | collective-permute-start | bytes 73736 | tf_op jit(solution)/shard_map/ppermute | solution.py:385
  46.9 10.1 %collective-permute-start.13 = (f32[528,128]{1,0:T(8,128)S(1)}, f32[528,128]{1,0:T(8,128)S(1)}, u32[]{:S(2)}, u32[]{:S(2)}) collective-permute-start(f32[528,128]{1,0:T(8,128)S(1)} %get-tuple-element.87.refs_0_), channel_id=1, source_target_pairs={{0,3},{1,0},{2,1},{3,2},{4,7},{5,4},{6,5},{7,6},{8,11},{9,8},{10,9... | collective-permute-start | bytes 811016 | tf_op jit(solution)/shard_map/ppermute | solution.py:375
  49.8 8.6 %collective-permute-start.12 = (f32[528,128]{1,0:T(8,128)S(1)}, f32[528,128]{1,0:T(8,128)S(1)}, u32[]{:S(2)}, u32[]{:S(2)}) collective-permute-start(f32[528,128]{1,0:T(8,128)S(1)} %get-tuple-element.87.refs_0_), channel_id=1, source_target_pairs={{0,1},{1,2},{2,3},{3,0},{4,5},{5,6},{6,7},{7,4},{8,9},{9,10},{10,1... | collective-permute-start | bytes 811016 | tf_op jit(solution)/shard_map/ppermute | solution.py:375
  53.3 11.6 %collective-permute-start.16 = (f32[600,128]{1,0:T(8,128)S(1)}, f32[600,128]{1,0:T(8,128)S(1)}, u32[]{:S(2)}, u32[]{:S(2)}) collective-permute-start(f32[600,128]{1,0:T(8,128)S(1)} %get-tuple-element.94), channel_id=1, source_target_pairs={{0,1},{1,2},{2,3},{3,0},{4,5},{5,6},{6,7},{7,4},{8,9},{9,10},{10,1... | collective-permute-start | bytes 921608 | tf_op jit(solution)/shard_map/ppermute | solution.py:375
  53.4 11.6 %collective-permute-start.17 = (f32[600,128]{1,0:T(8,128)S(1)}, f32[600,128]{1,0:T(8,128)S(1)}, u32[]{:S(2)}, u32[]{:S(2)}) collective-permute-start(f32[600,128]{1,0:T(8,128)S(1)} %get-tuple-element.95), channel_id=1, source_target_pairs={{0,3},{1,0},{2,1},{3,2},{4,7},{5,4},{6,5},{7,6},{8,11},{9,8},{10,9... | collective-permute-start | bytes 921608 | tf_op jit(solution)/shard_map/ppermute | solution.py:375
  58.4 9.5 %collective-permute-start.18 = (f32[264,128]{1,0:T(8,128)S(1)}, f32[264,128]{1,0:T(8,128)S(1)}, u32[]{:S(2)}, u32[]{:S(2)}) collective-permute-start(f32[264,128]{1,0:T(8,128)S(1)} %get-tuple-element.102), channel_id=1, source_target_pairs={{0,1},{1,2},{2,3},{3,0},{4,5},{5,6},{6,7},{7,4},{8,9},{9,10},{10,1... | collective-permute-start | bytes 405512 | tf_op jit(solution)/shard_map/ppermute | solution.py:375
  58.5 9.4 %collective-permute-start.19 = (f32[264,128]{1,0:T(8,128)S(1)}, f32[264,128]{1,0:T(8,128)S(1)}, u32[]{:S(2)}, u32[]{:S(2)}) collective-permute-start(f32[264,128]{1,0:T(8,128)S(1)} %get-tuple-element.103), channel_id=1, source_target_pairs={{0,3},{1,0},{2,1},{3,2},{4,7},{5,4},{6,5},{7,6},{8,11},{9,8},{10,9... | collective-permute-start | bytes 405512 | tf_op jit(solution)/shard_map/ppermute | solution.py:375
